TPU v7x, 32 devices: a whole 2x2x4 slice. The times are simulated.
32 devices in a mesh: dp: 8 (over z, y), section: 4 (over x, core).
Axes of the slice: x: 2, y: 2, z: 4, core: 2. Of those that a mesh axis runs over, the one named last changes fastest.
Arguments:
- inputs: bfloat16 [8192, 768], P('dp'), may hold values from -6 to 6
- cotangent: bfloat16 [8192, 768], P('dp'), may hold values from -6 to 6
- in_master: float32 [4, 768, 3072], P('section', 'dp'), may hold values from -3 to 3
- in_first: float32 [4, 768, 3072], P('section', 'dp'), may hold values from -60 to 60
- in_second: float32 [4, 768, 3072], P('section', 'dp'), may hold values from 10 to 1000
- down_master: float32 [4, 1536, 768], P('section', 'dp'), may hold values from -0.109375 to 0.109375
- down_first: float32 [4, 1536, 768], P('section', 'dp'), may hold values from -60 to 60
- down_second: float32 [4, 1536, 768], P('section', 'dp'), may hold values from 10 to 1000
- vec_master: float32 [4, 4608], P('section', 'dp'), may hold values from -1 to 2
- vec_first: float32 [4, 4608], P('section', 'dp'), may hold values from -60 to 60
- vec_second: float32 [4, 4608], P('section', 'dp'), may hold values from 10 to 1000
Outputs:
- section_outputs: bfloat16 [4, 8192, 768], P('section', 'dp')
- section_input_grads: bfloat16 [4, 8192, 768], P('section', 'dp')
- in_grad: float32 [4, 768, 3072], P('section', 'dp')
- down_grad: float32 [4, 1536, 768], P('section', 'dp')
- vec_grad: float32 [4, 4608], P('section', 'dp')
- in_step: float32 [4, 768, 3072], P('section', 'dp')
- in_first_new: float32 [4, 768, 3072], P('section', 'dp')
- in_second_new: float32 [4, 768, 3072], P('section', 'dp')
- down_step: float32 [4, 1536, 768], P('section', 'dp')
- down_first_new: float32 [4, 1536, 768], P('section', 'dp')
- down_second_new: float32 [4, 1536, 768], P('section', 'dp')
- vec_step: float32 [4, 4608], P('section', 'dp')
- vec_first_new: float32 [4, 4608], P('section', 'dp')
- vec_second_new: float32 [4, 4608], P('section', 'dp')
All inputs are finite; a program needn't handle non-finite values.
Results may differ from a plain program's by a relative error of at most 0.02.
Values may be sent and summed in bfloat16 or wider, within the bound.
No kernel may reach another device: no remote copies, remote signals or barrier semaphores. Data moves between devices by JAX's collectives and lax.ppermute only.
A program may use at most 384 MiB of HBM per device.

v0:
```python
import jax
import jax.numpy as jnp
from jax import lax
from jax.sharding import PartitionSpec as P

D = 768
HEADS = 12
HEAD_DIM = 64
FF = 3072
SEQ = 512
MICRO = 2
SEQ_MB = 1
VEC = 4608


NORM_EPSILON = 1e-05
BETA_ONE = 0.9
BETA_TWO = 0.98
BIAS_ONE = 1.0 - 0.9**10
BIAS_TWO = 1.0 - 0.98**10
WEIGHT_DECAY = 0.01
ADAM_EPSILON = 1e-06
ROOT_HALF = 0.7071067811865476
ROOT_TWO_PI = 2.5066282746310002


def shifted(value, axis, steps):
    count = lax.axis_size(axis)
    leading, last = (max(0, -steps), min(count, count - steps))
    return lax.ppermute(value, axis, [(source, source + steps) for source in range(leading, last)])


def for_sending(value):
    return jax.tree.map(lambda a: a.astype(jnp.bfloat16) if a.dtype == jnp.float32 else a, value)


def product(former, latter):
    return jnp.dot(former, latter, preferred_element_type=jnp.float32)


def inner_rows(former, latter):
    return lax.dot_general(
        former, latter, (((0,), (0,)), ((), ())), preferred_element_type=jnp.float32
    )


def outer_cols(former, latter):
    return lax.dot_general(
        former, latter, (((1,), (1,)), ((), ())), preferred_element_type=jnp.float32
    )


def norm_forward(summed, norm_gain, norm_bias):
    average = jnp.mean(summed, axis=-1, keepdims=True)
    centered = summed - average
    variance = jnp.mean(centered * centered, axis=-1, keepdims=True)
    inverse_spread = lax.rsqrt(variance + NORM_EPSILON)
    normed = centered * inverse_spread
    return (normed * norm_gain + norm_bias, normed, inverse_spread)


def norm_backward(incoming, normed, inverse_spread, norm_gain):
    through = incoming * norm_gain
    summed_grad = inverse_spread * (
        through
        - jnp.mean(through, axis=-1, keepdims=True)
        - normed * jnp.mean(through * normed, axis=-1, keepdims=True)
    )
    return (summed_grad, jnp.sum(incoming * normed, axis=0), jnp.sum(incoming, axis=0))


def attention_parts(hidden, weights):
    w_in, w_down, vector, nearby = weights
    bias_qkv = jnp.concatenate([vector[:D], jnp.zeros((D,), jnp.float32), vector[D : 2 * D]])
    mixing = (product(hidden, w_in[:, : 3 * D]) + bias_qkv).astype(jnp.bfloat16)
    grouped = mixing.reshape(SEQ_MB, SEQ, 3, HEADS, HEAD_DIM)
    queries = grouped[:, :, 0]
    key_rows = grouped[:, :, 1]
    value_rows = grouped[:, :, 2]
    scores = jnp.einsum(
        "bqhd,bkhd->bhqk", queries, key_rows, preferred_element_type=jnp.float32
    ) * HEAD_DIM ** (-0.5)
    chances = jax.nn.softmax(scores, axis=-1)
    chances_low = chances.astype(jnp.bfloat16)
    context = jnp.einsum(
        "bhqk,bkhd->bqhd", chances_low, value_rows, preferred_element_type=jnp.float32
    )
    context = context.reshape(hidden.shape[0], D).astype(jnp.bfloat16)
    branch = product(context, w_in[:, 3 * D :]) + vector[2 * D : 3 * D]
    result, normed, inverse_spread = norm_forward(
        hidden.astype(jnp.float32) + branch, vector[FF : FF + D], vector[FF + D :]
    )
    return (
        result,
        (queries, key_rows, value_rows, chances, chances_low, context, normed, inverse_spread),
    )


def feed_parts(hidden, weights):
    w_in, w_down, vector, nearby = weights
    before = product(hidden, w_in) + vector[:FF]
    active = jax.nn.gelu(before, approximate=False).astype(jnp.bfloat16)
    branch = product(active, w_down) + nearby[3 * D : FF]
    result, normed, inverse_spread = norm_forward(
        hidden.astype(jnp.float32) + branch, vector[FF : FF + D], vector[FF + D :]
    )
    return (result, (before, active, normed, inverse_spread))


def spare_forward(hidden, weights):
    return jnp.zeros_like(hidden)


def attention_forward(hidden, weights):
    return attention_parts(hidden, weights)[0].astype(jnp.bfloat16)


def feed_forward(hidden, weights):
    return feed_parts(hidden, weights)[0].astype(jnp.bfloat16)


def spare_backward(hidden, incoming, weights):
    return (
        jnp.zeros_like(hidden),
        jnp.zeros((D, FF), jnp.float32),
        jnp.zeros((FF, D), jnp.float32),
        jnp.zeros((VEC,), jnp.float32),
        jnp.zeros((VEC,), jnp.float32),
    )


def attention_backward(hidden, incoming, weights):
    w_in, w_down, vector, nearby = weights
    score_scale = HEAD_DIM ** (-0.5)
    result, saved = attention_parts(hidden, weights)
    queries, key_rows, value_rows, chances, chances_low, context, normed, inverse_spread = saved
    summed_grad, gain_grad, bias_grad = norm_backward(
        incoming.astype(jnp.float32), normed, inverse_spread, vector[FF : FF + D]
    )
    branch_low = summed_grad.astype(jnp.bfloat16)
    out_weight_grad = inner_rows(context, branch_low)
    context_grad = (
        outer_cols(branch_low, w_in[:, 3 * D :])
        .astype(jnp.bfloat16)
        .reshape(SEQ_MB, SEQ, HEADS, HEAD_DIM)
    )
    chance_grad = jnp.einsum(
        "bqhd,bkhd->bhqk", context_grad, value_rows, preferred_element_type=jnp.float32
    )
    score_grad = (
        chances * (chance_grad - jnp.sum(chances * chance_grad, axis=-1, keepdims=True))
    ).astype(jnp.bfloat16)
    query_grad = (
        jnp.einsum("bhqk,bkhd->bqhd", score_grad, key_rows, preferred_element_type=jnp.float32)
        * score_scale
    )
    key_grad = (
        jnp.einsum("bhqk,bqhd->bkhd", score_grad, queries, preferred_element_type=jnp.float32)
        * score_scale
    )
    value_grad = jnp.einsum(
        "bhqk,bqhd->bkhd", chances_low, context_grad, preferred_element_type=jnp.float32
    )
    mixing_grad = (
        jnp.stack([query_grad, key_grad, value_grad], axis=2)
        .reshape(hidden.shape[0], 3 * D)
        .astype(jnp.bfloat16)
    )
    mixing_sum = jnp.sum(mixing_grad.astype(jnp.float32), axis=0)
    in_grad = jnp.concatenate([inner_rows(hidden, mixing_grad), out_weight_grad], axis=1)
    hidden_grad = (summed_grad + outer_cols(mixing_grad, w_in[:, : 3 * D])).astype(jnp.bfloat16)
    vector_grad = jnp.concatenate(
        [
            mixing_sum[:D],
            mixing_sum[2 * D :],
            jnp.sum(summed_grad, axis=0),
            jnp.zeros((D,), jnp.float32),
            gain_grad,
            bias_grad,
        ]
    )
    return (
        hidden_grad,
        in_grad,
        jnp.zeros((FF, D), jnp.float32),
        vector_grad,
        jnp.zeros((VEC,), jnp.float32),
    )


def feed_backward(hidden, incoming, weights):
    w_in, w_down, vector, nearby = weights
    result, saved = feed_parts(hidden, weights)
    before, active, normed, inverse_spread = saved
    summed_grad, gain_grad, bias_grad = norm_backward(
        incoming.astype(jnp.float32), normed, inverse_spread, vector[FF : FF + D]
    )
    branch_low = summed_grad.astype(jnp.bfloat16)
    down_grad = inner_rows(active, branch_low)
    active_grad = outer_cols(branch_low, w_down)
    slope = (
        0.5 * (1.0 + lax.erf(before * ROOT_HALF))
        + before * jnp.exp(-0.5 * before * before) / ROOT_TWO_PI
    )
    before_grad = (active_grad * slope).astype(jnp.bfloat16)
    in_grad = inner_rows(hidden, before_grad)
    hidden_grad = (summed_grad + outer_cols(before_grad, w_in)).astype(jnp.bfloat16)
    vector_grad = jnp.concatenate(
        [jnp.sum(before_grad.astype(jnp.float32), axis=0), gain_grad, bias_grad]
    )
    nearby_grad = jnp.concatenate(
        [
            jnp.zeros((3 * D,), jnp.float32),
            jnp.sum(summed_grad, axis=0),
            jnp.zeros((2 * D,), jnp.float32),
        ]
    )
    return (hidden_grad, in_grad, down_grad, vector_grad, nearby_grad)


def adam_update(master, first, second, gradient):
    first_new = BETA_ONE * first + (1.0 - BETA_ONE) * gradient
    second_new = BETA_TWO * second + (1.0 - BETA_TWO) * gradient * gradient
    update = first_new / BIAS_ONE / (jnp.sqrt(second_new / BIAS_TWO) + ADAM_EPSILON)
    return (update + WEIGHT_DECAY * master, first_new, second_new)


def on_device(
    inputs,
    cotangent,
    in_master,
    in_first,
    in_second,
    down_master,
    down_first,
    down_second,
    vec_master,
    vec_first,
    vec_second,
):
    sections = lax.axis_size("section")
    section_index = lax.axis_index("section")
    rows_micro = SEQ_MB * SEQ
    nearby_down, nearby_vec = (
        shifted(down_master.astype(jnp.bfloat16), "section", 1).astype(down_master.dtype),
        shifted(vec_master.astype(jnp.bfloat16), "section", 1).astype(vec_master.dtype),
    )
    w_in, w_own, w_near = (
        lax.all_gather(in_master.astype(jnp.bfloat16), "dp", axis=1, tiled=True),
        lax.all_gather(down_master.astype(jnp.bfloat16), "dp", axis=1, tiled=True),
        lax.all_gather(nearby_down.astype(jnp.bfloat16), "dp", axis=1, tiled=True),
    )
    vector, nearby = (
        lax.all_gather(vec_master, "dp", axis=1, tiled=True),
        lax.all_gather(nearby_vec, "dp", axis=1, tiled=True),
    )
    weights = (w_in[0], jnp.concatenate([w_near[0], w_own[0]], axis=0), vector[0], nearby[0])
    sublayer_kind = 1 + section_index % 2
    ticks = MICRO + sections - 1
    kept_inputs = jnp.zeros((MICRO, rows_micro, D), jnp.bfloat16)
    kept_outputs = jnp.zeros((MICRO, rows_micro, D), jnp.bfloat16)
    arriving = jnp.zeros((rows_micro, D), jnp.bfloat16)
    for tick_number in range(ticks):
        micro_index = tick_number - section_index
        active = (micro_index >= 0) & (micro_index < MICRO)
        slot_index = jnp.clip(micro_index, 0, MICRO - 1)
        if tick_number < MICRO:
            fresh_rows = inputs[tick_number * rows_micro : (tick_number + 1) * rows_micro]
            hidden = jnp.where(section_index == 0, fresh_rows, arriving)
        else:
            hidden = arriving
        branch_index = jnp.where(active, sublayer_kind, 0)
        result = lax.switch(
            branch_index, [spare_forward, attention_forward, feed_forward], hidden, weights
        )
        kept_inputs = jnp.where(
            active, lax.dynamic_update_index_in_dim(kept_inputs, hidden, slot_index, 0), kept_inputs
        )
        kept_outputs = jnp.where(
            active,
            lax.dynamic_update_index_in_dim(kept_outputs, result, slot_index, 0),
            kept_outputs,
        )
        if tick_number + 1 < ticks:
            arriving = jax.tree.map(
                lambda part, own: part.astype(own.dtype),
                shifted(for_sending(result), "section", 1),
                result,
            )
    in_total = jnp.zeros((D, FF), jnp.float32)
    down_total = jnp.zeros((FF, D), jnp.float32)
    vec_total = jnp.zeros((VEC,), jnp.float32)
    near_total = jnp.zeros((VEC,), jnp.float32)
    kept_grads = jnp.zeros((MICRO, rows_micro, D), jnp.bfloat16)
    arriving = jnp.zeros((rows_micro, D), jnp.bfloat16)
    for tick_number in range(ticks):
        micro_index = tick_number - (sections - 1 - section_index)
        active = (micro_index >= 0) & (micro_index < MICRO)
        slot_index = jnp.clip(micro_index, 0, MICRO - 1)
        if tick_number < MICRO:
            fresh_rows = cotangent[tick_number * rows_micro : (tick_number + 1) * rows_micro]
            incoming = jnp.where(section_index == sections - 1, fresh_rows, arriving)
        else:
            incoming = arriving
        hidden = lax.dynamic_index_in_dim(kept_inputs, slot_index, 0, keepdims=False)
        branch_index = jnp.where(active, sublayer_kind, 0)
        hidden_grad, in_grad, down_grad, vector_grad, nearby_grad = lax.switch(
            branch_index,
            [spare_backward, attention_backward, feed_backward],
            hidden,
            incoming,
            weights,
        )
        in_total = in_total + in_grad
        down_total = down_total + down_grad
        vec_total = vec_total + vector_grad
        near_total = near_total + nearby_grad
        kept_grads = jnp.where(
            active,
            lax.dynamic_update_index_in_dim(kept_grads, hidden_grad, slot_index, 0),
            kept_grads,
        )
        if tick_number + 1 < ticks:
            arriving = jax.tree.map(
                lambda part, own: part.astype(own.dtype),
                shifted(for_sending(hidden_grad), "section", -1),
                hidden_grad,
            )
    half_rows = FF // 2
    summed = (
        lax.psum_scatter(in_total[None], "dp", scatter_dimension=1, tiled=True),
        lax.psum_scatter(down_total[None, :half_rows], "dp", scatter_dimension=1, tiled=True),
        lax.psum_scatter(down_total[None, half_rows:], "dp", scatter_dimension=1, tiled=True),
        lax.psum_scatter(vec_total[None], "dp", scatter_dimension=1, tiled=True),
        lax.psum_scatter(near_total[None], "dp", scatter_dimension=1, tiled=True),
    )
    back_down, back_vec = (
        shifted(summed[1].astype(jnp.bfloat16), "section", -1).astype(jnp.float32),
        shifted(summed[4].astype(jnp.bfloat16), "section", -1).astype(jnp.float32),
    )
    in_sum = summed[0]
    down_sum = summed[2] + back_down
    vec_sum = summed[3] + back_vec
    in_step, in_first_new, in_second_new = adam_update(in_master, in_first, in_second, in_sum)
    down_step, down_first_new, down_second_new = adam_update(
        down_master, down_first, down_second, down_sum
    )
    vec_step, vec_first_new, vec_second_new = adam_update(
        vec_master, vec_first, vec_second, vec_sum
    )
    section_outputs = kept_outputs.reshape(1, MICRO * rows_micro, D)
    section_input_grads = kept_grads.reshape(1, MICRO * rows_micro, D)
    return (
        section_outputs,
        section_input_grads,
        in_sum,
        down_sum,
        vec_sum,
        in_step,
        in_first_new,
        in_second_new,
        down_step,
        down_first_new,
        down_second_new,
        vec_step,
        vec_first_new,
        vec_second_new,
    )


def solution(mesh):
    return jax.shard_map(
        on_device,
        mesh=mesh,
        in_specs=(
            P("dp", None),
            P("dp", None),
            P("section", "dp", None),
            P("section", "dp", None),
            P("section", "dp", None),
            P("section", "dp", None),
            P("section", "dp", None),
            P("section", "dp", None),
            P("section", "dp"),
            P("section", "dp"),
            P("section", "dp"),
        ),
        out_specs=(
            P("section", "dp", None),
            P("section", "dp", None),
            P("section", "dp", None),
            P("section", "dp", None),
            P("section", "dp"),
            P("section", "dp", None),
            P("section", "dp", None),
            P("section", "dp", None),
            P("section", "dp", None),
            P("section", "dp", None),
            P("section", "dp", None),
            P("section", "dp"),
            P("section", "dp"),
            P("section", "dp"),
        ),
        check_vma=False,
    )
```

profile of v0, /device:TPU:0, one launch (start us, length us, event | category | flops | bytes accessed | tf_op | source)
XLA Modules:
  0.0 1377.2 jit_solution(14062873075789039621)
XLA Ops:
  16.7 7.1 collective-permute-start.1
  27.2 38.4 %all-reduce.2 = (f32[4608]{0:T(1024)S(1)}, f32[4608]{0:T(1024)S(1)}) all-reduce(f32[4608]{0:T(1024)S(1)} %dynamic-update-slice.15, f32[4608]{0:T(1024)S(1)} %dynamic-update-slice.16), channel_id=1, replica_groups=mesh['dp'=8,'section'=4] {'dp'}, use_global_device_ids=true, to_apply=%add | all-reduce | flops 9216 | bytes 73728 | tf_op jit(solution)/shard_map/squeeze | solution.py:257
  66.8 53.5 %all-gather.6.cloned.1.call-done = bf16[1,1536,768]{2,1,0:T(8,128)(2,1)} async-done(((bf16[1,192,768]{2,1,0:T(8,128)(2,1)}), bf16[1,1536,768]{2,1,0:T(8,128)(2,1)}) %all-gather.6.cloned.1.call-update) | async-done | bytes 2359312 | tf_op jit(solution)/shard_map/all_gather | solution.py:251
  120.3 4.8 pad_maximum_fusion.25
  125.2 76.4 %all-gather.4.cloned.1.call-done = bf16[1,768,3072]{2,1,0:T(8,128)(2,1)} async-done(((bf16[1,96,3072]{2,1,0:T(8,128)(2,1)}), bf16[1,768,3072]{2,1,0:T(8,128)(2,1)}) %all-gather.4.cloned.1.call-update) | async-done | bytes 4718608 | tf_op jit(solution)/shard_map/all_gather | solution.py:249
  201.5 37.3 %conditional.10 = (bf16[512,768]{1,0:T(8,128)(2,1)}, bf16[1,512,768]{2,1,0:T(8,128)(2,1)}) conditional(s32[]{:T(128)} %clamp.30, () %tuple.155, (bf16[512,768]{1,0:T(8,128)(2,1)S(1)}, bf16[768,3072]{1,0:T(8,128)(2,1)}, f32[4608]{0:T(1024)S(1)}) %tuple.413, (bf16[512,768]{1,0:T(8,128)(2,1)S(1)}, bf16[768,3072]{1,0:T(8,128)(2,1)}, ...), branch_computations={%region_0.1_spmd, %region_1.6_spmd, %region_6.9_spmd} | conditional | flops 4942332416 | bytes 50480148 | solution.py:273
  201.6 5.5 fusion.6
  207.1 4.3 copy.140
  211.4 10.0 fusion.632
  221.4 6.1 fusion.10
  244.9 36.4 %conditional.11 = (bf16[512,768]{1,0:T(8,128)(2,1)S(1)}, bf16[1,512,768]{2,1,0:T(8,128)(2,1)S(1)}) conditional(s32[]{:T(128)} %clamp.31, () %tuple.158, (bf16[512,768]{1,0:T(8,128)(2,1)S(1)}, bf16[768,3072]{1,0:T(8,128)(2,1)}, f32[4608]{0:T(1024)S(1)}) %tuple.415, (bf16[512,768]{1,0:T(8,128)(2,1)S(1)}, ...), branch_computations={%region_9.10_spmd, %region_10.15_spmd, %region_15.18_spmd} | conditional | flops 4942332416 | bytes 56771660 | solution.py:273
  245.7 5.5 fusion.61
  251.3 4.3 copy.142
  255.6 10.0 fusion.637
  265.6 6.1 fusion.65
  284.6 11.6 conditional.12
  296.2 14.4 %collective-permute-start.4 = (bf16[512,768]{1,0:T(8,128)(2,1)}, bf16[512,768]{1,0:T(8,128)(2,1)S(1)}, u32[]{:S(2)}, u32[]{:S(2)}) collective-permute-start(bf16[512,768]{1,0:T(8,128)(2,1)} %get-tuple-element.344), channel_id=1, source_target_pairs={{0,1},{1,2},{2,3},{4,5},{5,6},{6,7},{8,9},{9,10},{10,11},{12,13},{... | collective-permute-start | bytes 2359304 | tf_op jit(solution)/shard_map/ppermute | solution.py:30
  314.7 4.8 conditional.13
  319.5 18.9 %collective-permute-start.5 = (bf16[512,768]{1,0:T(8,128)(2,1)}, bf16[512,768]{1,0:T(8,128)(2,1)S(1)}, u32[]{:S(2)}, u32[]{:S(2)}) collective-permute-start(bf16[512,768]{1,0:T(8,128)(2,1)} %get-tuple-element.346), channel_id=1, source_target_pairs={{0,1},{1,2},{2,3},{4,5},{5,6},{6,7},{8,9},{9,10},{10,11},{12,13},{... | collective-permute-start | bytes 2359304 | tf_op jit(solution)/shard_map/ppermute | solution.py:30
  346.8 19.5 %conditional.15 = (bf16[512,768]{1,0:T(8,128)(2,1)}, f32[3072,768]{1,0:T(8,128)}, f32[4608]{0:T(1024)}, f32[4608]{0:T(1024)S(1)}, bf16[1,512,768]{2,1,0:T(8,128)(2,1)S(1)}, /*index=5*/f32[768,3072]{1,0:T(8,128)}) conditional(s32[]{:T(128)} %clamp.35, () %tuple.170, (bf16[512,768]{1,0:T(8,128)(2,1)S(1)}, ...), branch_computations={%region_45.46_spmd, %region_46.58_spmd, %region_58.67_spmd} | conditional | flops 14631580672 | bytes 313459072 | solution.py:307
  346.8 4.8 broadcast.1750.clone
  351.6 4.3 broadcast.1751
  367.6 38.0 %collective-permute-done.6 = bf16[512,768]{1,0:T(8,128)(2,1)S(1)} collective-permute-done((bf16[512,768]{1,0:T(8,128)(2,1)}, bf16[512,768]{1,0:T(8,128)(2,1)S(1)}, u32[]{:S(2)}, u32[]{:S(2)}) %collective-permute-start.6) | collective-permute-done | bytes 786464 | tf_op jit(solution)/shard_map/ppermute | solution.py:30
  406.8 20.2 %conditional.16 = (bf16[512,768]{1,0:T(8,128)(2,1)}, f32[3072,768]{1,0:T(8,128)}, f32[4608]{0:T(1024)}, f32[4608]{0:T(1024)S(1)}, bf16[1,512,768]{2,1,0:T(8,128)(2,1)}, /*index=5*/f32[768,3072]{1,0:T(8,128)}) conditional(s32[]{:T(128)} %clamp.36, () %tuple.173, (bf16[512,768]{1,0:T(8,128)(2,1)}, bf16[768,3072]{1,0:T(8,128)(2,1)}, ...), branch_computations={%region_67.68_spmd, %region_68.80_spmd, %region_80.89_spmd} | conditional | flops 14631580672 | bytes 285160768 | solution.py:307
  406.8 4.8 broadcast.1797.clone
  411.6 4.2 broadcast.1798
  428.3 12.8 collective-permute-done.7
  441.2 19.8 %conditional.17 = (bf16[512,768]{1,0:T(8,128)(2,1)}, f32[3072,768]{1,0:T(8,128)}, f32[4608]{0:T(1024)}, f32[4608]{0:T(1024)S(1)}, bf16[1,512,768]{2,1,0:T(8,128)(2,1)}, /*index=5*/f32[768,3072]{1,0:T(8,128)}) conditional(s32[]{:T(128)} %clamp.37, () %tuple.176, (bf16[512,768]{1,0:T(8,128)(2,1)}, ...), branch_computations={%region_89.90_spmd, %region_90.102_spmd, %region_102.111_spmd} | conditional | flops 14631580672 | bytes 285160768 | solution.py:307
  441.2 4.7 broadcast.1844.clone
  445.9 4.2 broadcast.1845
  462.3 172.6 %collective-permute-done.8 = bf16[512,768]{1,0:T(8,128)(2,1)S(1)} collective-permute-done((bf16[512,768]{1,0:T(8,128)(2,1)}, bf16[512,768]{1,0:T(8,128)(2,1)S(1)}, u32[]{:S(2)}, u32[]{:S(2)}) %collective-permute-start.8) | collective-permute-done | bytes 786464 | tf_op jit(solution)/shard_map/ppermute | solution.py:30
  634.9 113.6 %conditional.18 = (bf16[512,768]{1,0:T(8,128)(2,1)}, f32[3072,768]{1,0:T(8,128)}, f32[4608]{0:T(1024)}, f32[4608]{0:T(1024)S(1)}, bf16[1,512,768]{2,1,0:T(8,128)(2,1)}, /*index=5*/f32[768,3072]{1,0:T(8,128)}) conditional(s32[]{:T(128)} %clamp.38, () %tuple.179, (bf16[512,768]{1,0:T(8,128)(2,1)}, ...), branch_computations={%region_111.112_spmd, %region_112.124_spmd, %region_124.133_spmd} | conditional | flops 14631580672 | bytes 285081920 | solution.py:307
  634.9 5.7 fusion.474
  643.5 7.1 fusion.673
  650.6 5.9 fusion.496
  666.2 11.4 multiply_reduce_fusion.27
  678.8 7.2 multiply_convert_fusion.3
  691.7 4.9 convolution_bitcast_fusion.6
  698.9 7.9 pad_maximum_fusion.17
  706.8 9.6 copy.224
  724.3 5.4 add_convert_fusion.16
  731.8 4.2 broadcast.1899
  752.9 107.1 %conditional.19 = (f32[3072,768]{1,0:T(8,128)}, f32[4608]{0:T(1024)}, f32[4608]{0:T(1024)S(1)}, bf16[1,512,768]{2,1,0:T(8,128)(2,1)}, f32[768,3072]{1,0:T(8,128)}) conditional(s32[]{:T(128)} %clamp.39, () %tuple.182, (bf16[768,3072]{1,0:T(8,128)(2,1)}, bf16[512,768]{1,0:T(8,128)(2,1)}, f32[4608]{0:T(1024)S(1)}, ...), branch_computations={%region_133.134_spmd, %region_134.146_spmd, %region_146.155_spmd} | conditional | flops 14631580672 | bytes 283509024 | solution.py:307
  753.0 5.7 fusion.538
  761.5 7.1 fusion.678
  768.6 5.9 fusion.560
  784.3 11.5 multiply_reduce_fusion.31
  796.9 7.0 multiply_convert_fusion.4
  809.5 4.8 convolution_bitcast_fusion.8
  816.7 7.9 pad_maximum_fusion.21
  824.5 9.7 copy.227
  834.3 5.4 fusion.563
  847.6 4.1 broadcast.1945
  863.3 16.0 %add_add_fusion.20 = f32[3072,768]{1,0:T(8,128)S(1)} fusion(f32[3072,768]{1,0:T(8,128)} %get-tuple-element.365, f32[3072,768]{1,0:T(8,128)} %get-tuple-element.364, f32[3072,768]{1,0:T(8,128)} %get-tuple-element.363, f32[3072,768]{1,0:T(8,128)} %get-tuple-element.361, f32[3072,768]{1,0:T(8,128)} %get-tuple-element.362), kind=kLoop, calls=%fused_computation.969 | loop fusion | flops 9437184 | bytes 56623104 | tf_op jit(solution)/shard_map/add | solution.py:315
  879.3 4.4 slice_bitcast_fusion.155
  888.5 20.9 %add_bitcast_fusion = f32[1,768,3072]{2,1,0:T(8,128)} fusion(f32[768,3072]{1,0:T(8,128)} %get-tuple-element.380, f32[768,3072]{1,0:T(8,128)} %get-tuple-element.379, f32[768,3072]{1,0:T(8,128)} %get-tuple-element.378, f32[768,3072]{1,0:T(8,128)} %get-tuple-element.376, f32[768,3072]{1,0:T(8,128)} %get-tuple-element.377), kind=kLoop, calls=%fused_computation.970 | loop fusion | flops 9437184 | bytes 56623104 | tf_op jit(solution)/shard_map/broadcast_in_dim | solution.py:331
  911.0 4.3 conditional.14
  917.9 12.1 reduce-scatter.18.cloned.1.call-done
  932.4 95.4 %reduce-scatter.14.cloned.1.call-done = f32[1,192,768]{2,1,0:T(8,128)} async-done(((f32[1,1536,768]{2,1,0:T(8,128)}), f32[1,192,768]{2,1,0:T(8,128)}) %reduce-scatter.14.cloned.1.call-update) | async-done | bytes 589840 | tf_op jit(solution)/shard_map/reduce_scatter | solution.py:332
  1032.3 67.8 %reduce-scatter.16.cloned.1.call-done = f32[576,1]{1,0:T(8,128)} async-done(((f32[4608,1]{1,0:T(8,128)}), f32[576,1]{1,0:T(8,128)}) %reduce-scatter.16.cloned.1.call-update) | async-done | bytes 2320
  1101.8 96.2 %reduce-scatter.12.cloned.1.call-done = f32[1,192,768]{2,1,0:T(8,128)} async-done(((f32[1,1536,768]{2,1,0:T(8,128)}), f32[1,192,768]{2,1,0:T(8,128)}) %reduce-scatter.12.cloned.1.call-update) | async-done | bytes 589840 | tf_op jit(solution)/shard_map/reduce_scatter | solution.py:333
  1198.1 3.1 multiply_add_fusion.2
  1201.2 164.3 %reduce-scatter.10.cloned.1.call-done = f32[1,96,3072]{2,1,0:T(8,128)} async-done(((f32[1,768,3072]{2,1,0:T(8,128)}), f32[1,96,3072]{2,1,0:T(8,128)}) %reduce-scatter.10.cloned.1.call-update) | async-done | bytes 1179664 | tf_op jit(solution)/shard_map/reduce_scatter | solution.py:331
  1365.4 4.7 multiply_add_fusion
  (269 shorter events, 145.4 us)
Async XLA Ops:
  7.2 18.1 %copy-start.86 = (u32[32]{0:T(128)S(1)}, u32[32]{0:T(128)}, u32[]{:S(2)}) copy-start(u32[32]{0:T(128)} %constant.1049) | copy-start | bytes 388
  7.2 59.6 %all-gather.8.cloned.1.call-start = ((), (), s32[]{:S(2)}) async-start(), calls=%async_computation.7 | async-start | bytes 2654208 | tf_op jit(solution)/shard_map/all_gather | solution.py:250
  9.1 111.3 %all-gather.6.cloned.1.call-start = ((), (), s32[]{:S(2)}) async-start(), calls=%async_computation.6 | async-start | bytes 2654208 | tf_op jit(solution)/shard_map/all_gather | solution.py:251
  9.1 3.8 collective-permute-start
  13.6 187.9 %all-gather.4.cloned.1.call-start = ((), (), s32[]{:S(2)}) async-start(), calls=%async_computation.5 | async-start | bytes 5308416 | tf_op jit(solution)/shard_map/all_gather | solution.py:249
  15.9 914.1 %reduce-scatter.18.cloned.1.call-start = ((), (), s32[]{:S(2)}) async-start(), calls=%async_computation.12 | async-start | bytes 2654208
  16.7 10.2 collective-permute-start.1
  238.8 3.4 collective-permute-start.2
  243.7 1.1 copy-start
  265.6 6.1 copy-start.64
  281.2 3.3 copy-start.29
  281.2 3.3 collective-permute-start.3
  296.2 17.1 %collective-permute-start.4 = (bf16[512,768]{1,0:T(8,128)(2,1)}, bf16[512,768]{1,0:T(8,128)(2,1)S(1)}, u32[]{:S(2)}, u32[]{:S(2)}) collective-permute-start(bf16[512,768]{1,0:T(8,128)(2,1)} %get-tuple-element.344), channel_id=1, source_target_pairs={{0,1},{1,2},{2,3},{4,5},{5,6},{6,7},{8,9},{9,10},{10,11},{12,13},{... | collective-permute-start | bytes 2359304 | tf_op jit(solution)/shard_map/ppermute | solution.py:30
  313.3 1.4 copy-start.59
  314.7 26.2 %copy-start.1 = (bf16[2,512,768]{2,1,0:T(8,128)(2,1)S(1)}, bf16[2,512,768]{2,1,0:T(8,128)(2,1)}, u32[]{:S(2)}) copy-start(bf16[2,512,768]{2,1,0:T(8,128)(2,1)} %copy-done) | copy-start | bytes 4718596
  319.5 24.1 %copy-start.60 = (bf16[512,768]{1,0:T(8,128)(2,1)S(1)}, bf16[512,768]{1,0:T(8,128)(2,1)}, u32[]{:S(2)}) copy-start(bf16[512,768]{1,0:T(8,128)(2,1)} %copy-done.59) | copy-start | bytes 2359300
  319.5 24.3 %collective-permute-start.5 = (bf16[512,768]{1,0:T(8,128)(2,1)}, bf16[512,768]{1,0:T(8,128)(2,1)S(1)}, u32[]{:S(2)}, u32[]{:S(2)}) collective-permute-start(bf16[512,768]{1,0:T(8,128)(2,1)} %get-tuple-element.346), channel_id=1, source_target_pairs={{0,1},{1,2},{2,3},{4,5},{5,6},{6,7},{8,9},{9,10},{10,11},{12,13},{... | collective-permute-start | bytes 2359304 | tf_op jit(solution)/shard_map/ppermute | solution.py:30
  343.6 3.2 slice-start.15
  345.0 1.7 slice-start.16
  366.2 40.6 %copy-start.28 = (bf16[1,512,768]{2,1,0:T(8,128)(2,1)}, bf16[1,512,768]{2,1,0:T(8,128)(2,1)S(1)}, u32[]{:S(2)}) copy-start(bf16[1,512,768]{2,1,0:T(8,128)(2,1)S(1)} %get-tuple-element.347) | copy-start | bytes 2359300
  366.2 40.6 %copy-start.69 = (f32[4608]{0:T(1024)}, f32[4608]{0:T(1024)S(1)}, u32[]{:S(2)}) copy-start(f32[4608]{0:T(1024)S(1)} %get-tuple-element.371) | copy-start | bytes 55300
  366.3 39.3 %collective-permute-start.6 = (bf16[512,768]{1,0:T(8,128)(2,1)}, bf16[512,768]{1,0:T(8,128)(2,1)S(1)}, u32[]{:S(2)}, u32[]{:S(2)}) collective-permute-start(bf16[512,768]{1,0:T(8,128)(2,1)} %get-tuple-element.348), channel_id=1, source_target_pairs={{1,0},{2,1},{3,2},{5,4},{6,5},{7,6},{9,8},{10,9},{11,10},{13,12},{... | collective-permute-start | bytes 2359304 | tf_op jit(solution)/shard_map/ppermute | solution.py:30
  427.0 14.2 %copy-start.73 = (f32[4608]{0:T(1024)}, f32[4608]{0:T(1024)S(1)}, u32[]{:S(2)}) copy-start(f32[4608]{0:T(1024)S(1)} %get-tuple-element.372) | copy-start | bytes 55300
  427.0 14.2 %collective-permute-start.7 = (bf16[512,768]{1,0:T(8,128)(2,1)}, bf16[512,768]{1,0:T(8,128)(2,1)S(1)}, u32[]{:S(2)}, u32[]{:S(2)}) collective-permute-start(bf16[512,768]{1,0:T(8,128)(2,1)} %get-tuple-element.350), channel_id=1, source_target_pairs={{1,0},{2,1},{3,2},{5,4},{6,5},{7,6},{9,8},{10,9},{11,10},{13,12},{... | collective-permute-start | bytes 2359304 | tf_op jit(solution)/shard_map/ppermute | solution.py:30
  461.0 173.9 %copy-start.77 = (f32[4608]{0:T(1024)}, f32[4608]{0:T(1024)S(1)}, u32[]{:S(2)}) copy-start(f32[4608]{0:T(1024)S(1)} %get-tuple-element.373) | copy-start | bytes 55300
  461.0 173.9 %collective-permute-start.8 = (bf16[512,768]{1,0:T(8,128)(2,1)}, bf16[512,768]{1,0:T(8,128)(2,1)S(1)}, u32[]{:S(2)}, u32[]{:S(2)}) collective-permute-start(bf16[512,768]{1,0:T(8,128)(2,1)} %get-tuple-element.352), channel_id=1, source_target_pairs={{1,0},{2,1},{3,2},{5,4},{6,5},{7,6},{9,8},{10,9},{11,10},{13,12},{... | collective-permute-start | bytes 2359304 | tf_op jit(solution)/shard_map/ppermute | solution.py:30
  650.6 5.9 copy-start.33
  656.5 4.2 copy-start.52
  666.2 11.4 slice-start.9
  666.2 11.4 slice-start.10
  666.2 12.6 slice-start.11
  689.2 2.5 copy-start.34
  691.7 5.0 copy-start.14
  691.7 4.9 copy-start.53
  748.5 4.4 copy-start.79
  748.5 4.4 collective-permute-start.9
  752.9 107.1 %copy-start.70 = (f32[4608]{0:T(1024)S(1)}, f32[4608]{0:T(1024)}, u32[]{:S(2)}) copy-start(f32[4608]{0:T(1024)} %copy-done.69) | copy-start | bytes 55300
  752.9 107.1 %copy-start.74 = (f32[4608]{0:T(1024)S(1)}, f32[4608]{0:T(1024)}, u32[]{:S(2)}) copy-start(f32[4608]{0:T(1024)} %copy-done.73) | copy-start | bytes 55300
  752.9 107.2 %copy-start.78 = (f32[4608]{0:T(1024)S(1)}, f32[4608]{0:T(1024)}, u32[]{:S(2)}) copy-start(f32[4608]{0:T(1024)} %copy-done.77) | copy-start | bytes 55300
  752.9 107.2 %copy-start.80 = (f32[4608]{0:T(1024)S(1)}, f32[4608]{0:T(1024)}, u32[]{:S(2)}) copy-start(f32[4608]{0:T(1024)} %copy-done.79) | copy-start | bytes 55300
  768.6 5.9 copy-start.30
  774.5 4.2 copy-start.54
  784.3 11.5 slice-start.12
  784.3 11.5 slice-start.13
  784.3 12.6 slice-start.14
  807.0 2.5 copy-start.31
  809.5 4.9 copy-start.16
  809.5 4.8 copy-start.55
  863.2 164.6 %reduce-scatter.14.cloned.1.call-start = ((), (), s32[]{:S(2)}) async-start(), calls=%async_computation.10 | async-start | bytes 5308416 | tf_op jit(solution)/shard_map/reduce_scatter | solution.py:332
  879.3 4.5 copy-start.68
  879.3 4.5 copy-start.72
  879.3 4.5 copy-start.76
  883.8 216.3 %reduce-scatter.16.cloned.1.call-start = ((), (), s32[]{:S(2)}) async-start(), calls=%async_computation.11 | async-start | bytes 2654208
  887.7 310.4 %reduce-scatter.12.cloned.1.call-start = ((), (), s32[]{:S(2)}) async-start(), calls=%async_computation.9 | async-start | bytes 5308416 | tf_op jit(solution)/shard_map/reduce_scatter | solution.py:333
  888.4 477.0 %reduce-scatter.10.cloned.1.call-start = ((), (), s32[]{:S(2)}) async-start(), calls=%async_computation.8 | async-start | bytes 10616832 | tf_op jit(solution)/shard_map/reduce_scatter | solution.py:331
  909.3 1.4 copy-start.3
  909.4 1.7 copy-start.57
  915.6 185.5 %copy-start.81 = (f32[1,576]{1,0:T(1,128)S(1)}, f32[1,576]{1,0:T(1,128)}, u32[]{:S(2)}) copy-start(f32[1,576]{1,0:T(1,128)} %param.49) | copy-start | bytes 6916
  915.6 185.5 %copy-start.82 = (f32[1,576]{1,0:T(1,128)S(1)}, f32[1,576]{1,0:T(1,128)}, u32[]{:S(2)}) copy-start(f32[1,576]{1,0:T(1,128)} %param.50) | copy-start | bytes 6916
  915.6 185.5 %copy-start.83 = (f32[1,576]{1,0:T(1,128)S(1)}, f32[1,576]{1,0:T(1,128)}, u32[]{:S(2)}) copy-start(f32[1,576]{1,0:T(1,128)} %param.51) | copy-start | bytes 6916
  915.9 454.2 %copy-start.4 = (bf16[2,512,768]{2,1,0:T(8,128)(2,1)}, bf16[2,512,768]{2,1,0:T(8,128)(2,1)S(1)}, u32[]{:S(2)}) copy-start(bf16[2,512,768]{2,1,0:T(8,128)(2,1)S(1)} %select_dynamic-update-slice_fusion.5) | copy-start | bytes 4718596
  931.0 170.1 %collective-permute-start.11 = (bf16[1,576]{1,0:T(2,128)(2,1)S(1)}, bf16[1,576]{1,0:T(2,128)(2,1)S(1)}, u32[]{:S(2)}, u32[]{:S(2)}) collective-permute-start(bf16[1,576]{1,0:T(2,128)(2,1)S(1)} %copy.213), channel_id=1, source_target_pairs={{1,0},{2,1},{3,2},{5,4},{6,5},{7,6},{9,8},{10,9},{11,10},{13,12},{... | collective-permute-start | bytes 3464 | tf_op jit(solution)/shard_map/ppermute | solution.py:30
  1029.6 168.5 %collective-permute-start.10 = (bf16[1,192,768]{2,1,0:T(8,128)(2,1)}, bf16[1,192,768]{2,1,0:T(8,128)(2,1)S(1)}, u32[]{:S(2)}, u32[]{:S(2)}) collective-permute-start(bf16[1,192,768]{2,1,0:T(8,128)(2,1)} %convert_element_type.611), channel_id=1, source_target_pairs={{1,0},{2,1},{3,2},{5,4},{6,5},{7,6},{9,8},{10,9},{11,10},{13,12},{... | collective-permute-start | bytes 884744 | tf_op jit(solution)/shard_map/ppermute | solution.py:30
  1032.3 337.8 %copy-start.5 = (bf16[2,512,768]{2,1,0:T(8,128)(2,1)}, bf16[2,512,768]{2,1,0:T(8,128)(2,1)S(1)}, u32[]{:S(2)}) copy-start(bf16[2,512,768]{2,1,0:T(8,128)(2,1)S(1)} %select_dynamic-update-slice_fusion) | copy-start | bytes 4718596
  (6 other events, 5.9 us)
Sparse Core Ops, SparseCore 0:
  10.8 55.9 all-gather.7
  69.5 50.7 all-gather.5
  123.1 78.4 all-gather.3
  863.3 66.5 reduce-scatter.17
  933.4 94.3 reduce-scatter.13
  1031.1 68.8 reduce-scatter.15
  1103.7 94.3 reduce-scatter.11
  1202.2 163.1 reduce-scatter.9
where the time goes:
time: 1390 us; the launch traced here: 1380 us
  waiting for transfers between devices  799 us (57%)
  matrix products  154 us (11%)
  local copies, waits for them, and re-layouts  127 us (9%)
  other arithmetic  112 us (8%)
  loops' own time  76.8 us (6%)
  starting transfers between devices  54.3 us (4%)
  blocking collectives  38.4 us (3%)
  between operations  15.8 us (1%)
    ppermute x12, waiting for transfers between devices, shifted(): lax.ppermute(value, axis, [(source, source + steps) for source in range(l...  231 us
    reduce_scatter x1, waiting for transfers between devices, on_device(): lax.psum_scatter(in_total[None], 'dp', scatter_dimension=1, tiled=True)  164 us
    reduce_scatter x1, waiting for transfers between devices, on_device(): lax.psum_scatter(down_total[None, half_rows:], 'dp', scatter_dimension=1,...  96.2 us
    reduce_scatter x1, waiting for transfers between devices, on_device(): lax.psum_scatter(down_total[None, :half_rows], 'dp', scatter_dimension=1,...  95.4 us
    unnamed x10, waiting for transfers between devices  80.6 us
    all_gather x1, waiting for transfers between devices, on_device(): lax.all_gather(in_master.astype(jnp.bfloat16), 'dp', axis=1, tiled=True)  76.4 us
    ppermute x12, starting transfers between devices, shifted(): lax.ppermute(value, axis, [(source, source + steps) for source in range(l...  54 us
    all_gather x1, waiting for transfers between devices, on_device(): lax.all_gather(nearby_down.astype(jnp.bfloat16), 'dp', axis=1, tiled=True)  53.5 us
  transfers between devices with their start and end apart: 20, of which 15 were waited for; matrix products, arithmetic and copies ran while one was open for 6% of the time, Pallas kernels for 0%

commit v1 on v0

v1 whole, which is shorter than its diff:
```python
import jax
import jax.numpy as jnp
from jax import lax
from jax.sharding import Mesh
from jax.sharding import PartitionSpec as P

D = 768
HEADS = 12
HEAD_DIM = 64
FF = 3072
SEQ = 512
VEC = 4608
HALF = D // 2
LANES = 384

NORM_EPSILON = 1e-05
BETA_ONE = 0.9
BETA_TWO = 0.98
BIAS_ONE = 1.0 - 0.9**10
BIAS_TWO = 1.0 - 0.98**10
WEIGHT_DECAY = 0.01
ADAM_EPSILON = 1e-06
ROOT_HALF = 0.7071067811865476
ROOT_TWO_PI = 2.5066282746310002
SCALE = HEAD_DIM**-0.5

AXES = ("dp", "x", "c")
LOW = jnp.bfloat16
WIDE = jnp.float32


def product(former, latter):
    return jnp.dot(former, latter, preferred_element_type=WIDE)


def inner_rows(former, latter):
    return lax.dot_general(former, latter, (((0,), (0,)), ((), ())), preferred_element_type=WIDE)


def outer_cols(former, latter):
    return lax.dot_general(former, latter, (((1,), (1,)), ((), ())), preferred_element_type=WIDE)


class Links:
    def __init__(self):
        self.count = lax.axis_size("dp")
        self.bits = self.count.bit_length() - 1
        self.dp = lax.axis_index("dp")
        self.x = lax.axis_index("x")
        self.c = lax.axis_index("c")

    def own(self, bit):
        if bit == "c":
            return self.c
        if bit == "x":
            return self.x
        return (self.dp >> bit) & 1

    def flip(self, value, bit):
        step = {"c": 1, "x": 2}.get(bit)
        if step is None:
            step = 4 << bit
        pairs = [(place, place ^ step) for place in range(4 * self.count)]
        return lax.ppermute(value, AXES, pairs)

    def axis(self, bit):
        return 0 if bit == "x" else self.bits - bit

    def gather(self, shard, order):
        held = shard.reshape((1,) * (self.bits + 1) + shard.shape)
        for bit in order:
            got = self.flip(held, bit)
            first = self.own(bit) == 0
            held = jnp.concatenate(
                [jnp.where(first, held, got), jnp.where(first, got, held)], axis=self.axis(bit)
            )
        return held.reshape((2, self.count) + shard.shape)

    def scatter(self, parts, order):
        held = parts.reshape((2,) * (self.bits + 1) + parts.shape[2:])
        for bit in order:
            own, axis = self.own(bit), self.axis(bit)
            kept = lax.dynamic_slice_in_dim(held, own, 1, axis)
            sent = lax.dynamic_slice_in_dim(held, 1 - own, 1, axis)
            got = self.flip(sent, bit)
            held = (kept.astype(WIDE) + got.astype(WIDE)).astype(parts.dtype)
        return held.reshape(parts.shape[2:])


def norm_forward(summed, norm_gain, norm_bias):
    average = jnp.mean(summed, axis=-1, keepdims=True)
    centered = summed - average
    variance = jnp.mean(centered * centered, axis=-1, keepdims=True)
    inverse_spread = lax.rsqrt(variance + NORM_EPSILON)
    normed = centered * inverse_spread
    return (normed * norm_gain + norm_bias).astype(LOW), normed, inverse_spread


def norm_backward(incoming, normed, inverse_spread, norm_gain):
    incoming = incoming.astype(WIDE)
    through = incoming * norm_gain
    summed_grad = inverse_spread * (
        through
        - jnp.mean(through, axis=-1, keepdims=True)
        - normed * jnp.mean(through * normed, axis=-1, keepdims=True)
    )
    return summed_grad, jnp.sum(incoming * normed, axis=0), jnp.sum(incoming, axis=0)


def attend_forward(links, hidden, w_qkv, w_out, bias_qkv, vector):
    rows = hidden.shape[0]
    mixing = (product(hidden, w_qkv) + bias_qkv).astype(LOW)
    queries, key_rows, value_rows = [
        mixing[:, i * HALF : (i + 1) * HALF].reshape(rows, HEADS // 2, HEAD_DIM) for i in range(3)
    ]
    scores = jnp.einsum("qhd,khd->hqk", queries, key_rows, preferred_element_type=WIDE) * SCALE
    chances = jax.nn.softmax(scores, axis=-1)
    context = jnp.einsum(
        "hqk,khd->qhd", chances.astype(LOW), value_rows, preferred_element_type=WIDE
    )
    context = context.reshape(rows, HALF).astype(LOW)
    part = product(context, w_out)
    branch = part + links.flip(part.astype(LOW), "c").astype(WIDE) + vector[2 * D : 3 * D]
    result, normed, spread = norm_forward(
        hidden.astype(WIDE) + branch, vector[FF : FF + D], vector[FF + D :]
    )
    return result, (hidden, queries, key_rows, value_rows, chances, context, normed, spread)


def feed_forward(links, hidden, w_up, w_down, bias_up, vector, nearby):
    before = product(hidden, w_up) + bias_up
    curve = 0.5 * (1.0 + lax.erf(before * ROOT_HALF))
    active = (before * curve).astype(LOW)
    slope = curve + before * jnp.exp(-0.5 * before * before) / ROOT_TWO_PI
    part = product(active, w_down)
    branch = part + links.flip(part.astype(LOW), "c").astype(WIDE) + nearby[3 * D : FF]
    result, normed, spread = norm_forward(
        hidden.astype(WIDE) + branch, vector[FF : FF + D], vector[FF + D :]
    )
    return result, (hidden, active, slope, normed, spread)


def attend_backward(links, incoming, saved, w_qkv, w_out, vector):
    hidden, queries, key_rows, value_rows, chances, context, normed, spread = saved
    rows = hidden.shape[0]
    summed_grad, gain_grad, bias_grad = norm_backward(
        incoming, normed, spread, vector[FF : FF + D]
    )
    branch_low = summed_grad.astype(LOW)
    out_grad = inner_rows(context, branch_low)
    context_grad = (
        outer_cols(branch_low, w_out).astype(LOW).reshape(rows, HEADS // 2, HEAD_DIM)
    )
    chance_grad = jnp.einsum(
        "qhd,khd->hqk", context_grad, value_rows, preferred_element_type=WIDE
    )
    score_grad = (
        chances * (chance_grad - jnp.sum(chances * chance_grad, axis=-1, keepdims=True))
    ).astype(LOW)
    query_grad = jnp.einsum("hqk,khd->qhd", score_grad, key_rows, preferred_element_type=WIDE)
    key_grad = jnp.einsum("hqk,qhd->khd", score_grad, queries, preferred_element_type=WIDE)
    value_grad = jnp.einsum(
        "hqk,qhd->khd", chances.astype(LOW), context_grad, preferred_element_type=WIDE
    )
    mixing_grad = jnp.concatenate(
        [
            (query_grad * SCALE).astype(LOW).reshape(rows, HALF),
            (key_grad * SCALE).astype(LOW).reshape(rows, HALF),
            value_grad.astype(LOW).reshape(rows, HALF),
        ],
        axis=1,
    )
    mixing_sum = jnp.sum(mixing_grad.astype(WIDE), axis=0)
    qkv_grad = inner_rows(hidden, mixing_grad)
    part = outer_cols(mixing_grad, w_qkv)
    hidden_grad = (
        summed_grad + part + links.flip(part.astype(LOW), "c").astype(WIDE)
    ).astype(LOW)
    return (
        hidden_grad,
        qkv_grad,
        out_grad,
        mixing_sum[:HALF],
        mixing_sum[2 * HALF :],
        jnp.sum(summed_grad, axis=0),
        gain_grad,
        bias_grad,
    )


def feed_backward(links, incoming, saved, w_up, w_down, vector):
    hidden, active, slope, normed, spread = saved
    summed_grad, gain_grad, bias_grad = norm_backward(
        incoming, normed, spread, vector[FF : FF + D]
    )
    branch_low = summed_grad.astype(LOW)
    down_grad = inner_rows(active, branch_low)
    before_grad = (outer_cols(branch_low, w_down) * slope).astype(LOW)
    up_grad = inner_rows(hidden, before_grad)
    part = outer_cols(before_grad, w_up)
    hidden_grad = (
        summed_grad + part + links.flip(part.astype(LOW), "c").astype(WIDE)
    ).astype(LOW)
    return (
        hidden_grad,
        down_grad,
        up_grad,
        jnp.sum(before_grad.astype(WIDE), axis=0),
        jnp.sum(summed_grad, axis=0),
        gain_grad,
        bias_grad,
    )


def adam_update(master, first, second, gradient):
    first_new = BETA_ONE * first + (1.0 - BETA_ONE) * gradient
    second_new = BETA_TWO * second + (1.0 - BETA_TWO) * gradient * gradient
    update = first_new / BIAS_ONE / (jnp.sqrt(second_new / BIAS_TWO) + ADAM_EPSILON)
    return (update + WEIGHT_DECAY * master, first_new, second_new)


def blocks_of(whole, rows):
    return whole.reshape(rows, 8, LANES).transpose(1, 0, 2)


def padded_rows(flat):
    rows = -(-flat.shape[-1] // LANES)
    rows = -(-rows // 16) * 16
    pad = [(0, 0)] * (flat.ndim - 1) + [(0, rows * LANES - flat.shape[-1])]
    return jnp.pad(flat, pad).reshape(flat.shape[:-1] + (rows, LANES))


def on_device(
    inputs,
    cotangent,
    in_master,
    in_first,
    in_second,
    down_master,
    down_first,
    down_second,
    vec_master,
    vec_first,
    vec_second,
):
    links = Links()
    count, x, c = links.count, links.x, links.c
    dp_bits = list(range(links.bits))[::-1]
    rows = D // count
    half_rows = rows // 2
    vec_part = VEC // count
    first_core = c == 0

    blocks = blocks_of(in_master[0].astype(LOW), rows)
    out_rows = blocks[6:8]
    sent = jnp.where(
        first_core,
        jnp.concatenate([blocks[1:6:2], out_rows[:, half_rows:].reshape(1, rows, LANES)]),
        blocks[:4],
    )
    kept = jnp.where(
        first_core,
        jnp.concatenate([blocks[0:6:2], out_rows[:, :half_rows].reshape(1, rows, LANES)]),
        blocks[4:],
    )
    vec_high = lax.reduce_precision(vec_master[0], 8, 7)
    vec_both = jnp.concatenate([vec_high, vec_master[0] - vec_high]).astype(LOW)
    vec_rows = padded_rows(vec_both)
    got = links.flip(
        jnp.concatenate([sent.reshape(4 * rows, LANES), vec_rows]), "c"
    )
    vec_got = got[4 * rows :]
    got = got[: 4 * rows].reshape(4, rows, LANES)
    attend_shard = jnp.where(first_core, kept, got)
    up_shard = jnp.where(first_core, got, kept)
    vec_shard = jnp.concatenate(
        [jnp.where(first_core, vec_rows, vec_got), jnp.where(first_core, vec_got, vec_rows)]
    )
    down_shard = down_master[0].astype(LOW)

    attend_all = links.gather(
        jnp.concatenate([attend_shard.reshape(4 * rows, LANES), vec_shard]), dp_bits + ["x"]
    )
    up_all = links.gather(up_shard.reshape(4 * rows, LANES), dp_bits[:-1] + ["x"] + dp_bits[-1:])
    down_all = links.gather(down_shard, dp_bits + ["x"])

    vec_all = attend_all[:, :, 4 * rows :].reshape(2, count, 2, -1)[..., : 2 * vec_part]
    vec_all = vec_all.reshape(2, count, 2, 2, vec_part).astype(WIDE)
    vec_all = (vec_all[:, :, :, 0] + vec_all[:, :, :, 1]).transpose(0, 2, 1, 3).reshape(2, 2, VEC)

    attend_all = attend_all[:, :, : 4 * rows].reshape(2, count, 4, rows, LANES)
    qkv_all = attend_all[:, :, :3].transpose(0, 1, 3, 2, 4).reshape(2, D, 3 * HALF)
    out_all = attend_all[:, :, 3].reshape(2, count, 2, half_rows, LANES)
    out_all = out_all.transpose(0, 1, 3, 2, 4).reshape(2, 2, count // 2, half_rows, D)
    out_own = jnp.where(first_core, out_all[:, 0], out_all[:, 1])
    out_got = links.flip(jnp.where(first_core, out_all[:, 1], out_all[:, 0]), "c")
    out_full = jnp.concatenate(
        [jnp.where(first_core, out_own, out_got), jnp.where(first_core, out_got, out_own)], axis=2
    ).reshape(2, HALF, D)
    up_full = up_all.reshape(2, count, 4, rows, LANES).transpose(0, 1, 3, 2, 4).reshape(2, D, FF // 2)
    down_full = down_all.reshape(2, FF // 2, D)

    def half_of(vector, start, width):
        return jnp.where(
            first_core, vector[start : start + width], vector[start + width : start + 2 * width]
        )

    hidden = lax.dynamic_slice_in_dim(inputs, x * SEQ, SEQ, 0)
    outputs, kept_parts = [], []
    for layer in range(2):
        attend_vec, feed_vec = vec_all[layer, 0], vec_all[layer, 1]
        bias_qkv = jnp.concatenate(
            [half_of(attend_vec, 0, HALF), jnp.zeros((HALF,), WIDE), half_of(attend_vec, D, HALF)]
        )
        hidden, saved = attend_forward(
            links, hidden, qkv_all[layer], out_full[layer], bias_qkv, attend_vec
        )
        outputs.append(hidden)
        kept_parts.append(saved)
        hidden, saved = feed_forward(
            links,
            hidden,
            up_full[layer],
            down_full[layer],
            half_of(feed_vec, 0, FF // 2),
            feed_vec,
            attend_vec,
        )
        outputs.append(hidden)
        kept_parts.append(saved)

    def to_sections(values):
        own = jnp.where(x == 0, *[jnp.where(first_core, values[2 * i], values[2 * i + 1]) for i in (0, 1)])
        away = jnp.where(x == 0, *[jnp.where(first_core, values[2 * i], values[2 * i + 1]) for i in (1, 0)])
        got = links.flip(away, "x")
        return jnp.concatenate([jnp.where(x == 0, own, got), jnp.where(x == 0, got, own)])[None]

    section_outputs = to_sections(outputs)

    def wide_half(value, width):
        zeros = jnp.zeros((width,), WIDE)
        return [jnp.where(first_core, value, zeros), jnp.where(first_core, zeros, value)]

    def scatter_rows(parts, order):
        n, lanes = parts.shape[1], parts.shape[3]
        split = parts.reshape(count, n, 2, half_rows, lanes).transpose(2, 0, 1, 3, 4)
        return links.scatter(split.reshape(2, count, n * half_rows, lanes), order)

    order_one = ["x"] + dp_bits[::-1]
    order_two = dp_bits[-1:] + ["x"] + dp_bits[:-1][::-1]
    grad = lax.dynamic_slice_in_dim(cotangent, x * SEQ, SEQ, 0)
    grads, vec_grads, sums = [None] * 4, [None] * 2, [None] * 2
    once = jnp.where(first_core, 1.0, 0.0)
    for layer in (1, 0):
        attend_vec, feed_vec = vec_all[layer, 0], vec_all[layer, 1]
        grad, down_grad, up_grad, up_sum, branch_sum, gain_sum, bias_sum = feed_backward(
            links, grad, kept_parts[2 * layer + 1], up_full[layer], down_full[layer], feed_vec
        )
        grads[2 * layer + 1] = grad
        down_sum = scatter_rows(down_grad.astype(LOW).reshape(count, 1, 2 * rows, D).reshape(count, 2, rows, D), order_one)
        up_sum_w = scatter_rows(
            up_grad.astype(LOW).reshape(count, rows, 4, LANES).transpose(0, 2, 1, 3), order_two
        )
        feed_grads = jnp.concatenate(
            wide_half(up_sum, FF // 2) + [once * gain_sum, once * bias_sum]
        )
        down_bias = once * branch_sum
        grad, qkv_grad, out_grad, query_sum, value_sum, branch_sum, gain_sum, bias_sum = (
            attend_backward(
                links, grad, kept_parts[2 * layer], qkv_all[layer], out_full[layer], attend_vec
            )
        )
        grads[2 * layer] = grad
        out_parts = out_grad.astype(LOW).reshape(count // 2, 2, half_rows, D)
        out_got = links.flip(jnp.where(first_core, out_parts[:, 1], out_parts[:, 0]), "c")
        out_own = jnp.where(first_core, out_parts[:, 0], out_parts[:, 1])
        out_parts = jnp.concatenate(
            [jnp.where(first_core, out_own, out_got), jnp.where(first_core, out_got, out_own)]
        )
        out_parts = out_parts.reshape(count, half_rows, 2, LANES).transpose(0, 2, 1, 3)
        attend_parts = jnp.concatenate(
            [
                qkv_grad.astype(LOW).reshape(count, rows, 3, LANES).transpose(0, 2, 1, 3),
                out_parts.reshape(count, 1, rows, LANES),
            ],
            axis=1,
        )
        attend_grads = jnp.concatenate(
            wide_half(query_sum, HALF)
            + wide_half(value_sum, HALF)
            + [once * branch_sum, down_bias, once * gain_sum, once * bias_sum]
        )
        vec_grads[layer] = (
            jnp.stack([attend_grads, feed_grads]).reshape(2, count, vec_part).transpose(1, 0, 2)
        )
        if layer:
            sums[layer] = [scatter_rows(attend_parts, order_two), up_sum_w, down_sum]
        else:
            split = attend_parts.reshape(count, 4, 2, half_rows, LANES).transpose(2, 0, 1, 3, 4)
            split = split.reshape(2, count, 4 * half_rows, LANES)
            vec_rows = padded_rows(jnp.stack(vec_grads).astype(LOW).reshape(2, count, -1))
            last = links.scatter(jnp.concatenate([split, vec_rows], axis=2), order_two)
            vec_last = last[4 * half_rows :]
            sums[layer] = [last[: 4 * half_rows], up_sum_w, down_sum]

    section_input_grads = to_sections(grads)

    flat = [jnp.concatenate([part.reshape(-1, LANES) for part in sums[i]]) for i in (0, 1)]
    own = jnp.where(x == 0, flat[0], flat[1])
    got = links.flip(jnp.where(x == 0, flat[1], flat[0]), "x")
    whole = [jnp.where(x == 0, own, got), jnp.where(x == 0, got, own)]
    n = 4 * half_rows
    both = [
        jnp.stack([w[i * n : (i + 1) * n].reshape(4, half_rows, LANES) for w in whole], axis=1).reshape(4, rows, LANES)
        for i in (0, 1)
    ]
    attend_sum, up_sum = both
    down_sum = jnp.stack(
        [w[2 * n :].reshape(2, half_rows, D) for w in whole], axis=1
    ).reshape(2 * rows, D)

    sent = jnp.where(first_core, up_sum, attend_sum).reshape(4 * rows, LANES)
    got = links.flip(jnp.concatenate([sent, vec_last]), "c")
    vec_got = got[4 * rows :]
    got = got[: 4 * rows].reshape(4, rows, LANES)
    kept = jnp.where(first_core, attend_sum, up_sum)

    def sides(part):
        return part.reshape(2, half_rows, LANES)

    attend_cols = [part for i in range(3) for part in (kept[i], got[i])] + [
        jnp.concatenate([sides(kept[3])[i], sides(got[3])[i]]) for i in (0, 1)
    ]
    up_cols = [got[i] for i in range(4)] + [kept[i] for i in range(4)]
    in_sum = jnp.concatenate(
        [jnp.where(first_core, a, u).astype(WIDE) for a, u in zip(attend_cols, up_cols)], axis=1
    )[None]
    down_sum = down_sum.astype(WIDE)[None]

    def vec_of(part):
        flat_vec = part.reshape(-1)[: 2 * vec_part].astype(WIDE)
        return jnp.where(first_core, flat_vec[:vec_part], flat_vec[vec_part:])

    vec_sum = (vec_of(vec_last) + vec_of(vec_got))[None]

    in_step, in_first_new, in_second_new = adam_update(in_master, in_first, in_second, in_sum)
    down_step, down_first_new, down_second_new = adam_update(
        down_master, down_first, down_second, down_sum
    )
    vec_step, vec_first_new, vec_second_new = adam_update(
        vec_master, vec_first, vec_second, vec_sum
    )
    return (
        section_outputs,
        section_input_grads,
        in_sum,
        down_sum,
        vec_sum,
        in_step,
        in_first_new,
        in_second_new,
        down_step,
        down_first_new,
        down_second_new,
        vec_step,
        vec_first_new,
        vec_second_new,
    )


def solution(mesh):
    grid = Mesh(mesh.devices.reshape(mesh.shape["dp"], 2, 2), AXES)
    tokens = P("dp", None)
    matrix = P(("x", "c"), "dp", None)
    vector = P(("x", "c"), "dp")
    return jax.shard_map(
        on_device,
        mesh=grid,
        in_specs=(tokens,) * 2 + (matrix,) * 6 + (vector,) * 3,
        out_specs=(matrix,) * 4 + (vector,) + (matrix,) * 6 + (vector,) * 3,
        check_vma=False,
    )
```

time: 1390 us -> 629 us (0.45)
  waiting for transfers between devices: 799 us -> 230 us
  loops' own time: 76.8 us -> 0 us
  matrix products: 154 us -> 83.9 us
  blocking collectives: 38.4 us -> 0 us
  local copies, waits for them, and re-layouts: 127 us -> 145 us
  other arithmetic: 112 us -> 98.1 us
    reduce_scatter x3 -> x0, waiting for transfers between devices: 356 us -> none  [the longest x1 164 us: on_device(): lax.psum_scatter(in_total[None], 'dp', scatter_dimension=1, tiled=True)]
    all_gather x3 -> x0, waiting for transfers between devices: 131 us -> none  [the longest x1 76.4 us: on_device(): lax.all_gather(in_master.astype(jnp.bfloat16), 'dp', axis=1, tiled=True)]
    unnamed x10 -> x0, waiting for transfers between devices: 80.6 us -> none
    another operation x10 -> x0, loops' own time: 76.8 us -> none  [the longest x5 47 us: on_device(): lax.switch(branch_index, [spare_backward, attention_backward, feed_backwa...]
    dot_general x20 -> x18, matrix products: 89 us -> 33.9 us  [the longest x8 17.7 us: product(): return jnp.dot(former, latter, preferred_element_type=WIDE)]
    cond x53 -> x0, local copies, waits for them, and re-layouts: 39.8 us -> none
    squeeze x1 -> x0, blocking collectives: 38.4 us -> none  [on_device(): vector[0]]
    another operation x28 -> x14, local copies, waits for them, and re-layouts: 42.2 us -> 6.29 us  [the longest x4 2.95 us: on_device(): jnp.stack([attend_grads, feed_grads]).reshape(2, count, vec_part)]
  transfers between devices with their start and end apart: 20 -> 52, of which waited for: 15 -> 27; matrix products, arithmetic and copies ran while one was open for 6% -> 34% of each run, Pallas kernels for 0% -> 0%
where the time goes in v1:
time: 629 us; the launch traced here: 617 us
  waiting for transfers between devices  230 us (37%)
  local copies, waits for them, and re-layouts  145 us (23%)
  other arithmetic  98.1 us (16%)
  matrix products  83.9 us (13%)
  starting transfers between devices  56 us (9%)
    ppermute x52, waiting for transfers between devices, flip(): return lax.ppermute(value, AXES, pairs)  230 us
    ppermute x52, starting transfers between devices, flip(): return lax.ppermute(value, AXES, pairs)  56 us
    unnamed x341, local copies, waits for them, and re-layouts  37.1 us
    dot_general x8, matrix products, inner_rows(): lax.dot_general(former, latter, (((0,), (0,)), ((), ())), preferred_eleme...  19.9 us
    dot_general x8, matrix products, outer_cols(): lax.dot_general(former, latter, (((1,), (1,)), ((), ())), preferred_eleme...  18.8 us
    dot_general x8, matrix products, product(): return jnp.dot(former, latter, preferred_element_type=WIDE)  17.7 us
    convert_element_type x21, other arithmetic, scatter(): held = (kept.astype(WIDE) + got.astype(WIDE)).astype(parts.dtype)  14.4 us
  transfers between devices with their start and end apart: 52, of which 27 were waited for; matrix products, arithmetic and copies ran while one was open for 34% of the time, Pallas kernels for 0%

profile of v1, /device:TPU:0, one launch (start us, length us, event | category | flops | bytes accessed | tf_op | source)
XLA Modules:
  0.0 617.2 jit_solution(13720861790647275318)
XLA Ops:
  1.7 4.1 collective-permute-start.11
  10.9 8.3 %collective-permute-done.11 = bf16[1,1,1,1,192,768]{5,4,3,2,1,0:T(8,128)(2,1)S(1)} collective-permute-done((bf16[1,1,1,1,192,768]{5,4,3,2,1,0:T(8,128)(2,1)S(1)}, bf16[1,1,1,1,192,768]{5,4,3,2,1,0:T(8,128)(2,1)S(1)}, u32[]{:S(2)}, u32[]{:S(2)}) %collective-permute-start.11) | collective-permute-done | bytes 294944 | tf_op jit(solution)/shard_map/ppermute | solution.py:64
  20.9 3.4 collective-permute-start.7
  24.4 15.7 %collective-permute-done.7 = bf16[1,1,1,1,384,384]{5,4,3,2,1,0:T(8,128)(2,1)S(1)} collective-permute-done((bf16[1,1,1,1,384,384]{5,4,3,2,1,0:T(8,128)(2,1)S(1)}, bf16[1,1,1,1,384,384]{5,4,3,2,1,0:T(8,128)(2,1)S(1)}, u32[]{:S(2)}, u32[]{:S(2)}) %collective-permute-start.7) | collective-permute-done | bytes 294944 | tf_op jit(solution)/shard_map/ppermute | solution.py:64
  40.3 3.9 collective-permute-start.8
  44.2 7.2 %collective-permute-done.1 = bf16[1,1,1,1,416,384]{5,4,3,2,1,0:T(8,128)(2,1)S(1)} collective-permute-done((bf16[1,1,1,1,416,384]{5,4,3,2,1,0:T(8,128)(2,1)S(1)}, bf16[1,1,1,1,416,384]{5,4,3,2,1,0:T(8,128)(2,1)S(1)}, u32[]{:S(2)}, u32[]{:S(2)}) %collective-permute-start.1) | collective-permute-done | bytes 319520 | tf_op jit(solution)/shard_map/ppermute | solution.py:64
  54.4 6.8 %collective-permute-done.8 = bf16[1,2,1,1,384,384]{5,4,3,2,1,0:T(8,128)(2,1)S(1)} collective-permute-done((bf16[1,2,1,1,384,384]{5,4,3,2,1,0:T(8,128)(2,1)S(1)}, bf16[1,2,1,1,384,384]{5,4,3,2,1,0:T(8,128)(2,1)S(1)}, u32[]{:S(2)}, u32[]{:S(2)}) %collective-permute-start.8) | collective-permute-done | bytes 589856 | tf_op jit(solution)/shard_map/ppermute | solution.py:64
  63.5 9.9 %collective-permute-done.2 = bf16[1,2,1,1,416,384]{5,4,3,2,1,0:T(8,128)(2,1)S(1)} collective-permute-done((bf16[1,2,1,1,416,384]{5,4,3,2,1,0:T(8,128)(2,1)S(1)}, bf16[1,2,1,1,416,384]{5,4,3,2,1,0:T(8,128)(2,1)S(1)}, u32[]{:S(2)}, u32[]{:S(2)}) %collective-permute-start.2) | collective-permute-done | bytes 639008 | tf_op jit(solution)/shard_map/ppermute | solution.py:64
  76.8 5.3 collective-permute-done.13
  87.2 3.7 collective-permute-done.9
  96.2 13.3 %collective-permute-done.3 = bf16[1,2,2,1,416,384]{5,4,3,2,1,0:T(8,128)(2,1)} collective-permute-done((bf16[1,2,2,1,416,384]{5,4,3,2,1,0:T(8,128)(2,1)}, bf16[1,2,2,1,416,384]{5,4,3,2,1,0:T(8,128)(2,1)}, u32[]{:S(2)}, u32[]{:S(2)}) %collective-permute-start.3) | collective-permute-done | bytes 1277984 | tf_op jit(solution)/shard_map/ppermute | solution.py:64
  114.4 27.0 %collective-permute-done.14 = bf16[1,2,2,2,192,768]{5,4,3,2,1,0:T(8,128)(2,1)} collective-permute-done((bf16[1,2,2,2,192,768]{5,4,3,2,1,0:T(8,128)(2,1)}, bf16[1,2,2,2,192,768]{5,4,3,2,1,0:T(8,128)(2,1)}, u32[]{:S(2)}, u32[]{:S(2)}) %collective-permute-start.14) | collective-permute-done | bytes 2359328 | tf_op jit(solution)/shard_map/ppermute | solution.py:64
  141.5 4.9 broadcast_select_fusion.2
  146.4 11.7 %collective-permute-done.10 = bf16[2,2,2,1,384,384]{5,4,3,2,1,0:T(8,128)(2,1)} collective-permute-done((bf16[2,2,2,1,384,384]{5,4,3,2,1,0:T(8,128)(2,1)}, bf16[2,2,2,1,384,384]{5,4,3,2,1,0:T(8,128)(2,1)}, u32[]{:S(2)}, u32[]{:S(2)}) %collective-permute-start.10) | collective-permute-done | bytes 2359328 | tf_op jit(solution)/shard_map/ppermute | solution.py:64
  158.1 4.4 broadcast_select_fusion.5
  162.5 30.8 %collective-permute-done.4 = bf16[1,2,2,2,416,384]{5,4,3,2,1,0:T(8,128)(2,1)} collective-permute-done((bf16[1,2,2,2,416,384]{5,4,3,2,1,0:T(8,128)(2,1)}, bf16[1,2,2,2,416,384]{5,4,3,2,1,0:T(8,128)(2,1)}, u32[]{:S(2)}, u32[]{:S(2)}) %collective-permute-start.4) | collective-permute-done | bytes 2555936 | tf_op jit(solution)/shard_map/ppermute | solution.py:64
  208.7 3.2 copy.171
  211.9 4.2 reshape.797
  218.4 3.2 copy.165
  221.6 3.0 squeeze.31
  225.2 2.9 fusion.20
  228.9 4.8 fusion.153
  233.7 3.5 fusion.64
  243.4 3.0 fusion.144
  249.5 3.3 multiply_convert_fusion.3
  252.8 2.8 fusion.155
  256.1 2.8 copy.179
  258.9 4.7 squeeze.35
  275.0 6.5 %fusion.156 = (f32[6,512]{1,0:T(8,128)}, f32[6,512,512]{1,2,0:T(8,128)}) fusion(bf16[512,6,64]{0,2,1:T(8,128)(2,1)} %bitcast.437, bf16[512,6,64]{0,2,1:T(8,128)(2,1)} %bitcast.435), kind=kOutput, calls=%fused_computation.471 | convolution fusion | flops 206045696 | bytes 7090176 | tf_op jit(solution)/shard_map/sub | solution.py:117
  281.5 3.5 fusion.70
  289.5 3.4 multiply_convert_fusion.2
  293.0 2.8 fusion.158
  298.4 2.7 fusion.140
  308.6 2.8 fusion.159
  311.5 3.1 convolution_convert_fusion.1
  314.6 2.9 convolution_convert_fusion
  319.5 5.2 reshape.819
  330.9 4.5 broadcast_select_fusion.20
  369.1 4.5 fusion.160
  379.2 3.9 copy.200
  383.1 5.2 reshape.815
  388.3 4.2 copy.201
  415.4 3.1 convolution_convert_fusion.4
  418.5 2.8 convolution_convert_fusion.3
  421.5 5.4 reshape.812
  434.3 3.5 collective-permute-done.47
  444.0 3.9 collective-permute-done.48
  449.9 4.7 collective-permute-done.44
  454.6 5.1 collective-permute-start.49
  460.6 6.5 %collective-permute-done.49 = bf16[1,1,1,1,96,768]{5,4,3,2,1,0:T(8,128)(2,1)S(1)} collective-permute-done((bf16[1,1,1,1,96,768]{5,4,3,2,1,0:T(8,128)(2,1)S(1)}, bf16[1,1,1,1,96,768]{5,4,3,2,1,0:T(8,128)(2,1)S(1)}, u32[]{:S(2)}, u32[]{:S(2)}) %collective-permute-start.49) | collective-permute-done | bytes 147488 | tf_op jit(solution)/shard_map/ppermute | solution.py:64
  467.2 6.9 %collective-permute-done.45 = bf16[1,1,1,1,192,384]{5,4,3,2,1,0:T(8,128)(2,1)} collective-permute-done((bf16[1,1,1,1,192,384]{5,4,3,2,1,0:T(8,128)(2,1)}, bf16[1,1,1,1,192,384]{5,4,3,2,1,0:T(8,128)(2,1)}, u32[]{:S(2)}, u32[]{:S(2)}) %collective-permute-start.45) | collective-permute-done | bytes 147488 | tf_op jit(solution)/shard_map/ppermute | solution.py:64
  494.2 3.7 convolution_convert_fusion.5
  498.0 3.9 copy.190
  501.8 5.0 reshape.809
  506.9 4.2 copy.191
  511.1 2.8 fusion.162
  524.9 6.6 %collective-permute-done.40 = bf16[1,2,1,1,192,384]{5,4,3,2,1,0:T(8,128)(2,1)S(1)} collective-permute-done((bf16[1,2,1,1,192,384]{5,4,3,2,1,0:T(8,128)(2,1)S(1)}, bf16[1,2,1,1,192,384]{5,4,3,2,1,0:T(8,128)(2,1)S(1)}, u32[]{:S(2)}, u32[]{:S(2)}) %collective-permute-start.40) | collective-permute-done | bytes 294944 | tf_op jit(solution)/shard_map/ppermute | solution.py:64
  534.5 6.2 collective-permute-done.41
  541.0 18.5 %collective-permute-done.34 = bf16[1,2,2,1,96,768]{5,4,3,2,1,0:T(8,128)(2,1)S(1)} collective-permute-done((bf16[1,2,2,1,96,768]{5,4,3,2,1,0:T(8,128)(2,1)S(1)}, bf16[1,2,2,1,96,768]{5,4,3,2,1,0:T(8,128)(2,1)S(1)}, u32[]{:S(2)}, u32[]{:S(2)}) %collective-permute-start.34) | collective-permute-done | bytes 589856 | tf_op jit(solution)/shard_map/ppermute | solution.py:64
  564.9 6.1 collective-permute-done.35
  571.2 4.9 collective-permute-done.26
  579.8 5.8 collective-permute-done.27
  590.8 4.3 collective-permute-done.28
  597.2 9.0 %collective-permute-done.50 = bf16[576,384]{1,0:T(8,128)(2,1)S(1)} collective-permute-done((bf16[576,384]{1,0:T(8,128)(2,1)S(1)}, bf16[576,384]{1,0:T(8,128)(2,1)S(1)}, u32[]{:S(2)}, u32[]{:S(2)}) %collective-permute-start.50) | collective-permute-done | bytes 442400 | tf_op jit(solution)/shard_map/ppermute | solution.py:64
  (691 shorter events, 233.3 us)
Async XLA Ops:
  1.7 17.4 %collective-permute-start.11 = (bf16[1,1,1,1,192,768]{5,4,3,2,1,0:T(8,128)(2,1)S(1)}, bf16[1,1,1,1,192,768]{5,4,3,2,1,0:T(8,128)(2,1)S(1)}, u32[]{:S(2)}, u32[]{:S(2)}) collective-permute-start(bf16[1,1,1,1,192,768]{5,4,3,2,1,0:T(8,128)(2,1)S(1)} %convert_bitcast_fusion), channel_id=1, source_target_pairs={{0,16},{1,17},{2,18},{3,19},{4,20},{5,21},{6,22},{7,23},{8,24},{9,... | collective-permute-start | bytes 884744 | tf_op jit(solution)/shard_map/ppermute | solution.py:64
  8.9 10.2 %copy-start.47 = (f32[1,192,768]{2,1,0:T(8,128)S(1)}, f32[1,192,768]{2,1,0:T(8,128)}, u32[]{:S(2)}) copy-start(f32[1,192,768]{2,1,0:T(8,128)} %param.16) | copy-start | bytes 1769476
  9.4 10.7 %collective-permute-start = (bf16[400,384]{1,0:T(8,128)(2,1)S(1)}, bf16[400,384]{1,0:T(8,128)(2,1)S(1)}, u32[]{:S(2)}, u32[]{:S(2)}) collective-permute-start(bf16[400,384]{1,0:T(8,128)(2,1)S(1)} %pad_maximum_fusion.18), channel_id=1, source_target_pairs={{0,1},{1,0},{2,3},{3,2},{4,5},{5,4},{6,7},{7,6},{8,9},{9,8},{10,11... | collective-permute-start | bytes 921608 | tf_op jit(solution)/shard_map/ppermute | solution.py:64
  19.3 32.4 %collective-permute-start.12 = (bf16[1,2,1,1,192,768]{5,4,3,2,1,0:T(8,128)(2,1)S(1)}, bf16[1,2,1,1,192,768]{5,4,3,2,1,0:T(8,128)(2,1)S(1)}, u32[]{:S(2)}, u32[]{:S(2)}) collective-permute-start(bf16[1,2,1,1,192,768]{5,4,3,2,1,0:T(8,128)(2,1)S(1)} %pad_maximum_fusion.13), channel_id=1, source_target_pairs={{0,8},{1,9},{2,10},{3,11},{4,12},{5,13},{6,14},{7,15},{8,0},{9,1},... | collective-permute-start | bytes 1769480 | tf_op jit(solution)/shard_map/ppermute | solution.py:64
  20.9 19.3 %collective-permute-start.7 = (bf16[1,1,1,1,384,384]{5,4,3,2,1,0:T(8,128)(2,1)S(1)}, bf16[1,1,1,1,384,384]{5,4,3,2,1,0:T(8,128)(2,1)S(1)}, u32[]{:S(2)}, u32[]{:S(2)}) collective-permute-start(bf16[1,1,1,1,384,384]{5,4,3,2,1,0:T(8,128)(2,1)S(1)} %bitcast.453), channel_id=1, source_target_pairs={{0,16},{1,17},{2,18},{3,19},{4,20},{5,21},{6,22},{7,23},{8,24},{9,... | collective-permute-start | bytes 884744 | tf_op jit(solution)/shard_map/ppermute | solution.py:64
  24.3 27.0 %collective-permute-start.1 = (bf16[1,1,1,1,416,384]{5,4,3,2,1,0:T(8,128)(2,1)S(1)}, bf16[1,1,1,1,416,384]{5,4,3,2,1,0:T(8,128)(2,1)S(1)}, u32[]{:S(2)}, u32[]{:S(2)}) collective-permute-start(bf16[1,1,1,1,416,384]{5,4,3,2,1,0:T(8,128)(2,1)S(1)} %maximum_bitcast_fusion.4), channel_id=1, source_target_pairs={{0,16},{1,17},{2,18},{3,19},{4,20},{5,21},{6,22},{7,23},{8,24},{9,... | collective-permute-start | bytes 958472 | tf_op jit(solution)/shard_map/ppermute | solution.py:64
  40.3 20.9 %collective-permute-start.8 = (bf16[1,2,1,1,384,384]{5,4,3,2,1,0:T(8,128)(2,1)S(1)}, bf16[1,2,1,1,384,384]{5,4,3,2,1,0:T(8,128)(2,1)S(1)}, u32[]{:S(2)}, u32[]{:S(2)}) collective-permute-start(bf16[1,2,1,1,384,384]{5,4,3,2,1,0:T(8,128)(2,1)S(1)} %pad_maximum_fusion.12), channel_id=1, source_target_pairs={{0,8},{1,9},{2,10},{3,11},{4,12},{5,13},{6,14},{7,15},{8,0},{9,1},... | collective-permute-start | bytes 1769480 | tf_op jit(solution)/shard_map/ppermute | solution.py:64
  51.6 21.8 %collective-permute-start.2 = (bf16[1,2,1,1,416,384]{5,4,3,2,1,0:T(8,128)(2,1)S(1)}, bf16[1,2,1,1,416,384]{5,4,3,2,1,0:T(8,128)(2,1)S(1)}, u32[]{:S(2)}, u32[]{:S(2)}) collective-permute-start(bf16[1,2,1,1,416,384]{5,4,3,2,1,0:T(8,128)(2,1)S(1)} %pad_maximum_fusion.10), channel_id=1, source_target_pairs={{0,8},{1,9},{2,10},{3,11},{4,12},{5,13},{6,14},{7,15},{8,0},{9,1},... | collective-permute-start | bytes 1916936 | tf_op jit(solution)/shard_map/ppermute | solution.py:64
  52.9 29.2 %collective-permute-start.13 = (bf16[1,2,2,1,192,768]{5,4,3,2,1,0:T(8,128)(2,1)}, bf16[1,2,2,1,192,768]{5,4,3,2,1,0:T(8,128)(2,1)}, u32[]{:S(2)}, u32[]{:S(2)}) collective-permute-start(bf16[1,2,2,1,192,768]{5,4,3,2,1,0:T(8,128)(2,1)} %pad_maximum_fusion.7), channel_id=1, source_target_pairs={{0,4},{1,5},{2,6},{3,7},{4,0},{5,1},{6,2},{7,3},{8,12},{9,13},{10,... | collective-permute-start | bytes 3538952 | tf_op jit(solution)/shard_map/ppermute | solution.py:64
  62.5 28.4 %collective-permute-start.9 = (bf16[1,2,2,1,384,384]{5,4,3,2,1,0:T(8,128)(2,1)}, bf16[1,2,2,1,384,384]{5,4,3,2,1,0:T(8,128)(2,1)}, u32[]{:S(2)}, u32[]{:S(2)}) collective-permute-start(bf16[1,2,2,1,384,384]{5,4,3,2,1,0:T(8,128)(2,1)} %pad_maximum_fusion.6), channel_id=1, source_target_pairs={{0,2},{1,3},{2,0},{3,1},{4,6},{5,7},{6,4},{7,5},{8,10},{9,11},{10,... | collective-permute-start | bytes 3538952 | tf_op jit(solution)/shard_map/ppermute | solution.py:64
  75.6 33.9 %collective-permute-start.3 = (bf16[1,2,2,1,416,384]{5,4,3,2,1,0:T(8,128)(2,1)}, bf16[1,2,2,1,416,384]{5,4,3,2,1,0:T(8,128)(2,1)}, u32[]{:S(2)}, u32[]{:S(2)}) collective-permute-start(bf16[1,2,2,1,416,384]{5,4,3,2,1,0:T(8,128)(2,1)} %pad_maximum_fusion.5), channel_id=1, source_target_pairs={{0,4},{1,5},{2,6},{3,7},{4,0},{5,1},{6,2},{7,3},{8,12},{9,13},{10,... | collective-permute-start | bytes 3833864 | tf_op jit(solution)/shard_map/ppermute | solution.py:64
  85.7 55.8 %collective-permute-start.14 = (bf16[1,2,2,2,192,768]{5,4,3,2,1,0:T(8,128)(2,1)}, bf16[1,2,2,2,192,768]{5,4,3,2,1,0:T(8,128)(2,1)}, u32[]{:S(2)}, u32[]{:S(2)}) collective-permute-start(bf16[1,2,2,2,192,768]{5,4,3,2,1,0:T(8,128)(2,1)} %pad_maximum_fusion.4), channel_id=1, source_target_pairs={{0,2},{1,3},{2,0},{3,1},{4,6},{5,7},{6,4},{7,5},{8,10},{9,11},{10,... | collective-permute-start | bytes 7077896 | tf_op jit(solution)/shard_map/ppermute | solution.py:64
  92.5 17.0 %copy-start.41 = (bf16[1,2,1,1,416,384]{5,4,3,2,1,0:T(8,128)(2,1)S(1)}, bf16[1,2,1,1,416,384]{5,4,3,2,1,0:T(8,128)(2,1)}, u32[]{:S(2)}) copy-start(bf16[1,2,1,1,416,384]{5,4,3,2,1,0:T(8,128)(2,1)} %copy-done.40) | copy-start | bytes 1916932
  94.6 63.4 %collective-permute-start.10 = (bf16[2,2,2,1,384,384]{5,4,3,2,1,0:T(8,128)(2,1)}, bf16[2,2,2,1,384,384]{5,4,3,2,1,0:T(8,128)(2,1)}, u32[]{:S(2)}, u32[]{:S(2)}) collective-permute-start(bf16[2,2,2,1,384,384]{5,4,3,2,1,0:T(8,128)(2,1)} %pad_maximum_fusion.3), channel_id=1, source_target_pairs={{0,4},{1,5},{2,6},{3,7},{4,0},{5,1},{6,2},{7,3},{8,12},{9,13},{10,... | collective-permute-start | bytes 7077896 | tf_op jit(solution)/shard_map/ppermute | solution.py:64
  112.9 80.3 %collective-permute-start.4 = (bf16[1,2,2,2,416,384]{5,4,3,2,1,0:T(8,128)(2,1)}, bf16[1,2,2,2,416,384]{5,4,3,2,1,0:T(8,128)(2,1)}, u32[]{:S(2)}, u32[]{:S(2)}) collective-permute-start(bf16[1,2,2,2,416,384]{5,4,3,2,1,0:T(8,128)(2,1)} %pad_maximum_fusion.2), channel_id=1, source_target_pairs={{0,2},{1,3},{2,0},{3,1},{4,6},{5,7},{6,4},{7,5},{8,10},{9,11},{10,... | collective-permute-start | bytes 7667720 | tf_op jit(solution)/shard_map/ppermute | solution.py:64
  114.4 43.7 %copy-start.10 = (bf16[1,2,2,1,384,384]{5,4,3,2,1,0:T(8,128)(2,1)S(1)}, bf16[1,2,2,1,384,384]{5,4,3,2,1,0:T(8,128)(2,1)}, u32[]{:S(2)}) copy-start(bf16[1,2,2,1,384,384]{5,4,3,2,1,0:T(8,128)(2,1)} %copy-done.9) | copy-start | bytes 3538948
  114.4 43.7 %copy-start.12 = (bf16[1,2,2,1,384,384]{5,4,3,2,1,0:T(8,128)(2,1)S(1)}, bf16[1,2,2,1,384,384]{5,4,3,2,1,0:T(8,128)(2,1)}, u32[]{:S(2)}) copy-start(bf16[1,2,2,1,384,384]{5,4,3,2,1,0:T(8,128)(2,1)} %copy-done.11) | copy-start | bytes 3538948
  218.4 19.0 %collective-permute-start.5 = (bf16[2,4,48,768]{3,2,1,0:T(8,128)(2,1)S(1)}, bf16[2,4,48,768]{3,2,1,0:T(8,128)(2,1)S(1)}, u32[]{:S(2)}, u32[]{:S(2)}) collective-permute-start(bf16[2,4,48,768]{3,2,1,0:T(8,128)(2,1)S(1)} %fusion.86), channel_id=1, source_target_pairs={{0,1},{1,0},{2,3},{3,2},{4,5},{5,4},{6,7},{7,6},{8,9},{9,8},{10,11... | collective-permute-start | bytes 1769480 | tf_op jit(solution)/shard_map/ppermute | solution.py:64
  239.2 9.5 %collective-permute-start.6 = (bf16[512,768]{1,0:T(8,128)(2,1)S(1)}, bf16[512,768]{1,0:T(8,128)(2,1)S(1)}, u32[]{:S(2)}, u32[]{:S(2)}) collective-permute-start(bf16[512,768]{1,0:T(8,128)(2,1)S(1)} %get-tuple-element.180), channel_id=1, source_target_pairs={{0,1},{1,0},{2,3},{3,2},{4,5},{5,4},{6,7},{7,6},{8,9},{9,8},{10,11... | collective-permute-start | bytes 2359304 | tf_op jit(solution)/shard_map/ppermute | solution.py:64
  248.1 15.6 %copy-start.127 = (f32[768]{0:T(1024)}, f32[768]{0:T(1024)S(1)}, u32[]{:S(2)}) copy-start(f32[768]{0:T(1024)S(1)} %get-tuple-element.37) | copy-start | bytes 9220
  248.1 18.2 %copy-start.112 = (f32[768]{0:T(1024)}, f32[768]{0:T(1024)S(1)}, u32[]{:S(2)}) copy-start(f32[768]{0:T(1024)S(1)} %get-tuple-element.34) | copy-start | bytes 9220
  249.1 14.5 %copy-start.102 = (f32[512]{0:T(512)}, f32[512]{0:T(512)S(1)}, u32[]{:S(2)}) copy-start(f32[512]{0:T(512)S(1)} %broadcast_multiply_fusion.12) | copy-start | bytes 6148
  249.5 14.2 %copy-start.117 = (f32[512]{0:T(512)}, f32[512]{0:T(512)S(1)}, u32[]{:S(2)}) copy-start(f32[512]{0:T(512)S(1)} %add_rsqrt_fusion.3) | copy-start | bytes 6148
  255.6 8.0 %collective-permute-start.15 = (bf16[512,768]{1,0:T(8,128)(2,1)}, bf16[512,768]{1,0:T(8,128)(2,1)}, u32[]{:S(2)}, u32[]{:S(2)}) collective-permute-start(bf16[512,768]{1,0:T(8,128)(2,1)} %get-tuple-element.184), channel_id=1, source_target_pairs={{0,1},{1,0},{2,3},{3,2},{4,5},{5,4},{6,7},{7,6},{8,9},{9,8},{10,11... | collective-permute-start | bytes 2359304 | tf_op jit(solution)/shard_map/ppermute | solution.py:64
  285.7 2.4 collective-permute-start.16
  295.7 2.6 collective-permute-start.17
  305.1 9.5 %copy-start.36 = (f32[512,768]{1,0:T(8,128)}, f32[512,768]{1,0:T(8,128)S(1)}, u32[]{:S(2)}) copy-start(f32[512,768]{1,0:T(8,128)S(1)} %get-tuple-element.64) | copy-start | bytes 4718596
  326.9 10.0 %copy-start.21 = (bf16[8,4,2,48,384]{4,3,1,0,2:T(8,128)(2,1)}, bf16[8,4,2,48,384]{4,3,1,0,2:T(8,128)(2,1)S(1)}, u32[]{:S(2)}) copy-start(bf16[8,4,2,48,384]{4,3,1,0,2:T(8,128)(2,1)S(1)} %copy.206) | copy-start | bytes 7077892
  327.5 12.1 %copy-start.19 = (bf16[8,2,2,48,768]{4,3,1,0,2:T(8,128)(2,1)}, bf16[8,2,2,48,768]{4,3,1,0,2:T(8,128)(2,1)S(1)}, u32[]{:S(2)}) copy-start(bf16[8,2,2,48,768]{4,3,1,0,2:T(8,128)(2,1)S(1)} %copy.207) | copy-start | bytes 7077892
  328.8 13.0 %collective-permute-start.19 = (bf16[512,768]{1,0:T(8,128)(2,1)S(1)}, bf16[512,768]{1,0:T(8,128)(2,1)S(1)}, u32[]{:S(2)}, u32[]{:S(2)}) collective-permute-start(bf16[512,768]{1,0:T(8,128)(2,1)S(1)} %copy-done.150), channel_id=1, source_target_pairs={{0,1},{1,0},{2,3},{3,2},{4,5},{5,4},{6,7},{7,6},{8,9},{9,8},{10,11... | collective-permute-start | bytes 2359304 | tf_op jit(solution)/shard_map/ppermute | solution.py:64
  335.3 41.2 %collective-permute-start.18 = (bf16[512,768]{1,0:T(8,128)(2,1)}, bf16[512,768]{1,0:T(8,128)(2,1)}, u32[]{:S(2)}, u32[]{:S(2)}) collective-permute-start(bf16[512,768]{1,0:T(8,128)(2,1)} %get-tuple-element.73), channel_id=1, source_target_pairs={{0,2},{1,3},{2,0},{3,1},{4,6},{5,7},{6,4},{7,5},{8,10},{9,11},{10,... | collective-permute-start | bytes 2359304 | tf_op jit(solution)/shard_map/ppermute | solution.py:64
  338.1 58.6 %collective-permute-start.42 = (bf16[2,2,2,1,192,384]{5,4,3,2,1,0:T(8,128)(2,1)}, bf16[2,2,2,1,192,384]{5,4,3,2,1,0:T(8,128)(2,1)}, u32[]{:S(2)}, u32[]{:S(2)}) collective-permute-start(bf16[2,2,2,1,192,384]{5,4,3,2,1,0:T(8,128)(2,1)} %constant_dynamic-slice_fusion.7), channel_id=1, source_target_pairs={{0,4},{1,5},{2,6},{3,7},{4,0},{5,1},{6,2},{7,3},{8,12},{9,13},{10,... | collective-permute-start | bytes 3538952 | tf_op jit(solution)/shard_map/ppermute | solution.py:64
  340.7 62.2 %collective-permute-start.46 = (bf16[1,2,2,2,96,768]{5,4,3,2,1,0:T(8,128)(2,1)}, bf16[1,2,2,2,96,768]{5,4,3,2,1,0:T(8,128)(2,1)}, u32[]{:S(2)}, u32[]{:S(2)}) collective-permute-start(bf16[1,2,2,2,96,768]{5,4,3,2,1,0:T(8,128)(2,1)} %constant_dynamic-slice_fusion.3), channel_id=1, source_target_pairs={{0,2},{1,3},{2,0},{3,1},{4,6},{5,7},{6,4},{7,5},{8,10},{9,11},{10,... | collective-permute-start | bytes 3538952 | tf_op jit(solution)/shard_map/ppermute | solution.py:64
  353.0 12.6 %copy-start.138 = (f32[768]{0:T(1024)S(1)}, f32[768]{0:T(1024)}, u32[]{:S(2)}) copy-start(f32[768]{0:T(1024)} %get-tuple-element.29) | copy-start | bytes 9220
  354.9 37.6 %collective-permute-start.37 = (bf16[4,48,768]{2,1,0:T(8,128)(2,1)}, bf16[4,48,768]{2,1,0:T(8,128)(2,1)}, u32[]{:S(2)}, u32[]{:S(2)}) collective-permute-start(bf16[4,48,768]{2,1,0:T(8,128)(2,1)} %select_bitcast_fusion), channel_id=1, source_target_pairs={{0,1},{1,0},{2,3},{3,2},{4,5},{5,4},{6,7},{7,6},{8,9},{9,8},{10,11... | collective-permute-start | bytes 884744 | tf_op jit(solution)/shard_map/ppermute | solution.py:64
  373.5 32.4 %collective-permute-start.20 = (bf16[512,768]{1,0:T(8,128)(2,1)}, bf16[512,768]{1,0:T(8,128)(2,1)}, u32[]{:S(2)}, u32[]{:S(2)}) collective-permute-start(bf16[512,768]{1,0:T(8,128)(2,1)} %get-tuple-element.198), channel_id=1, source_target_pairs={{0,1},{1,0},{2,3},{3,2},{4,5},{5,4},{6,7},{7,6},{8,9},{9,8},{10,11... | collective-permute-start | bytes 2359304 | tf_op jit(solution)/shard_map/ppermute | solution.py:64
  396.1 79.8 %collective-permute-start.38 = (bf16[2,2,2,1,192,384]{5,4,3,2,1,0:T(8,128)(2,1)}, bf16[2,2,2,1,192,384]{5,4,3,2,1,0:T(8,128)(2,1)}, u32[]{:S(2)}, u32[]{:S(2)}) collective-permute-start(bf16[2,2,2,1,192,384]{5,4,3,2,1,0:T(8,128)(2,1)} %constant_dynamic-slice_fusion.11), channel_id=1, source_target_pairs={{0,4},{1,5},{2,6},{3,7},{4,0},{5,1},{6,2},{7,3},{8,12},{9,13},{10,... | collective-permute-start | bytes 3538952 | tf_op jit(solution)/shard_map/ppermute | solution.py:64
  401.3 39.3 %collective-permute-start.43 = (bf16[1,2,2,1,192,384]{5,4,3,2,1,0:T(8,128)(2,1)}, bf16[1,2,2,1,192,384]{5,4,3,2,1,0:T(8,128)(2,1)}, u32[]{:S(2)}, u32[]{:S(2)}) collective-permute-start(bf16[1,2,2,1,192,384]{5,4,3,2,1,0:T(8,128)(2,1)} %constant_dynamic-slice_fusion.6), channel_id=1, source_target_pairs={{0,2},{1,3},{2,0},{3,1},{4,6},{5,7},{6,4},{7,5},{8,10},{9,11},{10,... | collective-permute-start | bytes 1769480 | tf_op jit(solution)/shard_map/ppermute | solution.py:64
  405.4 32.5 %collective-permute-start.47 = (bf16[1,2,2,1,96,768]{5,4,3,2,1,0:T(8,128)(2,1)}, bf16[1,2,2,1,96,768]{5,4,3,2,1,0:T(8,128)(2,1)}, u32[]{:S(2)}, u32[]{:S(2)}) collective-permute-start(bf16[1,2,2,1,96,768]{5,4,3,2,1,0:T(8,128)(2,1)} %constant_dynamic-slice_fusion.2), channel_id=1, source_target_pairs={{0,4},{1,5},{2,6},{3,7},{4,0},{5,1},{6,2},{7,3},{8,12},{9,13},{10,... | collective-permute-start | bytes 1769480 | tf_op jit(solution)/shard_map/ppermute | solution.py:64
  429.5 49.9 %collective-permute-start.21 = (bf16[512,768]{1,0:T(8,128)(2,1)}, bf16[512,768]{1,0:T(8,128)(2,1)}, u32[]{:S(2)}, u32[]{:S(2)}) collective-permute-start(bf16[512,768]{1,0:T(8,128)(2,1)} %get-tuple-element.200), channel_id=1, source_target_pairs={{0,1},{1,0},{2,3},{3,2},{4,5},{5,4},{6,7},{7,6},{8,9},{9,8},{10,11... | collective-permute-start | bytes 2359304 | tf_op jit(solution)/shard_map/ppermute | solution.py:64
  431.7 85.4 %collective-permute-start.29 = (bf16[2,2,2,1,192,384]{5,4,3,2,1,0:T(8,128)(2,1)}, bf16[2,2,2,1,192,384]{5,4,3,2,1,0:T(8,128)(2,1)}, u32[]{:S(2)}, u32[]{:S(2)}) collective-permute-start(bf16[2,2,2,1,192,384]{5,4,3,2,1,0:T(8,128)(2,1)} %constant_dynamic-slice_fusion.19), channel_id=1, source_target_pairs={{0,4},{1,5},{2,6},{3,7},{4,0},{5,1},{6,2},{7,3},{8,12},{9,13},{10,... | collective-permute-start | bytes 3538952 | tf_op jit(solution)/shard_map/ppermute | solution.py:64
  437.8 84.7 %collective-permute-start.33 = (bf16[1,2,2,2,96,768]{5,4,3,2,1,0:T(8,128)(2,1)}, bf16[1,2,2,2,96,768]{5,4,3,2,1,0:T(8,128)(2,1)}, u32[]{:S(2)}, u32[]{:S(2)}) collective-permute-start(bf16[1,2,2,2,96,768]{5,4,3,2,1,0:T(8,128)(2,1)} %constant_dynamic-slice_fusion.15), channel_id=1, source_target_pairs={{0,2},{1,3},{2,0},{3,1},{4,6},{5,7},{6,4},{7,5},{8,10},{9,11},{10,... | collective-permute-start | bytes 3538952 | tf_op jit(solution)/shard_map/ppermute | solution.py:64
  440.6 7.3 %collective-permute-start.48 = (bf16[1,2,1,1,96,768]{5,4,3,2,1,0:T(8,128)(2,1)S(1)}, bf16[1,2,1,1,96,768]{5,4,3,2,1,0:T(8,128)(2,1)S(1)}, u32[]{:S(2)}, u32[]{:S(2)}) collective-permute-start(bf16[1,2,1,1,96,768]{5,4,3,2,1,0:T(8,128)(2,1)S(1)} %constant_dynamic-slice_fusion.1), channel_id=1, source_target_pairs={{0,8},{1,9},{2,10},{3,11},{4,12},{5,13},{6,14},{7,15},{8,0},{9,1},... | collective-permute-start | bytes 884744 | tf_op jit(solution)/shard_map/ppermute | solution.py:64
  447.9 6.7 %collective-permute-start.44 = (bf16[1,2,1,1,192,384]{5,4,3,2,1,0:T(8,128)(2,1)S(1)}, bf16[1,2,1,1,192,384]{5,4,3,2,1,0:T(8,128)(2,1)S(1)}, u32[]{:S(2)}, u32[]{:S(2)}) collective-permute-start(bf16[1,2,1,1,192,384]{5,4,3,2,1,0:T(8,128)(2,1)S(1)} %constant_dynamic-slice_fusion.5), channel_id=1, source_target_pairs={{0,8},{1,9},{2,10},{3,11},{4,12},{5,13},{6,14},{7,15},{8,0},{9,1},... | collective-permute-start | bytes 884744 | tf_op jit(solution)/shard_map/ppermute | solution.py:64
  454.6 12.5 %collective-permute-start.49 = (bf16[1,1,1,1,96,768]{5,4,3,2,1,0:T(8,128)(2,1)S(1)}, bf16[1,1,1,1,96,768]{5,4,3,2,1,0:T(8,128)(2,1)S(1)}, u32[]{:S(2)}, u32[]{:S(2)}) collective-permute-start(bf16[1,1,1,1,96,768]{5,4,3,2,1,0:T(8,128)(2,1)S(1)} %constant_dynamic-slice_fusion), channel_id=1, source_target_pairs={{0,16},{1,17},{2,18},{3,19},{4,20},{5,21},{6,22},{7,23},{8,24},{9,... | collective-permute-start | bytes 442376 | tf_op jit(solution)/shard_map/ppermute | solution.py:64
  467.1 7.0 %collective-permute-start.45 = (bf16[1,1,1,1,192,384]{5,4,3,2,1,0:T(8,128)(2,1)}, bf16[1,1,1,1,192,384]{5,4,3,2,1,0:T(8,128)(2,1)}, u32[]{:S(2)}, u32[]{:S(2)}) collective-permute-start(bf16[1,1,1,1,192,384]{5,4,3,2,1,0:T(8,128)(2,1)} %constant_dynamic-slice_fusion.4), channel_id=1, source_target_pairs={{0,16},{1,17},{2,18},{3,19},{4,20},{5,21},{6,22},{7,23},{8,24},{9,... | collective-permute-start | bytes 442376 | tf_op jit(solution)/shard_map/ppermute | solution.py:64
  478.9 42.3 %collective-permute-start.39 = (bf16[1,2,2,1,192,384]{5,4,3,2,1,0:T(8,128)(2,1)}, bf16[1,2,2,1,192,384]{5,4,3,2,1,0:T(8,128)(2,1)}, u32[]{:S(2)}, u32[]{:S(2)}) collective-permute-start(bf16[1,2,2,1,192,384]{5,4,3,2,1,0:T(8,128)(2,1)} %constant_dynamic-slice_fusion.10), channel_id=1, source_target_pairs={{0,2},{1,3},{2,0},{3,1},{4,6},{5,7},{6,4},{7,5},{8,10},{9,11},{10,... | collective-permute-start | bytes 1769480 | tf_op jit(solution)/shard_map/ppermute | solution.py:64
  491.8 22.8 %collective-permute-start.24 = (bf16[4,48,768]{2,1,0:T(8,128)(2,1)}, bf16[4,48,768]{2,1,0:T(8,128)(2,1)}, u32[]{:S(2)}, u32[]{:S(2)}) collective-permute-start(bf16[4,48,768]{2,1,0:T(8,128)(2,1)} %select_bitcast_fusion.1), channel_id=1, source_target_pairs={{0,1},{1,0},{2,3},{3,2},{4,5},{5,4},{6,7},{7,6},{8,9},{9,8},{10,11... | collective-permute-start | bytes 884744 | tf_op jit(solution)/shard_map/ppermute | solution.py:64
  513.9 18.4 %collective-permute-start.22 = (bf16[512,768]{1,0:T(8,128)(2,1)S(1)}, bf16[512,768]{1,0:T(8,128)(2,1)S(1)}, u32[]{:S(2)}, u32[]{:S(2)}) collective-permute-start(bf16[512,768]{1,0:T(8,128)(2,1)S(1)} %get-tuple-element.204), channel_id=1, source_target_pairs={{0,1},{1,0},{2,3},{3,2},{4,5},{5,4},{6,7},{7,6},{8,9},{9,8},{10,11... | collective-permute-start | bytes 2359304 | tf_op jit(solution)/shard_map/ppermute | solution.py:64
  516.5 43.3 %collective-permute-start.25 = (bf16[2,2,2,1,208,384]{5,4,3,2,1,0:T(8,128)(2,1)S(1)}, bf16[2,2,2,1,208,384]{5,4,3,2,1,0:T(8,128)(2,1)S(1)}, u32[]{:S(2)}, u32[]{:S(2)}) collective-permute-start(bf16[2,2,2,1,208,384]{5,4,3,2,1,0:T(8,128)(2,1)S(1)} %fusion.58), channel_id=1, source_target_pairs={{0,4},{1,5},{2,6},{3,7},{4,0},{5,1},{6,2},{7,3},{8,12},{9,13},{10,... | collective-permute-start | bytes 3833864 | tf_op jit(solution)/shard_map/ppermute | solution.py:64
  519.6 21.1 %collective-permute-start.30 = (bf16[1,2,2,1,192,384]{5,4,3,2,1,0:T(8,128)(2,1)S(1)}, bf16[1,2,2,1,192,384]{5,4,3,2,1,0:T(8,128)(2,1)S(1)}, u32[]{:S(2)}, u32[]{:S(2)}) collective-permute-start(bf16[1,2,2,1,192,384]{5,4,3,2,1,0:T(8,128)(2,1)S(1)} %constant_dynamic-slice_fusion.18), channel_id=1, source_target_pairs={{0,2},{1,3},{2,0},{3,1},{4,6},{5,7},{6,4},{7,5},{8,10},{9,11},{10,... | collective-permute-start | bytes 1769480 | tf_op jit(solution)/shard_map/ppermute | solution.py:64
  522.4 9.0 %collective-permute-start.40 = (bf16[1,2,1,1,192,384]{5,4,3,2,1,0:T(8,128)(2,1)S(1)}, bf16[1,2,1,1,192,384]{5,4,3,2,1,0:T(8,128)(2,1)S(1)}, u32[]{:S(2)}, u32[]{:S(2)}) collective-permute-start(bf16[1,2,1,1,192,384]{5,4,3,2,1,0:T(8,128)(2,1)S(1)} %constant_dynamic-slice_fusion.9), channel_id=1, source_target_pairs={{0,8},{1,9},{2,10},{3,11},{4,12},{5,13},{6,14},{7,15},{8,0},{9,1},... | collective-permute-start | bytes 884744 | tf_op jit(solution)/shard_map/ppermute | solution.py:64
  524.2 35.3 %collective-permute-start.34 = (bf16[1,2,2,1,96,768]{5,4,3,2,1,0:T(8,128)(2,1)S(1)}, bf16[1,2,2,1,96,768]{5,4,3,2,1,0:T(8,128)(2,1)S(1)}, u32[]{:S(2)}, u32[]{:S(2)}) collective-permute-start(bf16[1,2,2,1,96,768]{5,4,3,2,1,0:T(8,128)(2,1)S(1)} %constant_dynamic-slice_fusion.14), channel_id=1, source_target_pairs={{0,4},{1,5},{2,6},{3,7},{4,0},{5,1},{6,2},{7,3},{8,12},{9,13},{10,... | collective-permute-start | bytes 1769480 | tf_op jit(solution)/shard_map/ppermute | solution.py:64
  531.6 9.1 %collective-permute-start.41 = (bf16[1,1,1,1,192,384]{5,4,3,2,1,0:T(8,128)(2,1)S(1)}, bf16[1,1,1,1,192,384]{5,4,3,2,1,0:T(8,128)(2,1)S(1)}, u32[]{:S(2)}, u32[]{:S(2)}) collective-permute-start(bf16[1,1,1,1,192,384]{5,4,3,2,1,0:T(8,128)(2,1)S(1)} %constant_dynamic-slice_fusion.8), channel_id=1, source_target_pairs={{0,16},{1,17},{2,18},{3,19},{4,20},{5,21},{6,22},{7,23},{8,24},{9,... | collective-permute-start | bytes 442376 | tf_op jit(solution)/shard_map/ppermute | solution.py:64
  533.7 54.5 %collective-permute-start.23 = (bf16[512,768]{1,0:T(8,128)(2,1)}, bf16[512,768]{1,0:T(8,128)(2,1)}, u32[]{:S(2)}, u32[]{:S(2)}) collective-permute-start(bf16[512,768]{1,0:T(8,128)(2,1)} %get-tuple-element.67), channel_id=1, source_target_pairs={{0,2},{1,3},{2,0},{3,1},{4,6},{5,7},{6,4},{7,5},{8,10},{9,11},{10,... | collective-permute-start | bytes 2359304 | tf_op jit(solution)/shard_map/ppermute | solution.py:64
  540.9 20.8 %collective-permute-start.31 = (bf16[1,2,1,1,192,384]{5,4,3,2,1,0:T(8,128)(2,1)S(1)}, bf16[1,2,1,1,192,384]{5,4,3,2,1,0:T(8,128)(2,1)S(1)}, u32[]{:S(2)}, u32[]{:S(2)}) collective-permute-start(bf16[1,2,1,1,192,384]{5,4,3,2,1,0:T(8,128)(2,1)S(1)} %constant_dynamic-slice_fusion.17), channel_id=1, source_target_pairs={{0,8},{1,9},{2,10},{3,11},{4,12},{5,13},{6,14},{7,15},{8,0},{9,1},... | collective-permute-start | bytes 884744 | tf_op jit(solution)/shard_map/ppermute | solution.py:64
  559.7 11.3 %collective-permute-start.35 = (bf16[1,2,1,1,96,768]{5,4,3,2,1,0:T(8,128)(2,1)S(1)}, bf16[1,2,1,1,96,768]{5,4,3,2,1,0:T(8,128)(2,1)S(1)}, u32[]{:S(2)}, u32[]{:S(2)}) collective-permute-start(bf16[1,2,1,1,96,768]{5,4,3,2,1,0:T(8,128)(2,1)S(1)} %constant_dynamic-slice_fusion.13), channel_id=1, source_target_pairs={{0,8},{1,9},{2,10},{3,11},{4,12},{5,13},{6,14},{7,15},{8,0},{9,1},... | collective-permute-start | bytes 884744 | tf_op jit(solution)/shard_map/ppermute | solution.py:64
  560.2 15.9 %collective-permute-start.26 = (bf16[1,2,2,1,208,384]{5,4,3,2,1,0:T(8,128)(2,1)S(1)}, bf16[1,2,2,1,208,384]{5,4,3,2,1,0:T(8,128)(2,1)S(1)}, u32[]{:S(2)}, u32[]{:S(2)}) collective-permute-start(bf16[1,2,2,1,208,384]{5,4,3,2,1,0:T(8,128)(2,1)S(1)} %constant_dynamic-slice_fusion.22), channel_id=1, source_target_pairs={{0,2},{1,3},{2,0},{3,1},{4,6},{5,7},{6,4},{7,5},{8,10},{9,11},{10,... | collective-permute-start | bytes 1916936 | tf_op jit(solution)/shard_map/ppermute | solution.py:64
  562.5 16.4 %collective-permute-start.32 = (bf16[1,1,1,1,192,384]{5,4,3,2,1,0:T(8,128)(2,1)}, bf16[1,1,1,1,192,384]{5,4,3,2,1,0:T(8,128)(2,1)}, u32[]{:S(2)}, u32[]{:S(2)}) collective-permute-start(bf16[1,1,1,1,192,384]{5,4,3,2,1,0:T(8,128)(2,1)} %constant_dynamic-slice_fusion.16), channel_id=1, source_target_pairs={{0,16},{1,17},{2,18},{3,19},{4,20},{5,21},{6,22},{7,23},{8,24},{9,... | collective-permute-start | bytes 442376 | tf_op jit(solution)/shard_map/ppermute | solution.py:64
  571.1 7.7 %collective-permute-start.36 = (bf16[1,1,1,1,96,768]{5,4,3,2,1,0:T(8,128)(2,1)S(1)}, bf16[1,1,1,1,96,768]{5,4,3,2,1,0:T(8,128)(2,1)S(1)}, u32[]{:S(2)}, u32[]{:S(2)}) collective-permute-start(bf16[1,1,1,1,96,768]{5,4,3,2,1,0:T(8,128)(2,1)S(1)} %constant_dynamic-slice_fusion.12), channel_id=1, source_target_pairs={{0,16},{1,17},{2,18},{3,19},{4,20},{5,21},{6,22},{7,23},{8,24},{9,... | collective-permute-start | bytes 442376 | tf_op jit(solution)/shard_map/ppermute | solution.py:64
  577.0 8.7 %collective-permute-start.27 = (bf16[1,2,1,1,208,384]{5,4,3,2,1,0:T(8,128)(2,1)}, bf16[1,2,1,1,208,384]{5,4,3,2,1,0:T(8,128)(2,1)}, u32[]{:S(2)}, u32[]{:S(2)}) collective-permute-start(bf16[1,2,1,1,208,384]{5,4,3,2,1,0:T(8,128)(2,1)} %constant_dynamic-slice_fusion.21), channel_id=1, source_target_pairs={{0,8},{1,9},{2,10},{3,11},{4,12},{5,13},{6,14},{7,15},{8,0},{9,1},... | collective-permute-start | bytes 958472 | tf_op jit(solution)/shard_map/ppermute | solution.py:64
  586.8 8.3 %collective-permute-start.28 = (bf16[1,1,1,1,208,384]{5,4,3,2,1,0:T(8,128)(2,1)S(1)}, bf16[1,1,1,1,208,384]{5,4,3,2,1,0:T(8,128)(2,1)S(1)}, u32[]{:S(2)}, u32[]{:S(2)}) collective-permute-start(bf16[1,1,1,1,208,384]{5,4,3,2,1,0:T(8,128)(2,1)S(1)} %constant_dynamic-slice_fusion.20), channel_id=1, source_target_pairs={{0,16},{1,17},{2,18},{3,19},{4,20},{5,21},{6,22},{7,23},{8,24},{9,... | collective-permute-start | bytes 479240 | tf_op jit(solution)/shard_map/ppermute | solution.py:64
  595.3 11.0 %collective-permute-start.50 = (bf16[576,384]{1,0:T(8,128)(2,1)S(1)}, bf16[576,384]{1,0:T(8,128)(2,1)S(1)}, u32[]{:S(2)}, u32[]{:S(2)}) collective-permute-start(bf16[576,384]{1,0:T(8,128)(2,1)S(1)} %broadcast_select_fusion.32), channel_id=1, source_target_pairs={{0,2},{1,3},{2,0},{3,1},{4,6},{5,7},{6,4},{7,5},{8,10},{9,11},{10,... | collective-permute-start | bytes 1327112 | tf_op jit(solution)/shard_map/ppermute | solution.py:64
  607.2 2.9 collective-permute-start.51
  (149 other events, 434.2 us)

commit v2 on v1

v2 whole, which is shorter than its diff:
```python
import jax
import jax.numpy as jnp
from jax import lax
from jax.experimental import pallas as pl
from jax.experimental.pallas import tpu as pltpu
from jax.sharding import Mesh
from jax.sharding import PartitionSpec as P

D = 768
HEADS = 12
HEAD_DIM = 64
FF = 3072
SEQ = 512
VEC = 4608
HALF = D // 2
WIDTH = FF // 2
BLOCK = 128
STEP = 256
PAIR = 2 * HEAD_DIM

NORM_EPSILON = 1e-05
BETA_ONE = 0.9
BETA_TWO = 0.98
BIAS_ONE = 1.0 - 0.9**10
BIAS_TWO = 1.0 - 0.98**10
WEIGHT_DECAY = 0.01
ADAM_EPSILON = 1e-06
ROOT_HALF = 0.7071067811865476
ROOT_TWO_PI = 2.5066282746310002
SCALE = HEAD_DIM**-0.5

AXES = ("dp", "x", "c")
LOW = jnp.bfloat16
WIDE = jnp.float32


def mm(a, b):
    return lax.dot_general(a, b, (((1,), (0,)), ((), ())), preferred_element_type=WIDE)
def mm_cols(a, b):
    return lax.dot_general(a, b, (((1,), (1,)), ((), ())), preferred_element_type=WIDE)
def mm_rows(a, b):
    return lax.dot_general(a, b, (((0,), (0,)), ((), ())), preferred_element_type=WIDE)

def kernel_call(body, outs, ins, scratch=()):
    specs = [pl.BlockSpec(memory_space=pltpu.SMEM)] + [pl.BlockSpec(memory_space=pltpu.VMEM)] * (len(ins) - 1)
    return pl.pallas_call(
        body,
        out_shape=[jax.ShapeDtypeStruct(s, d) for s, d in outs],
        in_specs=specs,
        out_specs=[pl.BlockSpec(memory_space=pltpu.VMEM)] * len(outs),
        scratch_shapes=list(scratch),
        compiler_params=pltpu.CompilerParams(vmem_limit_bytes=48 * 2**20),
        cost_estimate=pl.CostEstimate(flops=1000, bytes_accessed=1000, transcendentals=0),
    )(*ins)

def norm_rows(total, vec, normed_ref, spread_ref, out_ref, rows):
    mean = jnp.mean(total, axis=-1, keepdims=True)
    centered = total - mean
    spread = lax.rsqrt(jnp.mean(centered * centered, axis=-1, keepdims=True) + NORM_EPSILON)
    normed = centered * spread
    normed_ref[rows, :] = normed.astype(LOW)
    spread_ref[rows, :] = spread
    out_ref[rows, :] = (normed * vec[4:5, :] + vec[5:6, :]).astype(LOW)

def joined_norm(before, own, got, bias, vec, normed, spread, out):
    def step(i, carry):
        rows = pl.ds(pl.multiple_of(i * BLOCK, BLOCK), BLOCK)
        total = before[rows, :].astype(WIDE) + own[rows, :].astype(WIDE) + got[rows, :].astype(WIDE) + bias
        norm_rows(total, vec, normed, spread, out, rows)
        return carry
    lax.fori_loop(0, SEQ // BLOCK, step, 0)

def half_row(place, row):
    return jnp.where(place[0] == 0, row[:, :HALF], row[:, HALF:])

NORM_OUTS = [((SEQ, D), LOW), ((SEQ, D), LOW), ((SEQ, 1), WIDE)]

def attend_body(place, hidden, w_qkv, w_out, vec, part, mixing, chances, context):
    bias = jnp.concatenate([half_row(place, vec[0:1, :]), jnp.zeros((1, HALF), WIDE), half_row(place, vec[1:2, :])], axis=1)
    for i in range(3):
        cols = slice(i * HALF, (i + 1) * HALF)
        mixing[:, cols] = (mm(hidden[...], w_qkv[:, cols]) + bias[:, cols]).astype(LOW)
    lane = lax.broadcasted_iota(jnp.int32, (SEQ, PAIR), 1)
    first = lane < HEAD_DIM
    for pair in range(HEADS // 4):
        at = pair * PAIR
        queries = mixing[:, at : at + PAIR] * jnp.asarray(SCALE, LOW)
        keys = mixing[:, HALF + at : HALF + at + PAIR]
        values = mixing[:, 2 * HALF + at : 2 * HALF + at + PAIR]
        sums = []
        for side in range(2):
            mine = first if side == 0 else ~first
            scores = mm_cols(jnp.where(mine, queries, jnp.zeros_like(queries)), keys)
            scores = jnp.exp(scores - jnp.max(scores, axis=-1, keepdims=True))
            low = (scores * (1.0 / jnp.sum(scores, axis=-1, keepdims=True))).astype(LOW)
            chances[2 * pair + side] = low
            sums.append(mm(low, values))
        context[:, at : at + PAIR] = jnp.where(first, sums[0], sums[1]).astype(LOW)
    for i in range(2):
        cols = slice(i * HALF, (i + 1) * HALF)
        part[:, cols] = mm(context[...], w_out[:, cols]).astype(LOW)

ATTEND_OUTS = [((SEQ, D), LOW), ((SEQ, 3 * HALF), LOW), ((HEADS // 2, SEQ, SEQ), LOW), ((SEQ, HALF), LOW)]

def attend_first(place, hidden, w_qkv, w_out, vec):
    return kernel_call(attend_body, ATTEND_OUTS, (place, hidden, w_qkv, w_out, vec))

def attend_next_body(place, before, own, got, feed_vec, last_vec, w_qkv, w_out, vec, hidden, normed, spread, *rest):
    joined_norm(before, own, got, last_vec[3:4, :], feed_vec, normed, spread, hidden)
    attend_body(place, hidden, w_qkv, w_out, vec, *rest)

def attend_next(place, before, own, got, feed_vec, last_vec, w_qkv, w_out, vec):
    return kernel_call(attend_next_body, NORM_OUTS + ATTEND_OUTS, (place, before, own, got, feed_vec, last_vec, w_qkv, w_out, vec))

def feed_body(place, before, own, got, vec, feed_vec, w_up, w_down, hidden, normed, spread, part, active, slope):
    joined_norm(before, own, got, vec[2:3, :], vec, normed, spread, hidden)
    for i in range(WIDTH // STEP):
        cols = slice(i * STEP, (i + 1) * STEP)
        row, col = divmod(i * STEP, D)
        bias = jnp.where(place[0] == 0, feed_vec[row : row + 1, col : col + STEP], feed_vec[row + 2 : row + 3, col : col + STEP])
        for j in range(2):
            rows = slice(j * SEQ // 2, (j + 1) * SEQ // 2)
            value = mm(hidden[rows, :], w_up[:, cols]) + bias
            curve = 0.5 * (1.0 + lax.erf(value * ROOT_HALF))
            active[rows, cols] = (value * curve).astype(LOW)
            slope[rows, cols] = (curve + value * jnp.exp(-0.5 * value * value) * (1.0 / ROOT_TWO_PI)).astype(LOW)
    for i in range(2):
        cols = slice(i * HALF, (i + 1) * HALF)
        part[:, cols] = mm(active[...], w_down[:, cols]).astype(LOW)

FEED_OUTS = NORM_OUTS + [((SEQ, D), LOW), ((SEQ, WIDTH), LOW), ((SEQ, WIDTH), LOW)]
def feed_forward(place, before, own, got, vec, feed_vec, w_up, w_down):
    return kernel_call(feed_body, FEED_OUTS, (place, before, own, got, vec, feed_vec, w_up, w_down))

def norm_backward(grad_rows, normed, spread, vec, summed, branch, sums, bias_row):
    def step(i, carry):
        rows = pl.ds(pl.multiple_of(i * BLOCK, BLOCK), BLOCK)
        grad = grad_rows(rows)
        n = normed[rows, :].astype(WIDE)
        through = grad * vec[4:5, :]
        out = spread[rows, :] * (
            through - jnp.mean(through, axis=-1, keepdims=True)
            - n * jnp.mean(through * n, axis=-1, keepdims=True))
        summed[rows, :] = out
        branch[rows, :] = out.astype(LOW)
        add = (jnp.sum(out, axis=0, keepdims=True), jnp.sum(grad * n, axis=0, keepdims=True), jnp.sum(grad, axis=0, keepdims=True))
        return tuple(a + b for a, b in zip(carry, add))
    zero = jnp.zeros((1, D), WIDE)
    return lax.fori_loop(0, SEQ // BLOCK, step, (zero, zero, zero))

def feed_back_core(place, grad_rows, normed, spread, feed_vec, w_up, w_down, slope, summed, branch, change, part, sums):
    once = jnp.where(place[0] == 0, 1.0, 0.0)
    branch_sum, gain_sum, bias_sum = norm_backward(grad_rows, normed, spread, feed_vec, summed, branch, sums, 0)
    sums[...] = jnp.zeros_like(sums)
    sums[4:5, :] = gain_sum * once
    sums[5:6, :] = bias_sum * once
    sums[6:7, :] = branch_sum * once
    for i in range(WIDTH // STEP):
        cols = slice(i * STEP, (i + 1) * STEP)
        row, col = divmod(i * STEP, D)
        total = jnp.zeros((1, STEP), WIDE)
        for j in range(2):
            rows = slice(j * SEQ // 2, (j + 1) * SEQ // 2)
            value = (mm_cols(branch[rows, :], w_down[cols, :]) * slope[rows, cols].astype(WIDE)).astype(LOW)
            change[rows, cols] = value
            total = total + jnp.sum(value.astype(WIDE), axis=0, keepdims=True)
        sums[row : row + 1, col : col + STEP] = total * once
        sums[row + 2 : row + 3, col : col + STEP] = total * (1.0 - once)
    for i in range(2):
        rows = slice(i * HALF, (i + 1) * HALF)
        part[:, rows] = mm_cols(change[...], w_up[rows, :]).astype(LOW)

BACK_OUTS = [((SEQ, D), WIDE), ((SEQ, D), LOW)]

def feed_last_body(place, before, own, got, last_vec, feed_vec, w_up, w_down, slope, cot, out, summed, branch, change, part, sums, normed, spread):
    joined_norm(before, own, got, last_vec[3:4, :], feed_vec, normed, spread, out)
    feed_back_core(place, lambda rows: cot[rows, :].astype(WIDE), normed, spread, feed_vec, w_up, w_down, slope, summed, branch, change, part, sums)

def feed_last(place, before, own, got, last_vec, feed_vec, w_up, w_down, slope, cot):
    return kernel_call(feed_last_body,
        [((SEQ, D), LOW)] + BACK_OUTS + [((SEQ, WIDTH), LOW), ((SEQ, D), LOW), ((8, D), WIDE)],
        (place, before, own, got, last_vec, feed_vec, w_up, w_down, slope, cot),
        [pltpu.VMEM((SEQ, D), LOW), pltpu.VMEM((SEQ, 1), WIDE)])

def joined_grad(before, own, got, grad):
    def rows_of(rows):
        value = (before[rows, :] + own[rows, :].astype(WIDE) + got[rows, :].astype(WIDE)).astype(LOW)
        grad[rows, :] = value
        return value.astype(WIDE)
    return rows_of

def feed_back_body(place, before, own, got, normed, spread, feed_vec, w_up, w_down, slope, grad, summed, branch, change, part, sums):
    feed_back_core(place, joined_grad(before, own, got, grad), normed, spread, feed_vec, w_up, w_down, slope, summed, branch, change, part, sums)

def feed_back(place, before, own, got, normed, spread, feed_vec, w_up, w_down, slope):
    return kernel_call(feed_back_body,
        [((SEQ, D), LOW)] + BACK_OUTS + [((SEQ, WIDTH), LOW), ((SEQ, D), LOW), ((8, D), WIDE)],
        (place, before, own, got, normed, spread, feed_vec, w_up, w_down, slope))

def attend_back_body(place, before, own, got, normed, spread, vec, w_qkv, w_out, mixing, chances, grad, summed, branch, change, part, sums, context_grad):
    once = jnp.where(place[0] == 0, 1.0, 0.0)
    branch_sum, gain_sum, bias_sum = norm_backward(joined_grad(before, own, got, grad), normed, spread, vec, summed, branch, sums, 2)
    sums[...] = jnp.zeros_like(sums)
    sums[2:3, :] = branch_sum * once
    sums[4:5, :] = gain_sum * once
    sums[5:6, :] = bias_sum * once
    context_grad[...] = mm_cols(branch[...], w_out[...]).astype(LOW)
    first = lax.broadcasted_iota(jnp.int32, (SEQ, PAIR), 1) < HEAD_DIM
    for pair in range(HEADS // 4):
        at = pair * PAIR
        queries = mixing[:, at : at + PAIR]
        keys = mixing[:, HALF + at : HALF + at + PAIR]
        values = mixing[:, 2 * HALF + at : 2 * HALF + at + PAIR]
        outer = context_grad[:, at : at + PAIR]
        parts = []
        for side in range(2):
            mine = first if side == 0 else ~first
            low = chances[2 * pair + side]
            change_c = mm_cols(jnp.where(mine, outer, jnp.zeros_like(outer)), values)
            weight = low.astype(WIDE)
            product = weight * change_c
            scores = (product - weight * jnp.sum(product, axis=-1, keepdims=True)).astype(LOW)
            parts.append((mm(scores, keys), mm_rows(scores, queries), mm_rows(low, outer)))
        for i, scale in ((0, SCALE), (1, SCALE), (2, 1.0)):
            cols = slice(i * HALF + at, i * HALF + at + PAIR)
            value = (jnp.where(first, parts[0][i], parts[1][i]) * scale).astype(LOW)
            change[:, cols] = value
            if i != 1:
                total = jnp.sum(value.astype(WIDE), axis=0, keepdims=True)
                row = i // 2
                sums[row : row + 1, at : at + PAIR] = total * once
                sums[row : row + 1, HALF + at : HALF + at + PAIR] = total * (1.0 - once)
    for i in range(2):
        rows = slice(i * HALF, (i + 1) * HALF)
        part[:, rows] = mm_cols(change[...], w_qkv[rows, :]).astype(LOW)

def attend_back(place, before, own, got, normed, spread, vec, w_qkv, w_out, mixing, chances):
    return kernel_call(attend_back_body,
        [((SEQ, D), LOW)] + BACK_OUTS + [((SEQ, 3 * HALF), LOW), ((SEQ, D), LOW), ((8, D), WIDE)],
        (place, before, own, got, normed, spread, vec, w_qkv, w_out, mixing, chances),
        [pltpu.VMEM((SEQ, HALF), LOW)])


def source_rows(place, bits, rows):
    starts = []
    for relative in range(1 << len(bits)):
        dp_mask = x_mask = 0
        for i, bit in enumerate(bits):
            if (relative >> (len(bits) - 1 - i)) & 1:
                if bit == "x":
                    x_mask = 1
                else:
                    dp_mask |= 1 << bit
        start = ((place[1] ^ dp_mask) * 2 + (place[2] ^ x_mask)) * rows
        starts.append(pl.multiple_of(start, 16))
    return starts


def spread_rows(place, bits, whole, kept, sent):
    rows = whole.shape[0] >> len(bits)
    half = 1 << (len(bits) - 1)
    for i, start in enumerate(source_rows(place, bits, rows)):
        target = kept if i < half else sent
        at = (i % half) * rows
        target[at : at + rows, :] = whole[pl.ds(start, rows), :]


def feed_weights_grad(place, active, branch, hidden, change, bits_down, bits_up):
    chips = 1 << len(bits_down)
    if (D // chips) % 16:
        plain = lambda a, b: mm_rows(a, b).astype(LOW)
        return plain(active, branch), plain(hidden, change)

    def body(place, active, branch, hidden, change, down_kept, down_sent, up_kept, up_sent, down, up):
        for i in range(WIDTH // HALF):
            rows = slice(i * HALF, (i + 1) * HALF)
            down[rows, :] = mm_rows(active[:, rows], branch[...]).astype(LOW)
        spread_rows(place, bits_down, down, down_kept, down_sent)
        for i in range(WIDTH // HALF):
            cols = slice(i * HALF, (i + 1) * HALF)
            up[:, cols] = mm_rows(hidden[...], change[:, cols]).astype(LOW)
        spread_rows(place, bits_up, up, up_kept, up_sent)

    down = kernel_call(
        body,
        [((WIDTH // 2, D), LOW)] * 2 + [((D // 2, WIDTH), LOW)] * 2,
        (place, active, branch, hidden, change),
        [pltpu.VMEM((WIDTH, D), LOW), pltpu.VMEM((D, WIDTH), LOW)],
    )
    return down[:2], down[2:]


def out_weight_grad(place, count, context, branch):
    rows = D // count
    if (rows // 2) % 16:
        parts = mm_rows(context, branch).astype(LOW).reshape(count // 2, 2, rows // 2, 2, HALF)
        parts = parts.transpose(1, 0, 3, 2, 4).reshape(2, count // 2, rows, HALF)
        first = place[0] == 0
        return jnp.where(first, parts[0], parts[1]), jnp.where(first, parts[1], parts[0])

    def body(place, context, branch, own, other, whole):
        half = rows // 2
        whole[...] = mm_rows(context[...], branch[...]).astype(LOW)
        for j in range(count // 2):
            for target, core in ((own, place[0]), (other, 1 - place[0])):
                start = pl.multiple_of(j * rows + core * half, 16)
                target[j, :half, :] = whole[pl.ds(start, half), :HALF]
                target[j, half:, :] = whole[pl.ds(start, half), HALF:]

    return kernel_call(
        body,
        [((count // 2, rows, HALF), LOW)] * 2,
        (place, context, branch),
        [pltpu.VMEM((HALF, D), LOW)],
    )


def out_weight(place, count, own, got):
    rows = D // count
    half = rows // 2
    if half % 16:
        first = place[0] == 0
        own, got = [p.reshape(count // 2, 2, half, HALF) for p in (own, got)]
        both = jnp.stack([jnp.where(first, own, got), jnp.where(first, got, own)], axis=1)
        return both.transpose(0, 1, 3, 2, 4).reshape(HALF, D)

    def body(place, own, got, whole):
        for j in range(count // 2):
            for source, core in ((own, place[0]), (got, 1 - place[0])):
                start = pl.multiple_of(j * rows + core * half, 16)
                whole[pl.ds(start, half), :HALF] = source[j, :half, :]
                whole[pl.ds(start, half), HALF:] = source[j, half:, :]

    return kernel_call(body, [((HALF, D), LOW)], (place, own, got))[0]


def attend_weights_grad(place, count, hidden, change, out_own, out_got, bits, sums=None):
    rows = D // count
    extra = 0 if sums is None else 16

    def vec_rows(sums):
        attend, feed = [
            jnp.concatenate([part[...][:8] for part in pair], axis=0) for pair in (sums[::2], sums[1::2])
        ]
        row = lax.broadcasted_iota(jnp.int32, (16, 1), 0) % 8
        down = jnp.concatenate(
            [jnp.broadcast_to(part[...][6:7], (8, D)) for part in sums[1::2]], axis=0
        )
        return jnp.concatenate([jnp.where(row == 3, down, attend), feed], axis=1).astype(LOW)

    if (rows // 2) % 16:
        first = place[0] == 0
        out_parts = jnp.concatenate(
            [jnp.where(first, out_own, out_got), jnp.where(first, out_got, out_own)]
        )
        parts = mm_rows(hidden, change).astype(LOW).reshape(count, rows, 3 * HALF)
        whole = jnp.concatenate([parts, out_parts], axis=2).reshape(D, WIDTH)
        return whole if sums is None else (whole, vec_rows(sums))

    def body(place, hidden, change, out_own, out_got, *rest):
        *sums, kept, sent, whole = rest
        for i in range(3):
            cols = slice(i * HALF, (i + 1) * HALF)
            whole[:, cols] = mm_rows(hidden[...], change[:, cols]).astype(LOW)
        for source, core in ((out_own, place[0]), (out_got, 1 - place[0])):
            for j in range(count // 2):
                start = pl.multiple_of((core * (count // 2) + j) * rows, 16)
                whole[pl.ds(start, rows), 3 * HALF :] = source[j]
        spread_rows(place, bits, whole, kept, sent)
        if sums:
            sent[D // 2 :, :] = vec_rows(sums)

    return kernel_call(
        body,
        [((D // 2, WIDTH), LOW), ((D // 2 + extra, WIDTH), LOW)],
        (place, hidden, change, out_own, out_got) + tuple(sums or ()),
        [pltpu.VMEM((D, WIDTH), LOW)],
    )


class Links:
    def __init__(self):
        self.count = lax.axis_size("dp")
        self.bits = self.count.bit_length() - 1
        self.dp = lax.axis_index("dp")
        self.x = lax.axis_index("x")
        self.c = lax.axis_index("c")
        self.plain = (D // self.count // 2) % 16 != 0

    def own(self, bit):
        if bit == "c":
            return self.c
        if bit == "x":
            return self.x
        return (self.dp >> bit) & 1

    def flip(self, value, bit):
        step = {"c": 1, "x": 2}.get(bit)
        if step is None:
            step = 4 << bit
        pairs = [(place, place ^ step) for place in range(4 * self.count)]
        return lax.ppermute(value, AXES, pairs)

    def order(self, names):
        bits = {"x": ["x"], "y": [0], "1": [1], "2": list(range(self.bits))[:1:-1]}
        return [bit for name in names for bit in bits[name]]

    def gather(self, shards, names, also=None):
        orders = [self.order(name) for name in names]
        held = [shard.reshape((1,) * (self.bits + 1) + shard.shape) for shard in shards]

        def joined(held, got, bit):
            first = self.own(bit) == 0
            axis = 0 if bit == "x" else self.bits - bit
            return jnp.concatenate(
                [jnp.where(first, held, got), jnp.where(first, got, held)], axis=axis
            )

        for step in range(self.bits):
            got = [self.flip(h, order[step]) for h, order in zip(held, orders)]
            got, more = lax.optimization_barrier((got, self.flip(also, step)))
            also = (also.astype(WIDE) + more.astype(WIDE)).astype(LOW)
            held = [joined(h, g, order[step]) for h, g, order in zip(held, got, orders)]
        more = self.flip(also, "x")
        first = self.x == 0
        vectors = [jnp.where(first, also, more), jnp.where(first, more, also)]
        layers = []
        for one, order, shard in zip(held, orders, shards):
            bit = order[-1]
            if bit == "x":
                got = self.flip(one, bit)
                both = [jnp.where(first, one, got), jnp.where(first, got, one)]
            else:
                both = [joined(h, self.flip(h, bit), bit) for h in (one[:1], one[1:])]
            layers.append([part.reshape((self.count,) + shard.shape) for part in both])
        return layers, vectors

    def scatter(self, parts, names, extra=None):
        bits = self.order(names)
        if self.plain:
            return self.scatter_plain(parts, bits, extra)
        kept, sent = parts
        if extra is not None:
            extra = sent[kept.shape[0] :]
        for step, bit in enumerate(bits):
            got = self.flip(sent, bit)
            kept, sent, extra = add_rows(kept, got, extra, step == len(bits) - 1)
        return kept if extra is None else (kept, extra)

    def scatter_plain(self, parts, bits, extra):
        lanes = parts.shape[1]
        held = parts.reshape((2,) * (self.bits + 1) + (-1, lanes))
        for bit in bits:
            own, axis = self.own(bit), self.bits if bit == "x" else self.bits - 1 - bit
            kept = lax.dynamic_slice_in_dim(held, own, 1, axis)
            sent = lax.dynamic_slice_in_dim(held, 1 - own, 1, axis)
            if extra is None:
                got = self.flip(sent, bit)
            else:
                got = self.flip(jnp.concatenate([sent.reshape(-1, lanes), extra]), bit)
                split = got.shape[0] - extra.shape[0]
                extra = (extra.astype(WIDE) + got[split:].astype(WIDE)).astype(LOW)
                got = got[:split].reshape(sent.shape)
            held = (kept.astype(WIDE) + got.astype(WIDE)).astype(LOW)
        held = held.reshape(-1, lanes)
        return held if extra is None else (held, extra)


def add_rows(kept, got, extra, last):
    rows, lanes = kept.shape
    more = 0 if extra is None else extra.shape[0]
    half = rows if last else rows // 2

    def body(place, kept, got, *rest):
        total = lambda at, size: (
            kept[at : at + size, :].astype(WIDE) + got[at : at + size, :].astype(WIDE)
        ).astype(LOW)
        if more:
            extra_sum = (rest[0][...].astype(WIDE) + got[rows:, :].astype(WIDE)).astype(LOW)
            rest[-1][...] = extra_sum
            rest = rest[1:-1]
        rest[0][...] = total(0, half)
        if not last:
            rest[1][:half, :] = total(half, half)
            if more:
                rest[1][half:, :] = extra_sum

    outs = [((half, lanes), LOW)]
    if not last:
        outs.append(((half + more, lanes), LOW))
    if more:
        outs.append(((more, lanes), LOW))
    ins = (jnp.zeros((1,), jnp.int32), kept, got) + ((extra,) if more else ())
    results = list(kernel_call(body, outs, ins))
    extra = results.pop() if more else None
    return results[0], None if last else results[1], extra


def adam_update(master, first, second, gradient):
    first_new = BETA_ONE * first + (1.0 - BETA_ONE) * gradient
    second_new = BETA_TWO * second + (1.0 - BETA_TWO) * gradient * gradient
    update = first_new / BIAS_ONE / (jnp.sqrt(second_new / BIAS_TWO) + ADAM_EPSILON)
    return (update + WEIGHT_DECAY * master, first_new, second_new)


def on_device(
    inputs,
    cotangent,
    in_master,
    in_first,
    in_second,
    down_master,
    down_first,
    down_second,
    vec_master,
    vec_first,
    vec_second,
):
    links = Links()
    count, x, c = links.count, links.x, links.c
    rows = D // count
    half_rows = rows // 2
    vec_part = VEC // count
    first_core = c == 0
    first_chip = x == 0
    place = jnp.stack([c, links.dp, x]).astype(jnp.int32)

    def mine(one, other):
        return jnp.where(first_core, one, other)

    def trade(part):
        return links.flip(part, "c")

    in_low = in_master[0].astype(LOW)
    out_rows = in_low[:, 3 * D :]
    pieces = []
    for core in (0, 1):
        out_half = out_rows[core * half_rows : (core + 1) * half_rows]
        pieces.append(
            jnp.concatenate(
                [in_low[:, i * D + core * HALF : i * D + (core + 1) * HALF] for i in range(3)]
                + [jnp.concatenate([out_half[:, :HALF], out_half[:, HALF:]], axis=0)],
                axis=1,
            )
        )
    got = trade(mine(pieces[1], in_low[:, :WIDTH]))
    attend_shard = mine(pieces[0], got)
    up_shard = mine(got, in_low[:, WIDTH:])
    down_shard = down_master[0].astype(LOW)

    placed = lax.dynamic_update_slice(
        jnp.zeros((VEC,), WIDE), vec_master[0], (links.dp * vec_part,)
    ).reshape(-1, D)
    high = lax.reduce_precision(placed, 8, 7)
    vec_both = jnp.pad(jnp.concatenate([high, placed - high]).astype(LOW), ((0, 4), (0, 0)))
    vec_got = trade(vec_both)
    vec_both = jnp.concatenate([mine(vec_both, vec_got), mine(vec_got, vec_both)])

    (attend_all, up_all, down_all), vectors = links.gather(
        [attend_shard, up_shard, down_shard], ["21xy", "2xy1", "2y1x"], vec_both
    )
    vecs, qkv, out, up, down = [], [], [], [], []
    for layer in (0, 1):
        vec = vectors[layer].astype(WIDE)
        vecs.append([vec[i : i + 6] + vec[i + 6 : i + 12] for i in (0, 16)])
        whole = attend_all[layer]
        qkv.append(whole[:, :, : 3 * HALF].reshape(D, 3 * HALF))
        parts = whole[:, :, 3 * HALF :].reshape(2, count // 2, rows, HALF)
        out.append(
            out_weight(place, count, mine(parts[0], parts[1]), trade(mine(parts[1], parts[0])))
        )
        up.append(up_all[layer].reshape(D, WIDTH))
        down.append(down_all[layer].reshape(WIDTH, D))

    hidden = [lax.dynamic_slice_in_dim(inputs, x * SEQ, SEQ, 0)]
    part, mixing_0, chances_0, context_0 = attend_first(
        place, hidden[0], qkv[0], out[0], vecs[0][0]
    )
    next_hidden, normed_0, spread_0, part, active_0, slope_0 = feed_forward(
        place, hidden[0], part, trade(part), vecs[0][0], vecs[0][1], up[0], down[0]
    )
    hidden.append(next_hidden)
    next_hidden, normed_1, spread_1, part, mixing_1, chances_1, context_1 = attend_next(
        place, hidden[1], part, trade(part), vecs[0][1], vecs[0][0], qkv[1], out[1], vecs[1][0]
    )
    hidden.append(next_hidden)
    next_hidden, normed_2, spread_2, part, active_1, slope_1 = feed_forward(
        place, hidden[2], part, trade(part), vecs[1][0], vecs[1][1], up[1], down[1]
    )
    hidden.append(next_hidden)

    def to_sections(values):
        low, high = mine(values[0], values[1]), mine(values[2], values[3])
        own = jnp.where(first_chip, low, high)
        got = links.flip(jnp.where(first_chip, high, low), "x")
        return jnp.concatenate(
            [jnp.where(first_chip, own, got), jnp.where(first_chip, got, own)]
        )[None]

    bits = {name: links.order(name) for name in ("x1y2", "1yx2", "yx21")}
    cotangent_rows = lax.dynamic_slice_in_dim(cotangent, x * SEQ, SEQ, 0)
    last, summed, branch, change, part, feed_sums_1 = feed_last(
        place, hidden[3], part, trade(part), vecs[1][0], vecs[1][1], up[1], down[1], slope_1, cotangent_rows
    )
    section_outputs = to_sections(hidden[1:] + [last])
    part_got = trade(part)
    down_parts_1, up_parts_1 = feed_weights_grad(
        place, active_1, branch, hidden[3], change, bits["x1y2"], bits["1yx2"]
    )
    down_sum_1 = links.scatter(down_parts_1, "x1y2")
    up_sum_1 = links.scatter(up_parts_1, "1yx2")
    grad_3, summed, branch, change, part, attend_sums_1 = attend_back(
        place, summed, part, part_got, normed_2, spread_2, vecs[1][0], qkv[1], out[1], mixing_1, chances_1
    )
    part_got = trade(part)
    out_own, out_other = out_weight_grad(place, count, context_1, branch)
    attend_parts = attend_weights_grad(
        place, count, hidden[2], change, out_own, trade(out_other), bits["yx21"]
    )
    attend_sum_1 = links.scatter(attend_parts, "yx21")
    grad_2, summed, branch, change, part, feed_sums_0 = feed_back(
        place, summed, part, part_got, normed_1, spread_1, vecs[0][1], up[0], down[0], slope_0
    )
    part_got = trade(part)
    down_parts_0, up_parts_0 = feed_weights_grad(
        place, active_0, branch, hidden[1], change, bits["x1y2"], bits["1yx2"]
    )
    down_sum_0 = links.scatter(down_parts_0, "x1y2")
    up_sum_0 = links.scatter(up_parts_0, "1yx2")
    grad_1, summed, branch, change, part, attend_sums_0 = attend_back(
        place, summed, part, part_got, normed_0, spread_0, vecs[0][0], qkv[0], out[0], mixing_0, chances_0
    )
    part_got = trade(part)
    out_own, out_other = out_weight_grad(place, count, context_0, branch)
    attend_parts = attend_weights_grad(
        place,
        count,
        hidden[0],
        change,
        out_own,
        trade(out_other),
        bits["yx21"],
        (attend_sums_0, feed_sums_0, attend_sums_1, feed_sums_1),
    )
    if links.plain:
        attend_sum_0, vec_total = links.scatter(attend_parts[0], "yx21", attend_parts[1])
    else:
        attend_sum_0, vec_total = links.scatter(attend_parts, "yx21", True)
    grad_0 = (summed + part.astype(WIDE) + part_got.astype(WIDE)).astype(LOW)
    section_input_grads = to_sections([grad_0, grad_1, grad_2, grad_3])

    whole = []
    for one, other in (
        (attend_sum_0, attend_sum_1),
        (up_sum_0, up_sum_1),
        (down_sum_0, down_sum_1),
    ):
        got = links.flip(jnp.where(first_chip, other, one), "x")
        own = jnp.where(first_chip, one, other)
        whole.append(
            jnp.concatenate([jnp.where(first_chip, own, got), jnp.where(first_chip, got, own)])
        )
    attend_sum, up_sum, down_sum = whole

    got = trade(jnp.concatenate([mine(up_sum, attend_sum), vec_total]))
    vec_total = vec_total.astype(WIDE) + got[rows:].astype(WIDE)
    got = got[:rows]
    kept = mine(attend_sum, up_sum)
    first, second = mine(kept, got), mine(got, kept)

    def joined(one, other):
        out_one, out_other = one[:, 3 * HALF :], other[:, 3 * HALF :]
        out_cols = [
            jnp.concatenate([out_one[i : i + half_rows], out_other[i : i + half_rows]])
            for i in (0, half_rows)
        ]
        cols = [part[:, i * HALF : (i + 1) * HALF] for i in range(3) for part in (one, other)]
        return jnp.concatenate(cols + out_cols, axis=1)

    in_sum = mine(joined(first, second), jnp.concatenate([first, second], axis=1))
    in_sum = in_sum.astype(WIDE)[None]
    down_sum = down_sum.astype(WIDE)[None]
    vec_sum = lax.dynamic_slice(vec_total, (8 * x, D * c), (6, D)).reshape(VEC)
    vec_sum = lax.dynamic_slice(vec_sum, (links.dp * vec_part,), (vec_part,))[None]

    in_step, in_first_new, in_second_new = adam_update(in_master, in_first, in_second, in_sum)
    down_step, down_first_new, down_second_new = adam_update(
        down_master, down_first, down_second, down_sum
    )
    vec_step, vec_first_new, vec_second_new = adam_update(
        vec_master, vec_first, vec_second, vec_sum
    )
    return (
        section_outputs,
        section_input_grads,
        in_sum,
        down_sum,
        vec_sum,
        in_step,
        in_first_new,
        in_second_new,
        down_step,
        down_first_new,
        down_second_new,
        vec_step,
        vec_first_new,
        vec_second_new,
    )


def solution(mesh):
    grid = Mesh(mesh.devices.reshape(mesh.shape["dp"], 2, 2), AXES)
    tokens = P("dp", None)
    matrix = P(("x", "c"), "dp", None)
    vector = P(("x", "c"), "dp")
    return jax.shard_map(
        on_device,
        mesh=grid,
        in_specs=(tokens,) * 2 + (matrix,) * 6 + (vector,) * 3,
        out_specs=(matrix,) * 4 + (vector,) + (matrix,) * 6 + (vector,) * 3,
        check_vma=False,
    )
```

time: 629 us -> 445 us (0.71)
  local copies, waits for them, and re-layouts: 145 us -> 17.2 us
  Pallas kernels: 0 us -> 108 us
  matrix products: 83.9 us -> 0 us
  other arithmetic: 98.1 us -> 48.2 us
  waiting for transfers between devices: 230 us -> 206 us
    pallas_call x0 -> x40, Pallas kernels: none -> 108 us  [kernel_call(): pl.pallas_call(body, out_shape=[jax.ShapeDtypeStruct(s, d) for s, d in ou...]
    dot_general x34 -> x0, matrix products: 72.6 us -> none  [the longest x8 19.9 us: inner_rows(): lax.dot_general(former, latter, (((0,), (0,)), ((), ())), preferred_eleme...]
    reshape x14 -> x2, local copies, waits for them, and re-layouts: 33.3 us -> 0.01 us  [the longest x1 0.01 us: on_device(): placed = lax.dynamic_update_slice(jnp.zeros((VEC,), WIDE), vec_master[0],...]
    unnamed x341 -> x142, local copies, waits for them, and re-layouts: 37.1 us -> 12.5 us
    ppermute x52 -> x62, waiting for transfers between devices: 230 us -> 206 us  [flip(): return lax.ppermute(value, AXES, pairs)]
    slice x29 -> x7, local copies, waits for them, and re-layouts: 24.8 us -> 3.67 us  [the longest x2 1.53 us: on_device(): qkv.append(whole[:, :, :3 * HALF].reshape(D, 3 * HALF))]
    convert_element_type x29 -> x5, other arithmetic: 20.4 us -> 1.52 us  [the longest x1 1.45 us: on_device(): in_low = in_master[0].astype(LOW)]
    reduce_sum x18 -> x0, other arithmetic: 17.2 us -> none  [the longest x4 6.72 us: norm_backward(): jnp.sum(incoming * normed, axis=0)]
  transfers between devices with their start and end apart: 52 -> 62, of which waited for: 27 -> 32; matrix products, arithmetic and copies ran while one was open for 34% -> 9% of each run, Pallas kernels for 0% -> 18%
where the time goes in v2:
time: 445 us; the launch traced here: 437 us
  waiting for transfers between devices  206 us (46%)
  Pallas kernels  108 us (24%)
  starting transfers between devices  55.2 us (12%)
  other arithmetic  48.2 us (11%)
  local copies, waits for them, and re-layouts  17.2 us (4%)
    ppermute x62, waiting for transfers between devices, flip(): return lax.ppermute(value, AXES, pairs)  206 us
    pallas_call x40, Pallas kernels, kernel_call(): pl.pallas_call(body, out_shape=[jax.ShapeDtypeStruct(s, d) for s, d in ou...  108 us
    ppermute x62, starting transfers between devices, flip(): return lax.ppermute(value, AXES, pairs)  55.2 us
    select_n x11, other arithmetic, joined(): jnp.where(first, held, got)  13.1 us
    unnamed x142, local copies, waits for them, and re-layouts  12.5 us
    concatenate x12, other arithmetic, joined(): jnp.concatenate([jnp.where(first, held, got), jnp.where(first, got, held)...  11 us
  transfers between devices with their start and end apart: 62, of which 32 were waited for; matrix products, arithmetic and copies ran while one was open for 9% of the time, Pallas kernels for 18%

profile of v2, /device:TPU:0, one launch (start us, length us, event | category | flops | bytes accessed | tf_op | source)
XLA Modules:
  0.0 436.6 jit_solution(2750759933109591155)
XLA Ops:
  5.3 4.0 collective-permute-start.3
  10.5 2.9 collective-permute-start.1
  13.5 1.6 collective-permute-start.5
  15.1 2.6 collective-permute-done.5
  17.6 18.8 %collective-permute-done.3 = bf16[1,1,1,1,192,768]{5,4,3,2,1,0:T(8,128)(2,1)} collective-permute-done((bf16[1,1,1,1,192,768]{5,4,3,2,1,0:T(8,128)(2,1)}, bf16[1,1,1,1,192,768]{5,4,3,2,1,0:T(8,128)(2,1)}, u32[]{:S(2)}, u32[]{:S(2)}) %collective-permute-start.3) | collective-permute-done | bytes 294944 | tf_op jit(solution)/shard_map/ppermute | solution.py:402
  36.4 6.3 %collective-permute-done.2 = bf16[1,1,1,1,96,1536]{5,4,3,2,1,0:T(8,128)(2,1)} collective-permute-done((bf16[1,1,1,1,96,1536]{5,4,3,2,1,0:T(8,128)(2,1)S(1)}, bf16[1,1,1,1,96,1536]{5,4,3,2,1,0:T(8,128)(2,1)}, u32[]{:S(2)}, u32[]{:S(2)}) %collective-permute-start.2) | collective-permute-done | bytes 294944 | tf_op jit(solution)/shard_map/ppermute | solution.py:402
  42.7 5.6 %collective-permute-done.1 = bf16[1,1,1,1,96,1536]{5,4,3,2,1,0:T(8,128)(2,1)S(1)} collective-permute-done((bf16[1,1,1,1,96,1536]{5,4,3,2,1,0:T(8,128)(2,1)S(1)}, bf16[1,1,1,1,96,1536]{5,4,3,2,1,0:T(8,128)(2,1)S(1)}, u32[]{:S(2)}, u32[]{:S(2)}) %collective-permute-start.1) | collective-permute-done | bytes 294944 | tf_op jit(solution)/shard_map/ppermute | solution.py:402
  54.9 1.6 collective-permute-start.8
  57.9 9.8 %collective-permute-done.9 = bf16[32,768]{1,0:T(8,128)(2,1)S(1)} collective-permute-done((bf16[32,768]{1,0:T(8,128)(2,1)S(1)}, bf16[32,768]{1,0:T(8,128)(2,1)S(1)}, u32[]{:S(2)}, u32[]{:S(2)}) %collective-permute-start.9) | collective-permute-done | bytes 49184 | tf_op jit(solution)/shard_map/ppermute | solution.py:402
  79.5 3.4 collective-permute-start.13
  83.0 21.8 %collective-permute-done.13 = bf16[32,768]{1,0:T(8,128)(2,1)S(1)} collective-permute-done((bf16[32,768]{1,0:T(8,128)(2,1)S(1)}, bf16[32,768]{1,0:T(8,128)(2,1)S(1)}, u32[]{:S(2)}, u32[]{:S(2)}) %collective-permute-start.13) | collective-permute-done | bytes 49184 | tf_op jit(solution)/shard_map/ppermute | solution.py:402
  104.7 1.8 collective-permute-done.12
  109.0 1.6 broadcast_select_fusion.4
  111.3 3.4 collective-permute-start.24
  116.3 1.6 broadcast_select_fusion.3
  117.9 1.7 pad_maximum_fusion.2
  120.9 18.7 %collective-permute-done.14 = bf16[1,2,2,1,96,1536]{5,4,3,2,1,0:T(8,128)(2,1)S(1)} collective-permute-done((bf16[1,2,2,1,96,1536]{5,4,3,2,1,0:T(8,128)(2,1)S(1)}, bf16[1,2,2,1,96,1536]{5,4,3,2,1,0:T(8,128)(2,1)S(1)}, u32[]{:S(2)}, u32[]{:S(2)}) %collective-permute-start.14) | collective-permute-done | bytes 1179680 | tf_op jit(solution)/shard_map/ppermute | solution.py:402
  140.0 22.5 %collective-permute-done.18 = bf16[1,2,1,2,96,1536]{5,4,3,2,1,0:T(8,128)(2,1)S(1)} collective-permute-done((bf16[1,2,1,2,96,1536]{5,4,3,2,1,0:T(8,128)(2,1)S(1)}, bf16[1,2,1,2,96,1536]{5,4,3,2,1,0:T(8,128)(2,1)S(1)}, u32[]{:S(2)}, u32[]{:S(2)}) %collective-permute-start.18) | collective-permute-done | bytes 1179680 | tf_op jit(solution)/shard_map/ppermute | solution.py:402
  164.5 6.1 %shard_map.219 = (bf16[512,768]{1,0:T(8,128)(2,1)S(1)}, bf16[512,1152]{1,0:T(8,128)(2,1)S(1)}, bf16[6,512,512]{2,1,0:T(8,128)(2,1)}, bf16[512,384]{1,0:T(8,128)(2,1)S(1)}) custom-call(s32[3]{0:T(128)S(1)} %pad_add_fusion.place, bf16[512,768]{1,0:T(8,128)(2,1)S(1)} %constant_dynamic-slice_fusion.1.hidden.before, bf16[768,1152]{1,0:T(8,128)(2,1)S(1)} %bitcast.63, ...), custom_call_target="tpu_custom_call" | custom-call | flops 1000 | bytes 1000 | tf_op jit(solution)/shard_map/pallas_call | solution.py:46
  170.7 3.6 broadcast_select_fusion.13
  174.3 1.6 pad_maximum_fusion.1
  175.9 4.3 broadcast_select_fusion
  180.3 7.9 %shard_map.220 = (bf16[512,768]{1,0:T(8,128)(2,1)S(1)}, bf16[512,768]{1,0:T(8,128)(2,1)S(1)}, f32[512,1]{1,0:T(8,128)S(1)}, bf16[512,768]{1,0:T(8,128)(2,1)S(1)}...) custom-call(s32[3]{0:T(128)S(1)} %pad_add_fusion.place, ...), custom_call_target="tpu_custom_call" | custom-call | flops 1000 | bytes 1000 | tf_op jit(solution)/shard_map/pallas_call | solution.py:46
  191.6 8.1 %shard_map.222 = (bf16[512,768]{1,0:T(8,128)(2,1)S(1)}, bf16[512,768]{1,0:T(8,128)(2,1)S(1)}, f32[512,1]{1,0:T(8,128)S(1)}, bf16[512,768]{1,0:T(8,128)(2,1)S(1)}...) custom-call(s32[3]{0:T(128)S(1)} %pad_add_fusion.place, ...), custom_call_target="tpu_custom_call" | custom-call | flops 1000 | bytes 1000 | tf_op jit(solution)/shard_map/pallas_call | solution.py:46
  200.0 1.6 broadcast_select_fusion.7
  201.5 1.6 pad_maximum_fusion.4
  203.2 7.5 %shard_map.223 = (bf16[512,768]{1,0:T(8,128)(2,1)S(1)}, bf16[512,768]{1,0:T(8,128)(2,1)S(1)}, f32[512,1]{1,0:T(8,128)S(1)}, bf16[512,768]{1,0:T(8,128)(2,1)S(1)}...) custom-call(s32[3]{0:T(128)S(1)} %pad_add_fusion.place, bf16[512,768]{1,0:T(8,128)(2,1)S(1)} %get-tuple-element.145.before.hidden, ...), custom_call_target="tpu_custom_call" | custom-call | flops 1000 | bytes 1000 | tf_op jit(solution)/shard_map/pallas_call | solution.py:46
  211.0 2.0 collective-permute-done.25.got
  213.0 8.3 %shard_map.224 = (bf16[512,768]{1,0:T(8,128)(2,1)S(1)}, f32[512,768]{1,0:T(8,128)}, bf16[512,768]{1,0:T(8,128)(2,1)S(1)}, bf16[512,1536]{1,0:T(8,128)(2,1)}, bf1...) custom-call(s32[3]{0:T(128)S(1)} %pad_add_fusion.place, bf16[512,768]{1,0:T(8,128)(2,1)S(1)} %get-tuple-element.147.before.hidden, ...), custom_call_target="tpu_custom_call" | custom-call | flops 1000 | bytes 1000 | tf_op jit(solution)/shard_map/pallas_call | solution.py:46
  221.6 2.1 collective-permute-done.27.got
  223.6 12.2 %shard_map.225 = (bf16[512,768]{1,0:T(8,128)(2,1)S(1)}, f32[512,768]{1,0:T(8,128)}, bf16[512,768]{1,0:T(8,128)(2,1)S(1)}, bf16[512,1152]{1,0:T(8,128)(2,1)}, bf1...) custom-call(s32[3]{0:T(128)S(1)} %pad_add_fusion.place, f32[512,768]{1,0:T(8,128)} %get-tuple-element.151.before, ...), custom_call_target="tpu_custom_call" | custom-call | flops 1000 | bytes 1000 | tf_op jit(solution)/shard_map/pallas_call | solution.py:46
  236.0 1.6 broadcast_select_fusion.25
  239.0 6.2 %shard_map.245 = (bf16[768,768]{1,0:T(8,128)(2,1)S(1)}, bf16[768,768]{1,0:T(8,128)(2,1)}, bf16[384,1536]{1,0:T(8,128)(2,1)S(1)}, bf16[384,1536]{1,0:T(8,128)(2,1)}) custom-call(s32[3]{0:T(128)S(1)} %pad_add_fusion.place, bf16[512,1536]{1,0:T(8,128)(2,1)} %get-tuple-element.218.active, bf16[512,768]{1,0:T(8,128)(2,1)S(1)} %get-tuple-element.219.branch, ...), custom_call_target="tpu_custom_call" | custom-call | flops 1000 | bytes 1000 | tf_op jit(solution)/shard_map/pallas_call | solution.py:46
  245.2 1.7 collective-permute-start.47
  248.8 1.6 collective-permute-done.37.out_got
  250.4 3.2 shard_map.235
  255.1 8.5 %shard_map.226 = (bf16[512,768]{1,0:T(8,128)(2,1)S(1)}, f32[512,768]{1,0:T(8,128)}, bf16[512,768]{1,0:T(8,128)(2,1)S(1)}, bf16[512,1536]{1,0:T(8,128)(2,1)}, bf1...) custom-call(s32[3]{0:T(128)S(1)} %pad_add_fusion.place, f32[512,768]{1,0:T(8,128)} %get-tuple-element.157.before, ...), custom_call_target="tpu_custom_call" | custom-call | flops 1000 | bytes 1000 | tf_op jit(solution)/shard_map/pallas_call | solution.py:46
  264.5 6.4 %shard_map.240 = (bf16[768,768]{1,0:T(8,128)(2,1)S(1)}, bf16[768,768]{1,0:T(8,128)(2,1)}, bf16[384,1536]{1,0:T(8,128)(2,1)S(1)}, bf16[384,1536]{1,0:T(8,128)(2,1)}) custom-call(s32[3]{0:T(128)S(1)} %pad_add_fusion.place, bf16[512,1536]{1,0:T(8,128)(2,1)} %get-tuple-element.207.active, bf16[512,768]{1,0:T(8,128)(2,1)S(1)} %get-tuple-element.208.branch, ...), custom_call_target="tpu_custom_call" | custom-call | flops 1000 | bytes 1000 | tf_op jit(solution)/shard_map/pallas_call | solution.py:46
  271.2 2.2 collective-permute-done.47.got
  274.0 2.2 shard_map.246
  276.3 7.3 %collective-permute-done.57.got = bf16[768,768]{1,0:T(8,128)(2,1)} collective-permute-done((bf16[768,768]{1,0:T(8,128)(2,1)}, bf16[768,768]{1,0:T(8,128)(2,1)}, u32[]{:S(2)}, u32[]{:S(2)}) %collective-permute-start.57) | collective-permute-done | bytes 1179680 | tf_op jit(solution)/shard_map/ppermute | solution.py:402
  285.1 2.3 shard_map.254
  289.1 1.7 collective-permute-start.58
  293.2 12.2 %shard_map.227 = (bf16[512,768]{1,0:T(8,128)(2,1)S(1)}, f32[512,768]{1,0:T(8,128)}, bf16[512,768]{1,0:T(8,128)(2,1)S(1)}, bf16[512,1152]{1,0:T(8,128)(2,1)}, bf1...) custom-call(s32[3]{0:T(128)S(1)} %pad_add_fusion.place, f32[512,768]{1,0:T(8,128)} %get-tuple-element.162.before, ...), custom_call_target="tpu_custom_call" | custom-call | flops 1000 | bytes 1000 | tf_op jit(solution)/shard_map/pallas_call | solution.py:46
  308.3 1.6 shard_map.241
  314.3 3.3 shard_map.229
  317.5 11.4 %collective-permute-done.49.got = bf16[96,1536]{1,0:T(8,128)(2,1)S(1)} collective-permute-done((bf16[96,1536]{1,0:T(8,128)(2,1)S(1)}, bf16[96,1536]{1,0:T(8,128)(2,1)S(1)}, u32[]{:S(2)}, u32[]{:S(2)}) %collective-permute-start.49) | collective-permute-done | bytes 294944 | tf_op jit(solution)/shard_map/ppermute | solution.py:402
  329.5 2.5 collective-permute-done.59.got
  333.4 1.7 collective-permute-start.50
  342.8 4.3 collective-permute-done.50.got
  347.1 3.1 collective-permute-done.60.got
  355.9 7.4 %collective-permute-done.40.got = bf16[96,1536]{1,0:T(8,128)(2,1)S(1)} collective-permute-done((bf16[96,1536]{1,0:T(8,128)(2,1)S(1)}, bf16[96,1536]{1,0:T(8,128)(2,1)S(1)}, u32[]{:S(2)}, u32[]{:S(2)}) %collective-permute-start.40) | collective-permute-done | bytes 294944 | tf_op jit(solution)/shard_map/ppermute | solution.py:402
  363.5 4.6 %collective-permute-done.54.got = bf16[384,768]{1,0:T(8,128)(2,1)} collective-permute-done((bf16[384,768]{1,0:T(8,128)(2,1)}, bf16[384,768]{1,0:T(8,128)(2,1)}, u32[]{:S(2)}, u32[]{:S(2)}) %collective-permute-start.54) | collective-permute-done | bytes 589856 | tf_op jit(solution)/shard_map/ppermute | solution.py:402
  370.0 2.1 broadcast_select_fusion.21
  372.7 3.6 collective-permute-done.55.got
  376.6 1.7 collective-permute-done.46.got
  379.2 1.7 collective-permute-start.51
  380.8 2.4 collective-permute-done.56.got
  383.8 22.5 %collective-permute-done.34.got = bf16[208,1536]{1,0:T(8,128)(2,1)S(1)} collective-permute-done((bf16[208,1536]{1,0:T(8,128)(2,1)S(1)}, bf16[208,1536]{1,0:T(8,128)(2,1)S(1)}, u32[]{:S(2)}, u32[]{:S(2)}) %collective-permute-start.34) | collective-permute-done | bytes 639008 | tf_op jit(solution)/shard_map/ppermute | solution.py:402
  406.4 2.7 collective-permute-start.35
  409.2 9.3 %collective-permute-done.35.got = bf16[112,1536]{1,0:T(8,128)(2,1)S(1)} collective-permute-done((bf16[112,1536]{1,0:T(8,128)(2,1)S(1)}, bf16[112,1536]{1,0:T(8,128)(2,1)S(1)}, u32[]{:S(2)}, u32[]{:S(2)}) %collective-permute-start.35) | collective-permute-done | bytes 344096 | tf_op jit(solution)/shard_map/ppermute | solution.py:402
  418.7 5.6 %collective-permute-done.36.got = bf16[64,1536]{1,0:T(8,128)(2,1)S(1)} collective-permute-done((bf16[64,1536]{1,0:T(8,128)(2,1)S(1)}, bf16[64,1536]{1,0:T(8,128)(2,1)S(1)}, u32[]{:S(2)}, u32[]{:S(2)}) %collective-permute-start.36) | collective-permute-done | bytes 196640 | tf_op jit(solution)/shard_map/ppermute | solution.py:402
  426.5 3.1 collective-permute-done.42
  433.9 2.5 multiply_add_fusion
  (323 shorter events, 84.1 us)
Async XLA Ops:
  0.6 78.8 %copy-start = (bf16[1024,768]{1,0:T(8,128)(2,1)S(1)}, bf16[1024,768]{1,0:T(8,128)(2,1)}, u32[]{:S(2)}) copy-start(bf16[1024,768]{1,0:T(8,128)(2,1)} %param.11) | copy-start | bytes 4718596
  3.5 5.8 %collective-permute-start = (bf16[96,1536]{1,0:T(8,128)(2,1)S(1)}, bf16[96,1536]{1,0:T(8,128)(2,1)}, u32[]{:S(2)}, u32[]{:S(2)}) collective-permute-start(bf16[96,1536]{1,0:T(8,128)(2,1)S(1)} %slice_select_fusion.1), channel_id=1, source_target_pairs={{0,1},{1,0},{2,3},{3,2},{4,5},{5,4},{6,7},{7,6},{8,9},{9,8},{10,11... | collective-permute-start | bytes 884744 | tf_op jit(solution)/shard_map/ppermute | solution.py:402
  4.4 9.0 %collective-permute-start.4 = (bf16[16,768]{1,0:T(8,128)(2,1)S(1)}, bf16[16,768]{1,0:T(8,128)(2,1)S(1)}, u32[]{:S(2)}, u32[]{:S(2)}) collective-permute-start(bf16[16,768]{1,0:T(8,128)(2,1)S(1)} %fusion.18), channel_id=1, source_target_pairs={{0,1},{1,0},{2,3},{3,2},{4,5},{5,4},{6,7},{7,6},{8,9},{9,8},{10,11... | collective-permute-start | bytes 73736 | tf_op jit(solution)/shard_map/ppermute | solution.py:402
  5.3 31.1 %collective-permute-start.3 = (bf16[1,1,1,1,192,768]{5,4,3,2,1,0:T(8,128)(2,1)}, bf16[1,1,1,1,192,768]{5,4,3,2,1,0:T(8,128)(2,1)}, u32[]{:S(2)}, u32[]{:S(2)}) collective-permute-start(bf16[1,1,1,1,192,768]{5,4,3,2,1,0:T(8,128)(2,1)} %convert_bitcast_fusion.1), channel_id=1, source_target_pairs={{0,16},{1,17},{2,18},{3,19},{4,20},{5,21},{6,22},{7,23},{8,24},{9,... | collective-permute-start | bytes 884744 | tf_op jit(solution)/shard_map/ppermute | solution.py:402
  10.5 32.3 %collective-permute-start.2 = (bf16[1,1,1,1,96,1536]{5,4,3,2,1,0:T(8,128)(2,1)S(1)}, bf16[1,1,1,1,96,1536]{5,4,3,2,1,0:T(8,128)(2,1)}, u32[]{:S(2)}, u32[]{:S(2)}) collective-permute-start(bf16[1,1,1,1,96,1536]{5,4,3,2,1,0:T(8,128)(2,1)S(1)} %get-tuple-element.325), channel_id=1, source_target_pairs={{0,16},{1,17},{2,18},{3,19},{4,20},{5,21},{6,22},{7,23},{8,24},{9,... | collective-permute-start | bytes 884744 | tf_op jit(solution)/shard_map/ppermute | solution.py:402
  10.5 37.8 %collective-permute-start.1 = (bf16[1,1,1,1,96,1536]{5,4,3,2,1,0:T(8,128)(2,1)S(1)}, bf16[1,1,1,1,96,1536]{5,4,3,2,1,0:T(8,128)(2,1)S(1)}, u32[]{:S(2)}, u32[]{:S(2)}) collective-permute-start(bf16[1,1,1,1,96,1536]{5,4,3,2,1,0:T(8,128)(2,1)S(1)} %get-tuple-element.326), channel_id=1, source_target_pairs={{0,16},{1,17},{2,18},{3,19},{4,20},{5,21},{6,22},{7,23},{8,24},{9,... | collective-permute-start | bytes 884744 | tf_op jit(solution)/shard_map/ppermute | solution.py:402
  13.5 4.2 collective-permute-start.5
  51.8 16.0 %collective-permute-start.6 = (bf16[1,2,1,1,96,1536]{5,4,3,2,1,0:T(8,128)(2,1)}, bf16[1,2,1,1,96,1536]{5,4,3,2,1,0:T(8,128)(2,1)}, u32[]{:S(2)}, u32[]{:S(2)}) collective-permute-start(bf16[1,2,1,1,96,1536]{5,4,3,2,1,0:T(8,128)(2,1)} %pad_maximum_fusion.9), channel_id=1, source_target_pairs={{0,8},{1,9},{2,10},{3,11},{4,12},{5,13},{6,14},{7,15},{8,0},{9,1},... | collective-permute-start | bytes 1769480 | tf_op jit(solution)/shard_map/ppermute | solution.py:402
  53.4 15.2 %collective-permute-start.7 = (bf16[1,2,1,1,96,1536]{5,4,3,2,1,0:T(8,128)(2,1)}, bf16[1,2,1,1,96,1536]{5,4,3,2,1,0:T(8,128)(2,1)S(1)}, u32[]{:S(2)}, u32[]{:S(2)}) collective-permute-start(bf16[1,2,1,1,96,1536]{5,4,3,2,1,0:T(8,128)(2,1)} %pad_maximum_fusion.10), channel_id=1, source_target_pairs={{0,2},{1,3},{2,0},{3,1},{4,6},{5,7},{6,4},{7,5},{8,10},{9,11},{10,... | collective-permute-start | bytes 1769480 | tf_op jit(solution)/shard_map/ppermute | solution.py:402
  54.9 14.9 %collective-permute-start.8 = (bf16[1,2,1,1,192,768]{5,4,3,2,1,0:T(8,128)(2,1)S(1)}, bf16[1,2,1,1,192,768]{5,4,3,2,1,0:T(8,128)(2,1)}, u32[]{:S(2)}, u32[]{:S(2)}) collective-permute-start(bf16[1,2,1,1,192,768]{5,4,3,2,1,0:T(8,128)(2,1)S(1)} %pad_maximum_fusion.11), channel_id=1, source_target_pairs={{0,4},{1,5},{2,6},{3,7},{4,0},{5,1},{6,2},{7,3},{8,12},{9,13},{10,... | collective-permute-start | bytes 1769480 | tf_op jit(solution)/shard_map/ppermute | solution.py:402
  56.5 11.2 %collective-permute-start.9 = (bf16[32,768]{1,0:T(8,128)(2,1)S(1)}, bf16[32,768]{1,0:T(8,128)(2,1)S(1)}, u32[]{:S(2)}, u32[]{:S(2)}) collective-permute-start(bf16[32,768]{1,0:T(8,128)(2,1)S(1)} %add_convert_fusion.3), channel_id=1, source_target_pairs={{0,8},{1,9},{2,10},{3,11},{4,12},{5,13},{6,14},{7,15},{8,0},{9,1},... | collective-permute-start | bytes 147464 | tf_op jit(solution)/shard_map/ppermute | solution.py:402
  72.2 32.5 %collective-permute-start.10 = (bf16[1,2,2,1,96,1536]{5,4,3,2,1,0:T(8,128)(2,1)}, bf16[1,2,2,1,96,1536]{5,4,3,2,1,0:T(8,128)(2,1)}, u32[]{:S(2)}, u32[]{:S(2)}) collective-permute-start(bf16[1,2,2,1,96,1536]{5,4,3,2,1,0:T(8,128)(2,1)} %pad_maximum_fusion.6), channel_id=1, source_target_pairs={{0,2},{1,3},{2,0},{3,1},{4,6},{5,7},{6,4},{7,5},{8,10},{9,11},{10,... | collective-permute-start | bytes 3538952 | tf_op jit(solution)/shard_map/ppermute | solution.py:402
  74.8 29.9 %collective-permute-start.11 = (bf16[2,2,1,1,96,1536]{5,4,3,2,1,0:T(8,128)(2,1)}, bf16[2,2,1,1,96,1536]{5,4,3,2,1,0:T(8,128)(2,1)}, u32[]{:S(2)}, u32[]{:S(2)}) collective-permute-start(bf16[2,2,1,1,96,1536]{5,4,3,2,1,0:T(8,128)(2,1)} %pad_maximum_fusion.7), channel_id=1, source_target_pairs={{0,4},{1,5},{2,6},{3,7},{4,0},{5,1},{6,2},{7,3},{8,12},{9,13},{10,... | collective-permute-start | bytes 3538952 | tf_op jit(solution)/shard_map/ppermute | solution.py:402
  78.9 27.6 %collective-permute-start.12 = (bf16[1,2,1,2,192,768]{5,4,3,2,1,0:T(8,128)(2,1)}, bf16[1,2,1,2,192,768]{5,4,3,2,1,0:T(8,128)(2,1)}, u32[]{:S(2)}, u32[]{:S(2)}) collective-permute-start(bf16[1,2,1,2,192,768]{5,4,3,2,1,0:T(8,128)(2,1)} %pad_maximum_fusion.8), channel_id=1, source_target_pairs={{0,8},{1,9},{2,10},{3,11},{4,12},{5,13},{6,14},{7,15},{8,0},{9,1},... | collective-permute-start | bytes 3538952 | tf_op jit(solution)/shard_map/ppermute | solution.py:402
  79.5 25.2 %collective-permute-start.13 = (bf16[32,768]{1,0:T(8,128)(2,1)S(1)}, bf16[32,768]{1,0:T(8,128)(2,1)S(1)}, u32[]{:S(2)}, u32[]{:S(2)}) collective-permute-start(bf16[32,768]{1,0:T(8,128)(2,1)S(1)} %add_convert_fusion.2), channel_id=1, source_target_pairs={{0,16},{1,17},{2,18},{3,19},{4,20},{5,21},{6,22},{7,23},{8,24},{9,... | collective-permute-start | bytes 147464 | tf_op jit(solution)/shard_map/ppermute | solution.py:402
  108.1 11.5 %collective-permute-start.16 = (bf16[32,768]{1,0:T(8,128)(2,1)S(1)}, bf16[32,768]{1,0:T(8,128)(2,1)S(1)}, u32[]{:S(2)}, u32[]{:S(2)}) collective-permute-start(bf16[32,768]{1,0:T(8,128)(2,1)S(1)} %add_convert_fusion.1), channel_id=1, source_target_pairs={{0,2},{1,3},{2,0},{3,1},{4,6},{5,7},{6,4},{7,5},{8,10},{9,11},{10,... | collective-permute-start | bytes 147464 | tf_op jit(solution)/shard_map/ppermute | solution.py:402
  110.5 29.0 %collective-permute-start.14 = (bf16[1,2,2,1,96,1536]{5,4,3,2,1,0:T(8,128)(2,1)S(1)}, bf16[1,2,2,1,96,1536]{5,4,3,2,1,0:T(8,128)(2,1)S(1)}, u32[]{:S(2)}, u32[]{:S(2)}) collective-permute-start(bf16[1,2,2,1,96,1536]{5,4,3,2,1,0:T(8,128)(2,1)S(1)} %get-tuple-element.280), channel_id=1, source_target_pairs={{0,4},{1,5},{2,6},{3,7},{4,0},{5,1},{6,2},{7,3},{8,12},{9,13},{10,... | collective-permute-start | bytes 3538952 | tf_op jit(solution)/shard_map/ppermute | solution.py:402
  111.3 88.6 %collective-permute-start.24 = (bf16[1,2,1,2,96,1536]{5,4,3,2,1,0:T(8,128)(2,1)S(1)}, bf16[1,2,1,2,96,1536]{5,4,3,2,1,0:T(8,128)(2,1)}, u32[]{:S(2)}, u32[]{:S(2)}) collective-permute-start(bf16[1,2,1,2,96,1536]{5,4,3,2,1,0:T(8,128)(2,1)S(1)} %get-tuple-element.273), channel_id=1, source_target_pairs={{0,8},{1,9},{2,10},{3,11},{4,12},{5,13},{6,14},{7,15},{8,0},{9,1},... | collective-permute-start | bytes 3538952 | tf_op jit(solution)/shard_map/ppermute | solution.py:402
  114.7 47.9 %collective-permute-start.18 = (bf16[1,2,1,2,96,1536]{5,4,3,2,1,0:T(8,128)(2,1)S(1)}, bf16[1,2,1,2,96,1536]{5,4,3,2,1,0:T(8,128)(2,1)S(1)}, u32[]{:S(2)}, u32[]{:S(2)}) collective-permute-start(bf16[1,2,1,2,96,1536]{5,4,3,2,1,0:T(8,128)(2,1)S(1)} %get-tuple-element.274), channel_id=1, source_target_pairs={{0,8},{1,9},{2,10},{3,11},{4,12},{5,13},{6,14},{7,15},{8,0},{9,1},... | collective-permute-start | bytes 3538952 | tf_op jit(solution)/shard_map/ppermute | solution.py:402
  114.8 55.9 %collective-permute-start.21 = (bf16[1,2,2,1,96,1536]{5,4,3,2,1,0:T(8,128)(2,1)S(1)}, bf16[1,2,2,1,96,1536]{5,4,3,2,1,0:T(8,128)(2,1)}, u32[]{:S(2)}, u32[]{:S(2)}) collective-permute-start(bf16[1,2,2,1,96,1536]{5,4,3,2,1,0:T(8,128)(2,1)S(1)} %get-tuple-element.279), channel_id=1, source_target_pairs={{0,4},{1,5},{2,6},{3,7},{4,0},{5,1},{6,2},{7,3},{8,12},{9,13},{10,... | collective-permute-start | bytes 3538952 | tf_op jit(solution)/shard_map/ppermute | solution.py:402
  119.6 56.3 %collective-permute-start.19 = (bf16[1,2,2,2,192,768]{5,4,3,2,1,0:T(8,128)(2,1)}, bf16[1,2,2,2,192,768]{5,4,3,2,1,0:T(8,128)(2,1)}, u32[]{:S(2)}, u32[]{:S(2)}) collective-permute-start(bf16[1,2,2,2,192,768]{5,4,3,2,1,0:T(8,128)(2,1)} %pad_maximum_fusion.2), channel_id=1, source_target_pairs={{0,2},{1,3},{2,0},{3,1},{4,6},{5,7},{6,4},{7,5},{8,10},{9,11},{10,... | collective-permute-start | bytes 7077896 | tf_op jit(solution)/shard_map/ppermute | solution.py:402
  140.0 23.9 %collective-permute-start.15 = (bf16[4,96,384]{2,1,0:T(8,128)(2,1)S(1)}, bf16[4,96,384]{2,1,0:T(8,128)(2,1)S(1)}, u32[]{:S(2)}, u32[]{:S(2)}) collective-permute-start(bf16[4,96,384]{2,1,0:T(8,128)(2,1)S(1)} %get-tuple-element.287), channel_id=1, source_target_pairs={{0,1},{1,0},{2,3},{3,2},{4,5},{5,4},{6,7},{7,6},{8,9},{9,8},{10,11... | collective-permute-start | bytes 884744 | tf_op jit(solution)/shard_map/ppermute | solution.py:402
  170.6 9.6 %collective-permute-start.17 = (bf16[512,768]{1,0:T(8,128)(2,1)S(1)}, bf16[512,768]{1,0:T(8,128)(2,1)S(1)}, u32[]{:S(2)}, u32[]{:S(2)}) collective-permute-start(bf16[512,768]{1,0:T(8,128)(2,1)S(1)} %get-tuple-element.140.own), channel_id=1, source_target_pairs={{0,1},{1,0},{2,3},{3,2},{4,5},{5,4},{6,7},{7,6},{8,9},{9,8},{10,11... | collective-permute-start | bytes 2359304 | tf_op jit(solution)/shard_map/ppermute | solution.py:402
  188.2 3.3 collective-permute-start.20
  189.3 1.6 collective-permute-start.22
  199.6 3.6 collective-permute-start.23
  210.7 2.3 collective-permute-start.25
  221.3 2.4 collective-permute-start.27
  235.8 19.3 %collective-permute-start.28 = (bf16[512,768]{1,0:T(8,128)(2,1)}, bf16[512,768]{1,0:T(8,128)(2,1)S(1)}, u32[]{:S(2)}, u32[]{:S(2)}) collective-permute-start(bf16[512,768]{1,0:T(8,128)(2,1)} %get-tuple-element.158.own), channel_id=1, source_target_pairs={{0,1},{1,0},{2,3},{3,2},{4,5},{5,4},{6,7},{7,6},{8,9},{9,8},{10,11... | collective-permute-start | bytes 2359304 | tf_op jit(solution)/shard_map/ppermute | solution.py:402
  237.6 33.3 %collective-permute-start.26 = (bf16[512,768]{1,0:T(8,128)(2,1)}, bf16[512,768]{1,0:T(8,128)(2,1)}, u32[]{:S(2)}, u32[]{:S(2)}) collective-permute-start(bf16[512,768]{1,0:T(8,128)(2,1)} %get-tuple-element.262), channel_id=1, source_target_pairs={{0,2},{1,3},{2,0},{3,1},{4,6},{5,7},{6,4},{7,5},{8,10},{9,11},{10,... | collective-permute-start | bytes 2359304 | tf_op jit(solution)/shard_map/ppermute | solution.py:402
  245.2 28.2 %collective-permute-start.47 = (bf16[384,1536]{1,0:T(8,128)(2,1)}, bf16[384,1536]{1,0:T(8,128)(2,1)}, u32[]{:S(2)}, u32[]{:S(2)}) collective-permute-start(bf16[384,1536]{1,0:T(8,128)(2,1)} %get-tuple-element.222), channel_id=1, source_target_pairs={{0,8},{1,9},{2,10},{3,11},{4,12},{5,13},{6,14},{7,15},{8,0},{9,1},... | collective-permute-start | bytes 3538952 | tf_op jit(solution)/shard_map/ppermute | solution.py:402
  246.9 36.6 %collective-permute-start.57 = (bf16[768,768]{1,0:T(8,128)(2,1)}, bf16[768,768]{1,0:T(8,128)(2,1)}, u32[]{:S(2)}, u32[]{:S(2)}) collective-permute-start(bf16[768,768]{1,0:T(8,128)(2,1)} %get-tuple-element.239), channel_id=1, source_target_pairs={{0,2},{1,3},{2,0},{3,1},{4,6},{5,7},{6,4},{7,5},{8,10},{9,11},{10,... | collective-permute-start | bytes 3538952 | tf_op jit(solution)/shard_map/ppermute | solution.py:402
  248.7 1.6 collective-permute-start.37
  253.6 52.9 %collective-permute-start.38 = (bf16[384,1536]{1,0:T(8,128)(2,1)}, bf16[384,1536]{1,0:T(8,128)(2,1)S(1)}, u32[]{:S(2)}, u32[]{:S(2)}) collective-permute-start(bf16[384,1536]{1,0:T(8,128)(2,1)} %get-tuple-element.200), channel_id=1, source_target_pairs={{0,4},{1,5},{2,6},{3,7},{4,0},{5,1},{6,2},{7,3},{8,12},{9,13},{10,... | collective-permute-start | bytes 3538952 | tf_op jit(solution)/shard_map/ppermute | solution.py:402
  264.5 23.8 %collective-permute-start.29 = (bf16[512,768]{1,0:T(8,128)(2,1)S(1)}, bf16[512,768]{1,0:T(8,128)(2,1)S(1)}, u32[]{:S(2)}, u32[]{:S(2)}) collective-permute-start(bf16[512,768]{1,0:T(8,128)(2,1)S(1)} %get-tuple-element.163.own), channel_id=1, source_target_pairs={{0,1},{1,0},{2,3},{3,2},{4,5},{5,4},{6,7},{7,6},{8,9},{9,8},{10,11... | collective-permute-start | bytes 2359304 | tf_op jit(solution)/shard_map/ppermute | solution.py:402
  270.9 36.0 %collective-permute-start.43 = (bf16[384,1536]{1,0:T(8,128)(2,1)}, bf16[384,1536]{1,0:T(8,128)(2,1)}, u32[]{:S(2)}, u32[]{:S(2)}) collective-permute-start(bf16[384,1536]{1,0:T(8,128)(2,1)} %get-tuple-element.211), channel_id=1, source_target_pairs={{0,8},{1,9},{2,10},{3,11},{4,12},{5,13},{6,14},{7,15},{8,0},{9,1},... | collective-permute-start | bytes 3538952 | tf_op jit(solution)/shard_map/ppermute | solution.py:402
  273.4 60.0 %collective-permute-start.53 = (bf16[768,768]{1,0:T(8,128)(2,1)}, bf16[768,768]{1,0:T(8,128)(2,1)S(1)}, u32[]{:S(2)}, u32[]{:S(2)}) collective-permute-start(bf16[768,768]{1,0:T(8,128)(2,1)} %get-tuple-element.231), channel_id=1, source_target_pairs={{0,2},{1,3},{2,0},{3,1},{4,6},{5,7},{6,4},{7,5},{8,10},{9,11},{10,... | collective-permute-start | bytes 3538952 | tf_op jit(solution)/shard_map/ppermute | solution.py:402
  283.6 26.4 %collective-permute-start.48 = (bf16[192,1536]{1,0:T(8,128)(2,1)}, bf16[192,1536]{1,0:T(8,128)(2,1)}, u32[]{:S(2)}, u32[]{:S(2)}) collective-permute-start(bf16[192,1536]{1,0:T(8,128)(2,1)} %get-tuple-element.224), channel_id=1, source_target_pairs={{0,4},{1,5},{2,6},{3,7},{4,0},{5,1},{6,2},{7,3},{8,12},{9,13},{10,... | collective-permute-start | bytes 1769480 | tf_op jit(solution)/shard_map/ppermute | solution.py:402
  289.1 22.8 %collective-permute-start.58 = (bf16[384,768]{1,0:T(8,128)(2,1)}, bf16[384,768]{1,0:T(8,128)(2,1)S(1)}, u32[]{:S(2)}, u32[]{:S(2)}) collective-permute-start(bf16[384,768]{1,0:T(8,128)(2,1)} %get-tuple-element.241), channel_id=1, source_target_pairs={{0,8},{1,9},{2,10},{3,11},{4,12},{5,13},{6,14},{7,15},{8,0},{9,1},... | collective-permute-start | bytes 1769480 | tf_op jit(solution)/shard_map/ppermute | solution.py:402
  306.5 7.0 %collective-permute-start.32 = (bf16[4,96,384]{2,1,0:T(8,128)(2,1)S(1)}, bf16[4,96,384]{2,1,0:T(8,128)(2,1)S(1)}, u32[]{:S(2)}, u32[]{:S(2)}) collective-permute-start(bf16[4,96,384]{2,1,0:T(8,128)(2,1)S(1)} %get-tuple-element.177), channel_id=1, source_target_pairs={{0,1},{1,0},{2,3},{3,2},{4,5},{5,4},{6,7},{7,6},{8,9},{9,8},{10,11... | collective-permute-start | bytes 884744 | tf_op jit(solution)/shard_map/ppermute | solution.py:402
  306.9 28.2 %collective-permute-start.39 = (bf16[192,1536]{1,0:T(8,128)(2,1)S(1)}, bf16[192,1536]{1,0:T(8,128)(2,1)S(1)}, u32[]{:S(2)}, u32[]{:S(2)}) collective-permute-start(bf16[192,1536]{1,0:T(8,128)(2,1)S(1)} %get-tuple-element.202), channel_id=1, source_target_pairs={{0,2},{1,3},{2,0},{3,1},{4,6},{5,7},{6,4},{7,5},{8,10},{9,11},{10,... | collective-permute-start | bytes 1769480 | tf_op jit(solution)/shard_map/ppermute | solution.py:402
  310.0 28.2 %collective-permute-start.44 = (bf16[192,1536]{1,0:T(8,128)(2,1)S(1)}, bf16[192,1536]{1,0:T(8,128)(2,1)S(1)}, u32[]{:S(2)}, u32[]{:S(2)}) collective-permute-start(bf16[192,1536]{1,0:T(8,128)(2,1)S(1)} %get-tuple-element.213), channel_id=1, source_target_pairs={{0,4},{1,5},{2,6},{3,7},{4,0},{5,1},{6,2},{7,3},{8,12},{9,13},{10,... | collective-permute-start | bytes 1769480 | tf_op jit(solution)/shard_map/ppermute | solution.py:402
  311.9 17.1 %collective-permute-start.49 = (bf16[96,1536]{1,0:T(8,128)(2,1)S(1)}, bf16[96,1536]{1,0:T(8,128)(2,1)S(1)}, u32[]{:S(2)}, u32[]{:S(2)}) collective-permute-start(bf16[96,1536]{1,0:T(8,128)(2,1)S(1)} %get-tuple-element.226), channel_id=1, source_target_pairs={{0,2},{1,3},{2,0},{3,1},{4,6},{5,7},{6,4},{7,5},{8,10},{9,11},{10,... | collective-permute-start | bytes 884744 | tf_op jit(solution)/shard_map/ppermute | solution.py:402
  313.5 18.5 %collective-permute-start.59 = (bf16[192,768]{1,0:T(8,128)(2,1)S(1)}, bf16[192,768]{1,0:T(8,128)(2,1)S(1)}, u32[]{:S(2)}, u32[]{:S(2)}) collective-permute-start(bf16[192,768]{1,0:T(8,128)(2,1)S(1)} %get-tuple-element.243), channel_id=1, source_target_pairs={{0,4},{1,5},{2,6},{3,7},{4,0},{5,1},{6,2},{7,3},{8,12},{9,13},{10,... | collective-permute-start | bytes 884744 | tf_op jit(solution)/shard_map/ppermute | solution.py:402
  329.0 49.4 %collective-permute-start.33 = (bf16[400,1536]{1,0:T(8,128)(2,1)}, bf16[400,1536]{1,0:T(8,128)(2,1)S(1)}, u32[]{:S(2)}, u32[]{:S(2)}) collective-permute-start(bf16[400,1536]{1,0:T(8,128)(2,1)} %get-tuple-element.183), channel_id=1, source_target_pairs={{0,4},{1,5},{2,6},{3,7},{4,0},{5,1},{6,2},{7,3},{8,12},{9,13},{10,... | collective-permute-start | bytes 3686408 | tf_op jit(solution)/shard_map/ppermute | solution.py:402
  332.0 38.0 %collective-permute-start.30 = (bf16[512,768]{1,0:T(8,128)(2,1)}, bf16[512,768]{1,0:T(8,128)(2,1)}, u32[]{:S(2)}, u32[]{:S(2)}) collective-permute-start(bf16[512,768]{1,0:T(8,128)(2,1)} %get-tuple-element.169), channel_id=1, source_target_pairs={{0,1},{1,0},{2,3},{3,2},{4,5},{5,4},{6,7},{7,6},{8,9},{9,8},{10,11... | collective-permute-start | bytes 2359304 | tf_op jit(solution)/shard_map/ppermute | solution.py:402
  333.4 13.6 %collective-permute-start.50 = (bf16[48,1536]{1,0:T(8,128)(2,1)}, bf16[48,1536]{1,0:T(8,128)(2,1)}, u32[]{:S(2)}, u32[]{:S(2)}) collective-permute-start(bf16[48,1536]{1,0:T(8,128)(2,1)} %get-tuple-element.228), channel_id=1, source_target_pairs={{0,16},{1,17},{2,18},{3,19},{4,20},{5,21},{6,22},{7,23},{8,24},{9,... | collective-permute-start | bytes 442376 | tf_op jit(solution)/shard_map/ppermute | solution.py:402
  335.1 15.1 %collective-permute-start.60 = (bf16[96,768]{1,0:T(8,128)(2,1)}, bf16[96,768]{1,0:T(8,128)(2,1)}, u32[]{:S(2)}, u32[]{:S(2)}) collective-permute-start(bf16[96,768]{1,0:T(8,128)(2,1)} %get-tuple-element.245), channel_id=1, source_target_pairs={{0,16},{1,17},{2,18},{3,19},{4,20},{5,21},{6,22},{7,23},{8,24},{9,... | collective-permute-start | bytes 442376 | tf_op jit(solution)/shard_map/ppermute | solution.py:402
  339.0 29.1 %collective-permute-start.54 = (bf16[384,768]{1,0:T(8,128)(2,1)}, bf16[384,768]{1,0:T(8,128)(2,1)}, u32[]{:S(2)}, u32[]{:S(2)}) collective-permute-start(bf16[384,768]{1,0:T(8,128)(2,1)} %get-tuple-element.233), channel_id=1, source_target_pairs={{0,8},{1,9},{2,10},{3,11},{4,12},{5,13},{6,14},{7,15},{8,0},{9,1},... | collective-permute-start | bytes 1769480 | tf_op jit(solution)/shard_map/ppermute | solution.py:402
  347.0 16.3 %collective-permute-start.40 = (bf16[96,1536]{1,0:T(8,128)(2,1)S(1)}, bf16[96,1536]{1,0:T(8,128)(2,1)S(1)}, u32[]{:S(2)}, u32[]{:S(2)}) collective-permute-start(bf16[96,1536]{1,0:T(8,128)(2,1)S(1)} %get-tuple-element.204), channel_id=1, source_target_pairs={{0,16},{1,17},{2,18},{3,19},{4,20},{5,21},{6,22},{7,23},{8,24},{9,... | collective-permute-start | bytes 884744 | tf_op jit(solution)/shard_map/ppermute | solution.py:402
  350.2 19.6 %collective-permute-start.45 = (bf16[96,1536]{1,0:T(8,128)(2,1)S(1)}, bf16[96,1536]{1,0:T(8,128)(2,1)S(1)}, u32[]{:S(2)}, u32[]{:S(2)}) collective-permute-start(bf16[96,1536]{1,0:T(8,128)(2,1)S(1)} %get-tuple-element.215), channel_id=1, source_target_pairs={{0,2},{1,3},{2,0},{3,1},{4,6},{5,7},{6,4},{7,5},{8,10},{9,11},{10,... | collective-permute-start | bytes 884744 | tf_op jit(solution)/shard_map/ppermute | solution.py:402
  351.9 18.1 %copy-start.57 = (f32[512,768]{1,0:T(8,128)S(1)}, f32[512,768]{1,0:T(8,128)}, u32[]{:S(2)}) copy-start(f32[512,768]{1,0:T(8,128)} %get-tuple-element.168) | copy-start | bytes 4718596
  363.4 9.2 %collective-permute-start.41 = (bf16[48,1536]{1,0:T(8,128)(2,1)S(1)}, bf16[48,1536]{1,0:T(8,128)(2,1)S(1)}, u32[]{:S(2)}, u32[]{:S(2)}) collective-permute-start(bf16[48,1536]{1,0:T(8,128)(2,1)S(1)} %get-tuple-element.206), channel_id=1, source_target_pairs={{0,8},{1,9},{2,10},{3,11},{4,12},{5,13},{6,14},{7,15},{8,0},{9,1},... | collective-permute-start | bytes 442376 | tf_op jit(solution)/shard_map/ppermute | solution.py:402
  369.3 7.0 %collective-permute-start.55 = (bf16[192,768]{1,0:T(8,128)(2,1)S(1)}, bf16[192,768]{1,0:T(8,128)(2,1)S(1)}, u32[]{:S(2)}, u32[]{:S(2)}) collective-permute-start(bf16[192,768]{1,0:T(8,128)(2,1)S(1)} %get-tuple-element.235), channel_id=1, source_target_pairs={{0,4},{1,5},{2,6},{3,7},{4,0},{5,1},{6,2},{7,3},{8,12},{9,13},{10,... | collective-permute-start | bytes 884744 | tf_op jit(solution)/shard_map/ppermute | solution.py:402
  369.9 8.4 %collective-permute-start.46 = (bf16[48,1536]{1,0:T(8,128)(2,1)S(1)}, bf16[48,1536]{1,0:T(8,128)(2,1)S(1)}, u32[]{:S(2)}, u32[]{:S(2)}) collective-permute-start(bf16[48,1536]{1,0:T(8,128)(2,1)S(1)} %get-tuple-element.217), channel_id=1, source_target_pairs={{0,16},{1,17},{2,18},{3,19},{4,20},{5,21},{6,22},{7,23},{8,24},{9,... | collective-permute-start | bytes 442376 | tf_op jit(solution)/shard_map/ppermute | solution.py:402
  372.1 57.7 %collective-permute-start.31 = (bf16[512,768]{1,0:T(8,128)(2,1)S(1)}, bf16[512,768]{1,0:T(8,128)(2,1)S(1)}, u32[]{:S(2)}, u32[]{:S(2)}) collective-permute-start(bf16[512,768]{1,0:T(8,128)(2,1)S(1)} %get-tuple-element.259), channel_id=1, source_target_pairs={{0,2},{1,3},{2,0},{3,1},{4,6},{5,7},{6,4},{7,5},{8,10},{9,11},{10,... | collective-permute-start | bytes 2359304 | tf_op jit(solution)/shard_map/ppermute | solution.py:402
  376.5 6.7 %collective-permute-start.56 = (bf16[96,768]{1,0:T(8,128)(2,1)S(1)}, bf16[96,768]{1,0:T(8,128)(2,1)S(1)}, u32[]{:S(2)}, u32[]{:S(2)}) collective-permute-start(bf16[96,768]{1,0:T(8,128)(2,1)S(1)} %get-tuple-element.237), channel_id=1, source_target_pairs={{0,16},{1,17},{2,18},{3,19},{4,20},{5,21},{6,22},{7,23},{8,24},{9,... | collective-permute-start | bytes 442376 | tf_op jit(solution)/shard_map/ppermute | solution.py:402
  378.6 27.6 %collective-permute-start.34 = (bf16[208,1536]{1,0:T(8,128)(2,1)S(1)}, bf16[208,1536]{1,0:T(8,128)(2,1)S(1)}, u32[]{:S(2)}, u32[]{:S(2)}) collective-permute-start(bf16[208,1536]{1,0:T(8,128)(2,1)S(1)} %get-tuple-element.185), channel_id=1, source_target_pairs={{0,2},{1,3},{2,0},{3,1},{4,6},{5,7},{6,4},{7,5},{8,10},{9,11},{10,... | collective-permute-start | bytes 1916936 | tf_op jit(solution)/shard_map/ppermute | solution.py:402
  379.2 30.0 %collective-permute-start.51 = (bf16[48,1536]{1,0:T(8,128)(2,1)S(1)}, bf16[48,1536]{1,0:T(8,128)(2,1)S(1)}, u32[]{:S(2)}, u32[]{:S(2)}) collective-permute-start(bf16[48,1536]{1,0:T(8,128)(2,1)S(1)} %broadcast_select_fusion.51), channel_id=1, source_target_pairs={{0,2},{1,3},{2,0},{3,1},{4,6},{5,7},{6,4},{7,5},{8,10},{9,11},{10,... | collective-permute-start | bytes 442376 | tf_op jit(solution)/shard_map/ppermute | solution.py:402
  383.3 35.3 %collective-permute-start.61 = (bf16[96,768]{1,0:T(8,128)(2,1)S(1)}, bf16[96,768]{1,0:T(8,128)(2,1)S(1)}, u32[]{:S(2)}, u32[]{:S(2)}) collective-permute-start(bf16[96,768]{1,0:T(8,128)(2,1)S(1)} %broadcast_select_fusion.47), channel_id=1, source_target_pairs={{0,2},{1,3},{2,0},{3,1},{4,6},{5,7},{6,4},{7,5},{8,10},{9,11},{10,... | collective-permute-start | bytes 442376 | tf_op jit(solution)/shard_map/ppermute | solution.py:402
  406.4 12.0 %collective-permute-start.35 = (bf16[112,1536]{1,0:T(8,128)(2,1)S(1)}, bf16[112,1536]{1,0:T(8,128)(2,1)S(1)}, u32[]{:S(2)}, u32[]{:S(2)}) collective-permute-start(bf16[112,1536]{1,0:T(8,128)(2,1)S(1)} %get-tuple-element.188), channel_id=1, source_target_pairs={{0,16},{1,17},{2,18},{3,19},{4,20},{5,21},{6,22},{7,23},{8,24},{9,... | collective-permute-start | bytes 1032200 | tf_op jit(solution)/shard_map/ppermute | solution.py:402
  418.6 5.7 %collective-permute-start.36 = (bf16[64,1536]{1,0:T(8,128)(2,1)S(1)}, bf16[64,1536]{1,0:T(8,128)(2,1)S(1)}, u32[]{:S(2)}, u32[]{:S(2)}) collective-permute-start(bf16[64,1536]{1,0:T(8,128)(2,1)S(1)} %get-tuple-element.191), channel_id=1, source_target_pairs={{0,8},{1,9},{2,10},{3,11},{4,12},{5,13},{6,14},{7,15},{8,0},{9,1},... | collective-permute-start | bytes 589832 | tf_op jit(solution)/shard_map/ppermute | solution.py:402
  424.4 5.2 %collective-permute-start.42 = (bf16[48,1536]{1,0:T(8,128)(2,1)S(1)}, bf16[48,1536]{1,0:T(8,128)(2,1)S(1)}, u32[]{:S(2)}, u32[]{:S(2)}) collective-permute-start(bf16[48,1536]{1,0:T(8,128)(2,1)S(1)} %broadcast_select_fusion.55), channel_id=1, source_target_pairs={{0,2},{1,3},{2,0},{3,1},{4,6},{5,7},{6,4},{7,5},{8,10},{9,11},{10,... | collective-permute-start | bytes 442376 | tf_op jit(solution)/shard_map/ppermute | solution.py:402
  429.7 1.7 collective-permute-start.52
  (66 other events, 269.4 us)
